TPU v7x, 128 devices: a whole 4x4x4 slice. The times are simulated.
128 devices in a mesh: mem: 4 (over x), seqi: 8 (over z, core), seqo: 4 (over y).
Axes of the slice: x: 4, y: 4, z: 4, core: 2. Of those that a mesh axis runs over, the one named last changes fastest.
Arguments:
- queries: bfloat16 [32, 512, 2048], P(('seqi', 'seqo'), 'mem'), may hold values from -6 to 6
- keys: bfloat16 [32, 512, 2048], P(('seqi', 'seqo'), 'mem'), may hold values from -6 to 6
- values: bfloat16 [32, 512, 2048], P(('seqi', 'seqo'), 'mem'), may hold values from -6 to 6
- log_decay: bfloat16 [16, 32, 512], P(None, ('seqi', 'seqo'), 'mem'), may hold values from -1 to 0
- routes: int32 [32, 512, 2], P(('seqi', 'seqo'), 'mem'), may hold values from 0 to 3, all different within a row; in each aligned block of 128 rows (0 to 127, 128 to 255, ..., all dimensions but the last counted through in order) at most 80 rows name the same one
- route_logits: bfloat16 [32, 512, 2], P(('seqi', 'seqo'), 'mem'), may hold values from -6 to 6
- cotangent: bfloat16 [32, 512, 2048], P(('seqi', 'seqo'), 'mem'), may hold values from -6 to 6
Outputs:
- output: bfloat16 [32, 512, 2048], P(('seqi', 'seqo'), 'mem')
- grad_queries: bfloat16 [32, 512, 2048], P(('seqi', 'seqo'), 'mem')
- grad_keys: bfloat16 [32, 512, 2048], P(('seqi', 'seqo'), 'mem')
- grad_values: bfloat16 [32, 512, 2048], P(('seqi', 'seqo'), 'mem')
Inputs may be any that keep to these rules, and one draw needn't show every extreme that they name: `routes`: in the rows of one device no memory is named by more than 80 rows, and in every draw some device names some memory exactly 80 times.
All inputs are finite; a program needn't handle non-finite values.
Results may differ from a plain program's by a relative error of at most 0.014.
Values may be sent and summed in bfloat16 or wider, within the bound.
No kernel may reach another device: no remote copies, remote signals or barrier semaphores. Data moves between devices by JAX's collectives and lax.ppermute only.
A program may use at most 448 MiB of HBM per device.

v0:
```python
import math

import jax
import jax.numpy as jnp
from jax import lax
from jax.sharding import PartitionSpec as P

H = 16
DK = 128
MEM_DEV = 1
SHARD_STEPS = 128
CAP = 80


HIGH = lax.Precision.HIGH


def entering(value, axis, join, neutral, backward):
    count, mine = (lax.axis_size(axis), lax.axis_index(axis))
    pieces = jax.tree.map(lambda part: lax.all_gather(part, axis), value)
    if backward:
        pieces = jax.tree.map(lambda part: part[::-1], pieces)
        mine = count - 1 - mine
    total = jax.tree.map(
        lambda part, zero: jnp.full_like(part, 0) + jnp.asarray(zero, part.dtype), value, neutral
    )

    def hop(position, total):
        longer = join(total, jax.tree.map(lambda part: part[position], pieces))
        return jax.tree.map(lambda new, old: jnp.where(position < mine, new, old), longer, total)

    return lax.fori_loop(0, count - 1, hop, total)


def combine(earlier, later):
    return (earlier[0] * later[0], later[0][:, None, None] * earlier[1] + later[1])


def neutral(element):
    return (jnp.ones_like(element[0]), jnp.zeros_like(element[1]))


def seq_prefix(element, backward):
    return entering(element, ("seqi", "seqo"), combine, neutral(element), backward)


def as_blocks(array, count, span):
    return array.reshape((array.shape[0], count, span) + array.shape[2:])


def local_pass(raw_reads, factor, raw_writes, raw_values, log_rates):
    storage_channels, length, width = raw_reads.shape
    span = math.gcd(length, 128)
    count = length // span
    row_factor = jnp.broadcast_to(factor, (storage_channels, length, 1))
    reads = raw_reads.astype(jnp.float32) * row_factor
    writes = raw_writes.astype(jnp.float32)
    values_in = raw_values.astype(jnp.float32)
    cumulative = jnp.cumsum(log_rates, axis=1)
    inner = jnp.cumsum(log_rates.reshape(storage_channels, count, span), axis=2)
    lower = jnp.arange(span)[:, None] >= jnp.arange(span)[None, :]
    spread = inner[:, :, :, None] - inner[:, :, None, :]
    decay_matrix = jnp.where(lower, jnp.exp(jnp.where(lower, spread, 0.0)), 0.0)
    raw_scores = jnp.einsum(
        "nctd,ncsd->ncts",
        as_blocks(raw_reads, count, span),
        as_blocks(raw_writes, count, span),
        preferred_element_type=jnp.float32,
    )
    scores = raw_scores * as_blocks(row_factor, count, span) * decay_matrix
    within = jnp.einsum(
        "ncts,ncse->ncte", scores, as_blocks(values_in, count, span), precision=HIGH
    )
    inner_tail = jnp.exp(inner[:, :, -1:] - inner)
    stretch_decay = jnp.exp(inner[:, :, -1])
    stretch_state = jnp.einsum(
        "ncsd,ncse->ncde",
        as_blocks(writes, count, span) * inner_tail[..., None],
        as_blocks(values_in, count, span),
        precision=HIGH,
    )

    def advance(state, item):
        decay, addend = item
        return (decay[:, None, None] * state + addend, state)

    start = jnp.zeros((storage_channels, width, width), jnp.float32)
    unused, starts = lax.scan(
        advance, start, (stretch_decay.T, stretch_state.transpose(1, 0, 2, 3))
    )
    stretch_prefix = starts.transpose(1, 0, 2, 3)
    within = within + jnp.einsum(
        "nctd,ncde->ncte",
        as_blocks(reads, count, span) * jnp.exp(inner)[..., None],
        stretch_prefix,
        precision=HIGH,
    )
    within = within.reshape(storage_channels, length, width)
    tail_decay = jnp.exp(cumulative[:, -1:] - cumulative)
    total_decay = jnp.exp(cumulative[:, -1])
    state = jnp.einsum("nsd,nse->nde", writes * tail_decay[:, :, None], values_in, precision=HIGH)
    return (
        cumulative,
        decay_matrix,
        scores,
        within,
        tail_decay,
        total_decay,
        state,
        inner,
        stretch_prefix,
        stretch_decay,
        reads,
        writes,
        values_in,
        inner_tail,
    )


def carried(reads, cumulative, prefix):
    return jnp.einsum(
        "ntd,nde->nte", reads * jnp.exp(cumulative)[:, :, None], prefix, precision=HIGH
    )


def read_carry(reads, cumulative, cotan):
    return jnp.einsum(
        "ntd,nte->nde",
        reads * jnp.exp(cumulative)[:, :, None],
        cotan.astype(jnp.float32),
        precision=HIGH,
    )


def local_backward(raw_values, raw_cotan, passed, prefix, grad_state):
    (
        cumulative,
        decay_matrix,
        scores,
        within,
        tail_decay,
        total_decay,
        state,
        inner,
        stretch_prefix,
        stretch_decay,
        reads,
        writes,
        values_in,
        inner_tail,
    ) = passed
    storage_channels, length, width = reads.shape
    count = inner.shape[1]
    span = inner.shape[2]
    cotan = raw_cotan.astype(jnp.float32)
    cotan_blocks = as_blocks(cotan, count, span)
    read_blocks = as_blocks(reads, count, span)
    write_blocks = as_blocks(writes, count, span)
    value_blocks = as_blocks(values_in, count, span)
    masked = (
        jnp.einsum(
            "ncte,ncse->ncts",
            as_blocks(raw_cotan, count, span),
            as_blocks(raw_values, count, span),
            preferred_element_type=jnp.float32,
        )
        * decay_matrix
    )
    stretch_reads = jnp.einsum(
        "nctd,ncte->ncde", read_blocks * jnp.exp(inner)[..., None], cotan_blocks, precision=HIGH
    )

    def retreat(carry, item):
        decay, addend = item
        return (decay[:, None, None] * carry + addend, carry)

    start = jnp.zeros((storage_channels, width, width), jnp.float32)
    unused, later = lax.scan(
        retreat, start, (stretch_decay.T, stretch_reads.transpose(1, 0, 2, 3)), reverse=True
    )
    later_grad = later.transpose(1, 0, 2, 3)
    grad_reads = (
        jnp.einsum("ncts,ncsd->nctd", masked, write_blocks, precision=HIGH)
        + jnp.einsum("ncte,ncde->nctd", cotan_blocks, stretch_prefix, precision=HIGH)
        * jnp.exp(inner)[..., None]
    )
    grad_writes = (
        jnp.einsum("ncts,nctd->ncsd", masked, read_blocks, precision=HIGH)
        + jnp.einsum("ncse,ncde->ncsd", value_blocks, later_grad, precision=HIGH)
        * inner_tail[..., None]
    )
    grad_values = (
        jnp.einsum("ncts,ncte->ncse", scores, cotan_blocks, precision=HIGH)
        + jnp.einsum("ncsd,ncde->ncse", write_blocks, later_grad, precision=HIGH)
        * inner_tail[..., None]
    )
    grad_reads = (
        grad_reads.reshape(storage_channels, length, width)
        + jnp.einsum("nte,nde->ntd", cotan, prefix, precision=HIGH)
        * jnp.exp(cumulative)[:, :, None]
    )
    grad_writes = (
        grad_writes.reshape(storage_channels, length, width)
        + jnp.einsum("nse,nde->nsd", values_in, grad_state, precision=HIGH) * tail_decay[:, :, None]
    )
    grad_values = (
        grad_values.reshape(storage_channels, length, width)
        + jnp.einsum("nsd,nde->nse", writes, grad_state, precision=HIGH) * tail_decay[:, :, None]
    )
    return (grad_reads, grad_writes, grad_values)


def route_streams(block, head_count):
    groups, held, slots, features = block.shape
    head_size = features // head_count
    split = block.reshape(groups, held, slots, head_count, head_size).transpose(1, 3, 0, 2, 4)
    return split.reshape(held, head_count, groups * slots, head_size)


def route_rows(stream, groups):
    held, head_count, length, head_size = stream.shape
    slots = length // groups
    moved = stream.reshape(held, head_count, groups, slots, head_size).transpose(2, 0, 3, 1, 4)
    return moved.reshape(groups, held, slots, head_count * head_size)


def body(queries, keys, values, log_decay, routes, route_logits, cotangent):
    groups = lax.axis_size("mem")
    memories = MEM_DEV * groups
    features = H * DK
    total_tokens = SHARD_STEPS * groups * lax.axis_size("seqi") * lax.axis_size("seqo")
    scale = 2.0 / math.sqrt(DK * total_tokens)
    query_rows = queries[0]
    key_rows = keys[0]
    value_rows = values[0]
    cotan_rows = cotangent[0]
    gates = log_decay[:, 0, :]
    chosen = routes[0]
    logits = route_logits[0].astype(jnp.float32)
    first_weight = jax.nn.sigmoid(logits[:, 0] - logits[:, 1]).astype(jnp.bfloat16)
    second_weight = jax.nn.sigmoid(logits[:, 1] - logits[:, 0]).astype(jnp.bfloat16)
    member = chosen.reshape(-1)
    onehot = (member[:, None] == jnp.arange(memories, dtype=jnp.int32)[None, :]).astype(jnp.int32)
    earlier = jnp.cumsum(onehot, axis=0) - onehot
    position = jnp.sum(earlier * onehot, axis=1)
    slot_index = member * CAP + position
    owner_token = jnp.arange(2 * SHARD_STEPS, dtype=jnp.int32) // 2
    slot_table = jnp.full((memories * CAP,), SHARD_STEPS, jnp.int32).at[slot_index].set(owner_token)
    slot_weight = (
        jnp.zeros((memories * CAP,), jnp.bfloat16)
        .at[slot_index]
        .set(jnp.stack([first_weight, second_weight], 1).reshape(-1))
    )
    stacked = jnp.concatenate(
        [
            jnp.stack([query_rows, key_rows, value_rows], 1),
            jnp.zeros((1, 3, features), jnp.bfloat16),
        ],
        0,
    )
    packed = stacked[slot_table].reshape(groups, MEM_DEV, CAP, 3, features)
    gate_table = jnp.concatenate([gates.T, jnp.zeros((1, H), jnp.bfloat16)], 0)
    gate_rows = gate_table[slot_table].reshape(groups, MEM_DEV, CAP, H)
    weight_rows = slot_weight.reshape(groups, MEM_DEV, CAP)
    arrived, arrived_gates, arrived_weights = (
        lax.all_to_all(packed, "mem", split_axis=0, concat_axis=0, tiled=True),
        lax.all_to_all(gate_rows, "mem", split_axis=0, concat_axis=0, tiled=True),
        lax.all_to_all(weight_rows, "mem", split_axis=0, concat_axis=0, tiled=True),
    )
    length = groups * CAP
    routed_count = MEM_DEV * H
    factor = (
        arrived_weights.astype(jnp.float32).transpose(1, 0, 2).reshape(MEM_DEV, 1, length, 1)
        * scale
    )
    routed_factor = jnp.broadcast_to(factor, (MEM_DEV, H, length, 1)).reshape(
        routed_count, length, 1
    )
    routed_raw_reads = route_streams(arrived[:, :, :, 0], H).reshape(routed_count, length, DK)
    routed_raw_writes = route_streams(arrived[:, :, :, 1], H).reshape(routed_count, length, DK)
    routed_raw_values = route_streams(arrived[:, :, :, 2], H).reshape(routed_count, length, DK)
    routed_logs = (
        arrived_gates.astype(jnp.float32).transpose(1, 3, 0, 2).reshape(routed_count, length)
    )
    per_device = H // groups
    parted = jnp.stack(
        [
            query_rows.reshape(SHARD_STEPS, groups, per_device * DK),
            key_rows.reshape(SHARD_STEPS, groups, per_device * DK),
            value_rows.reshape(SHARD_STEPS, groups, per_device * DK),
        ],
        2,
    )
    gate_part = gates.T.reshape(SHARD_STEPS, groups, per_device)
    shared_in, shared_gates = (
        lax.all_to_all(parted, "mem", split_axis=1, concat_axis=0, tiled=True),
        lax.all_to_all(gate_part, "mem", split_axis=1, concat_axis=0, tiled=True),
    )
    shared_streams = (
        shared_in[:, 0].reshape(groups * SHARD_STEPS, 3, per_device, DK).transpose(1, 2, 0, 3)
    )
    shared_logs = shared_gates[:, 0].astype(jnp.float32).T
    shared_factor = jnp.full((1, 1, 1), scale, jnp.float32)
    routed_pass = local_pass(
        routed_raw_reads, routed_factor, routed_raw_writes, routed_raw_values, routed_logs
    )
    shared_pass = local_pass(
        shared_streams[0], shared_factor, shared_streams[1], shared_streams[2], shared_logs
    )
    shared_element = (shared_pass[5], shared_pass[6])
    joint = (
        jnp.concatenate([routed_pass[5], shared_element[0]], 0),
        jnp.concatenate([routed_pass[6], shared_element[1]], 0),
    )
    before_all = seq_prefix(joint, False)
    routed_prefix = before_all[1][:routed_count]
    shared_seq = (before_all[0][routed_count:], before_all[1][routed_count:])
    shared_prefix = shared_seq[1]
    routed_out = routed_pass[3] + carried(routed_pass[10], routed_pass[0], routed_prefix)
    routed_half = routed_out.astype(jnp.bfloat16).reshape(MEM_DEV, H, length, DK)
    returned = lax.all_to_all(
        route_rows(routed_half, groups), "mem", split_axis=0, concat_axis=0, tiled=True
    )
    routed_sum = (
        returned.reshape(memories * CAP, features)[slot_index]
        .reshape(SHARD_STEPS, 2, features)
        .astype(jnp.float32)
        .sum(1)
    )
    shared_out = (shared_pass[3] + carried(shared_pass[10], shared_pass[0], shared_prefix)).astype(
        jnp.bfloat16
    )
    outgoing = shared_out.transpose(1, 0, 2).reshape(groups * SHARD_STEPS, 1, per_device * DK)
    shared_back = lax.all_to_all(outgoing, "mem", split_axis=0, concat_axis=1, tiled=True).reshape(
        SHARD_STEPS, features
    )
    output = (routed_sum + shared_back.astype(jnp.float32)).astype(jnp.bfloat16)
    cotan_table = jnp.concatenate([cotan_rows, jnp.zeros((1, features), jnp.bfloat16)], 0)
    cotan_slots = cotan_table[slot_table].reshape(groups, MEM_DEV, CAP, features)
    arrived_cotan = lax.all_to_all(cotan_slots, "mem", split_axis=0, concat_axis=0, tiled=True)
    routed_cotan = route_streams(arrived_cotan, H).reshape(routed_count, length, DK)
    shared_cotan_in = lax.all_to_all(
        cotan_rows.reshape(SHARD_STEPS, groups, per_device * DK),
        "mem",
        split_axis=1,
        concat_axis=0,
        tiled=True,
    )
    shared_cotan = (
        shared_cotan_in[:, 0].reshape(groups * SHARD_STEPS, per_device, DK).transpose(1, 0, 2)
    )
    routed_carry = read_carry(routed_pass[10], routed_pass[0], routed_cotan)
    shared_carry = read_carry(shared_pass[10], shared_pass[0], shared_cotan)
    shared_grad_element = (shared_pass[5], shared_carry)
    joint_grad = (
        jnp.concatenate([routed_pass[5], shared_grad_element[0]], 0),
        jnp.concatenate([routed_carry, shared_grad_element[1]], 0),
    )
    after_all = seq_prefix(joint_grad, True)
    routed_grad_state = after_all[1][:routed_count]
    shared_after = (after_all[0][routed_count:], after_all[1][routed_count:])
    shared_grad_state = shared_after[1]
    routed_grads = local_backward(
        routed_raw_values, routed_cotan, routed_pass, routed_prefix, routed_grad_state
    )
    grad_query_slots = routed_grads[0].reshape(MEM_DEV, H, length, DK) * factor
    grad_key_slots = routed_grads[1].reshape(MEM_DEV, H, length, DK)
    grad_value_slots = routed_grads[2].reshape(MEM_DEV, H, length, DK)
    grad_stack = jnp.stack(
        [
            route_rows(grad_query_slots.astype(jnp.bfloat16), groups),
            route_rows(grad_key_slots.astype(jnp.bfloat16), groups),
            route_rows(grad_value_slots.astype(jnp.bfloat16), groups),
        ],
        3,
    )
    returned_grads = lax.all_to_all(grad_stack, "mem", split_axis=0, concat_axis=0, tiled=True)
    routed_grad_sum = (
        returned_grads.reshape(memories * CAP, 3, features)[slot_index]
        .reshape(SHARD_STEPS, 2, 3, features)
        .astype(jnp.float32)
        .sum(1)
    )
    shared_grads = local_backward(
        shared_streams[2], shared_cotan, shared_pass, shared_prefix, shared_grad_state
    )
    shared_stack = jnp.stack(
        [
            (shared_grads[0] * scale).astype(jnp.bfloat16),
            shared_grads[1].astype(jnp.bfloat16),
            shared_grads[2].astype(jnp.bfloat16),
        ],
        0,
    )
    outgoing_grads = shared_stack.transpose(2, 0, 1, 3).reshape(
        groups * SHARD_STEPS, 3, 1, per_device * DK
    )
    shared_grad_back = lax.all_to_all(
        outgoing_grads, "mem", split_axis=0, concat_axis=2, tiled=True
    ).reshape(SHARD_STEPS, 3, features)
    grads_all = (routed_grad_sum + shared_grad_back.astype(jnp.float32)).astype(jnp.bfloat16)
    return (
        output.reshape(1, SHARD_STEPS, features),
        grads_all[:, 0].reshape(1, SHARD_STEPS, features),
        grads_all[:, 1].reshape(1, SHARD_STEPS, features),
        grads_all[:, 2].reshape(1, SHARD_STEPS, features),
    )


def solution(mesh):
    return jax.shard_map(
        body,
        mesh=mesh,
        in_specs=(
            P(("seqi", "seqo"), "mem", None),
            P(("seqi", "seqo"), "mem", None),
            P(("seqi", "seqo"), "mem", None),
            P(None, ("seqi", "seqo"), "mem"),
            P(("seqi", "seqo"), "mem", None),
            P(("seqi", "seqo"), "mem", None),
            P(("seqi", "seqo"), "mem", None),
        ),
        out_specs=(
            P(("seqi", "seqo"), "mem", None),
            P(("seqi", "seqo"), "mem", None),
            P(("seqi", "seqo"), "mem", None),
            P(("seqi", "seqo"), "mem", None),
        ),
        check_vma=False,
    )
```

profile of v0, /device:TPU:0, one launch (start us, length us, event | category | flops | bytes accessed | tf_op | source)
XLA Modules:
  0.0 778.7 jit_solution(4326349134215656997)
XLA Ops:
  47.9 5.0 all-to-all-done.8
  63.4 7.1 all-to-all-done.7
  81.3 13.3 %gather_fusion = bf16[320,3,2048]{2,1,0:T(4,128)(2,1)} fusion(bf16[129,3,2048]{2,1,0:T(4,128)(2,1)S(1)} %fusion.44, s32[1024]{0:T(1024)S(1)} %pad_clamp_fusion.1), kind=kCustom, calls=%fused_computation | custom fusion | bytes 7865600 | tf_op jit(solution)/shard_map/gather | solution.py:261
  94.6 7.3 copy.285
  101.8 5.0 all-to-all-start
  120.9 26.1 %all-to-all-done = bf16[4,1,80,3,2048]{4,2,3,1,0:T(8,128)(2,1)} async-done(((bf16[4,1,80,3,2048]{4,2,3,1,0:T(8,128)(2,1)}), bf16[4,1,80,3,2048]{4,2,3,1,0:T(8,128)(2,1)}, u32[]{:S(2)}, u32[]{:S(2)}) %all-to-all-start) | async-done | bytes 3932192 | tf_op jit(solution)/shard_map/all_to_all | solution.py:266
  170.1 65.8 %all-reduce.4 = f32[640]{0:T(1024)S(1)} all-reduce(f32[640]{0:T(1024)S(1)} %maximum_dynamic-update-slice_fusion), channel_id=2, replica_groups=mesh['mem'=4,'seqi'=8,'seqo'=4] {'seqi','seqo'}, use_global_device_ids=true, to_apply=%add.4 | all-reduce | flops 640 | bytes 5120
  248.6 15.7 %while.90 = (s32[]{:T(128)}, f32[4,128,128]{2,1,0:T(8,128)}, f32[4,4,128,128]{3,2,1,0:T(8,128)}, f32[4,4]{1,0:T(4,128)}, f32[4,4,128,128]{3,2,0,1:T(8,128)}, /*index=5*/s32[]{:T(128)}, s32[]{:T(128)}) while((s32[]{:T(128)}, f32[4,128,128]{2,1,0:T(8,128)}, f32[4,4,128,128]{3,2,1,0:T(8,128)}, f32[4,4]{1,0:T(4,128)}, ...), condition=%wide.region_16.17_spmd.clone, body=%wide.region_15.16_spmd.clone.sunk | while | flops 262147 | bytes 1311376 | solution.py:88
  282.0 15.8 %while.93 = (s32[]{:T(128)}, f32[4,128,128]{2,1,0:T(8,128)}, f32[4,4,128,128]{3,2,1,0:T(8,128)}, f32[4,4]{1,0:T(4,128)}, f32[4,4,128,128]{3,2,0,1:T(8,128)}, /*index=5*/s32[]{:T(128)}, s32[]{:T(128)}, s32[]{:T(128)}) while((s32[]{:T(128)}, f32[4,128,128]{2,1,0:T(8,128)}, f32[4,4,128,128]{3,2,1,0:T(8,128)}, f32[4,4]{1,0:T(4,128)}, ...), condition=%wide.region_23.24_spmd.clone, body=%wide.region_22.23_spmd.clone.sunk | while | flops 262148 | bytes 1310888 | solution.py:178
  317.7 5.4 fusion.38
  323.1 5.4 fusion.35
  331.5 16.6 %while.91 = (s32[]{:T(128)}, f32[16,128,128]{2,1,0:T(8,128)S(1)}, f32[5,16,128,128]{3,2,1,0:T(8,128)}, f32[5,16]{1,0:T(8,128)}, f32[5,16,128,128]{3,2,0,1:T(8,128)}, /*index=5*/s32[]{:T(128)}, s32[]{:T(128)}, s32[]{:T(128)}) while((s32[]{:T(128)}, f32[16,128,128]{2,1,0:T(8,128)S(1)}, f32[5,16,128,128]{3,2,1,0:T(8,128)}, ...), condition=%wide.region_18.19_spmd.clone, body=%wide.region_17.18_spmd.clone.sunk | while | flops 1048580 | bytes 5243192 | solution.py:178
  348.1 5.9 fusion.6
  357.0 16.3 %while.88 = (s32[]{:T(128)}, f32[16,128,128]{2,1,0:T(8,128)S(1)}, f32[5,16,128,128]{3,2,1,0:T(8,128)}, f32[5,16]{1,0:T(8,128)}, f32[5,16,128,128]{3,2,0,1:T(8,128)}, /*index=5*/s32[]{:T(128)}, s32[]{:T(128)}) while((s32[]{:T(128)}, f32[16,128,128]{2,1,0:T(8,128)S(1)}, f32[5,16,128,128]{3,2,1,0:T(8,128)}, f32[5,16]{1,0:T(8,128)}, ...), condition=%wide.region_7.8_spmd.clone, body=%wide.region_6.7_spmd.clone.sunk | while | flops 1048579 | bytes 5243680 | solution.py:88
  373.4 5.8 fusion.12
  396.5 29.3 %rev.7 = f32[32,20,128,128]{3,2,1,0:T(8,128)} reverse(f32[32,20,128,128]{3,2,1,0:T(8,128)} %bitcast.465), dimensions={0} | reverse | bytes 83886080 | tf_op jit(solution)/shard_map/rev | solution.py:22
  425.8 5.3 all-gather.6.cloned.1.call-done
  431.1 71.8 %while.89 = (s32[]{:T(128)}, f32[20,128,128]{2,1,0:T(8,128)S(1)}, s32[]{:T(128)}, f32[32,20]{1,0:T(8,128)}, f32[32,20,128,128]{3,2,1,0:T(8,128)}, /*index=5*/s32[]{:T(128)}, s32[]{:T(128)}) while((s32[]{:T(128)}, f32[20,128,128]{2,1,0:T(8,128)S(1)}, s32[]{:T(128)}, f32[32,20]{1,0:T(8,128)}, f32[32,20,128,128]{3,2,1,0:T(8,128)}, ...), condition=%wide.region_13.14_spmd.clone, body=%wide.region_12.13_spmd.clone.sunk | while | flops 1310724 | bytes 3932505 | solution.py:32
  527.3 114.9 %while.92 = (s32[]{:T(128)}, f32[20,128,128]{2,1,0:T(8,128)}, s32[]{:T(128)}, f32[32,20]{1,0:T(8,128)}, f32[32,20,128,128]{3,2,1,0:T(8,128)}, /*index=5*/s32[]{:T(128)}, s32[]{:T(128)}) while((s32[]{:T(128)}, f32[20,128,128]{2,1,0:T(8,128)}, s32[]{:T(128)}, f32[32,20]{1,0:T(8,128)}, f32[32,20,128,128]{3,2,1,0:T(8,128)}, ...), condition=%wide.region_20.21_spmd.clone, body=%wide.region_19.20_spmd.clone.sunk | while | flops 1310724 | bytes 3932505 | solution.py:32
  687.2 5.0 all-to-all-start.9
  717.3 20.2 %all-to-all-done.9 = bf16[4,1,80,3,2048]{4,2,3,1,0:T(8,128)(2,1)} async-done(((bf16[4,1,80,3,2048]{4,2,3,1,0:T(8,128)(2,1)}), bf16[4,1,80,3,2048]{4,2,3,1,0:T(8,128)(2,1)}, u32[]{:S(2)}, u32[]{:S(2)}) %all-to-all-start.9) | async-done | bytes 3932192 | tf_op jit(solution)/shard_map/all_to_all | solution.py:377
  737.6 7.9 %copy.342 = bf16[4,1,80,3,2048]{4,3,2,0,1:T(4,128)(2,1)} copy(bf16[4,1,80,3,2048]{4,2,3,1,0:T(8,128)(2,1)} %all-to-all-done.9) | data formatting | bytes 7864320 | tf_op jit(solution)/shard_map/all_to_all | solution.py:377
  745.4 12.7 %gather_fusion.4 = bf16[256,3,2048]{2,1,0:T(4,128)(2,1)} fusion(bf16[320,3,2048]{2,1,0:T(4,128)(2,1)} %bitcast.473, s32[1024]{0:T(1024)S(1)} %pad_clamp_fusion), kind=kCustom, calls=%fused_computation.4 | custom fusion | bytes 6292480 | tf_op jit(solution)/shard_map/gather | solution.py:379
  758.1 6.3 convert_reduce_fusion
  (543 shorter events, 522.7 us)
Async XLA Ops:
  7.2 37.7 %copy-start.46 = (bf16[1,128,2048]{2,1,0:T(8,128)(2,1)S(1)}, bf16[1,128,2048]{2,1,0:T(8,128)(2,1)}, u32[]{:S(2)}) copy-start(bf16[1,128,2048]{2,1,0:T(8,128)(2,1)} %param.25) | copy-start | bytes 1572868
  14.7 9.6 %all-to-all-start.1 = ((bf16[4,1,80]{2,1,0:T(2,128)(2,1)}), bf16[4,1,80]{2,1,0:T(2,128)(2,1)S(1)}, u32[]{:S(2)}, u32[]{:S(2)}) async-start(bf16[4,1,80]{2,1,0:T(2,128)(2,1)} %reshape.436), calls=%async_computation.1 | async-start | bytes 4096 | tf_op jit(solution)/shard_map/all_to_all | solution.py:268
  24.3 8.5 %all-to-all-start.3 = ((bf16[128,4,4]{0,2,1:T(4,128)(2,1)}), bf16[128,4,4]{0,2,1:T(4,128)(2,1)S(1)}, u32[]{:S(2)}, u32[]{:S(2)}) async-start(bf16[128,4,4]{0,2,1:T(4,128)(2,1)} %bitcast.535), calls=%async_computation.3 | async-start | bytes 8192 | tf_op jit(solution)/shard_map/all_to_all | solution.py:297
  32.8 8.6 %all-to-all-start.2 = ((bf16[4,1,80,16]{2,3,1,0:T(8,128)(2,1)}), bf16[4,1,80,16]{2,3,1,0:T(8,128)(2,1)S(1)}, u32[]{:S(2)}, u32[]{:S(2)}) async-start(bf16[4,1,80,16]{2,3,1,0:T(8,128)(2,1)} %copy.291), calls=%async_computation.2 | async-start | bytes 32768 | tf_op jit(solution)/shard_map/all_to_all | solution.py:267
  41.4 11.5 %all-to-all-start.8 = ((bf16[128,4,512]{2,0,1:T(8,128)(2,1)}), bf16[128,4,512]{2,0,1:T(8,128)(2,1)S(1)}, u32[]{:S(2)}, u32[]{:S(2)}) async-start(bf16[128,4,512]{2,0,1:T(8,128)(2,1)} %copy.334), calls=%async_computation.8 | async-start | bytes 1048576 | tf_op jit(solution)/shard_map/all_to_all | solution.py:342
  53.7 16.8 %all-to-all-start.7 = ((bf16[4,1,80,2048]{3,2,1,0:T(8,128)(2,1)}), bf16[4,1,80,2048]{3,2,1,0:T(8,128)(2,1)S(1)}, u32[]{:S(2)}, u32[]{:S(2)}) async-start(bf16[4,1,80,2048]{3,2,1,0:T(8,128)(2,1)} %bitcast.64), calls=%async_computation.7 | async-start | bytes 2621440 | tf_op jit(solution)/shard_map/all_to_all | solution.py:340
  70.5 31.3 %all-to-all-start.4 = ((bf16[128,4,3,512]{3,0,2,1:T(8,128)(2,1)}), bf16[128,4,3,512]{3,0,2,1:T(8,128)(2,1)}, u32[]{:S(2)}, u32[]{:S(2)}) async-start(bf16[128,4,3,512]{3,0,2,1:T(8,128)(2,1)} %copy.312), calls=%async_computation.4 | async-start | bytes 3145728 | tf_op jit(solution)/shard_map/all_to_all | solution.py:296
  101.8 45.2 %all-to-all-start = ((bf16[4,1,80,3,2048]{4,2,3,1,0:T(8,128)(2,1)}), bf16[4,1,80,3,2048]{4,2,3,1,0:T(8,128)(2,1)}, u32[]{:S(2)}, u32[]{:S(2)}) async-start(bf16[4,1,80,3,2048]{4,2,3,1,0:T(8,128)(2,1)} %copy.285), calls=%async_computation | async-start | bytes 7864320 | tf_op jit(solution)/shard_map/all_to_all | solution.py:266
  106.8 289.7 %all-gather.8.cloned.1.call-start = ((), (), s32[]{:S(2)}) async-start(), calls=%async_computation.12 | async-start | bytes 43253760 | tf_op jit(solution)/shard_map/all_gather | solution.py:20
  107.3 46.3 %copy-start.65 = (f32[320]{0:T(512)}, f32[320]{0:T(512)S(1)}, u32[]{:S(2)}) copy-start(f32[320]{0:T(512)S(1)} %mul.405) | copy-start | bytes 3844
  110.4 47.2 %copy-start.58 = (f32[4,512]{1,0:T(4,128)}, f32[4,512]{1,0:T(4,128)S(1)}, u32[]{:S(2)}) copy-start(f32[4,512]{1,0:T(4,128)S(1)} %get-tuple-element.744) | copy-start | bytes 24580
  111.9 41.7 %copy-start.53 = (f32[16,320]{1,0:T(8,128)}, f32[16,320]{1,0:T(8,128)S(1)}, u32[]{:S(2)}) copy-start(f32[16,320]{1,0:T(8,128)S(1)} %get-tuple-element.741) | copy-start | bytes 61444
  112.0 48.9 %copy-start.51 = (f32[16,320]{1,0:T(8,128)}, f32[16,320]{1,0:T(8,128)S(1)}, u32[]{:S(2)}) copy-start(f32[16,320]{1,0:T(8,128)S(1)} %get-tuple-element.742) | copy-start | bytes 61444
  113.5 40.1 %copy-start.1 = (bf16[1,16,4,80,128]{4,3,2,1,0:T(8,128)(2,1)}, bf16[1,16,4,80,128]{4,3,2,1,0:T(8,128)(2,1)S(1)}, u32[]{:S(2)}) copy-start(bf16[1,16,4,80,128]{4,3,2,1,0:T(8,128)(2,1)S(1)} %copy.327) | copy-start | bytes 3932164
  119.2 38.4 %copy-start.12 = (bf16[512,3,4,128]{3,0,2,1:T(8,128)(2,1)}, bf16[512,3,4,128]{3,0,2,1:T(8,128)(2,1)S(1)}, u32[]{:S(2)}) copy-start(bf16[512,3,4,128]{3,0,2,1:T(8,128)(2,1)S(1)} %copy.439) | copy-start | bytes 4718596
  157.5 273.6 %all-gather.6.cloned.1.call-start = ((), (), s32[]{:S(2)}) async-start(), calls=%async_computation.11 | async-start | bytes 43253760 | tf_op jit(solution)/shard_map/all_gather | solution.py:20
  248.6 15.7 %copy-start.60 = (f32[4,4,128]{2,1,0:T(4,128)S(1)}, f32[4,4,128]{2,1,0:T(4,128)}, u32[]{:S(2)}) copy-start(f32[4,4,128]{2,1,0:T(4,128)} %get-tuple-element.747) | copy-start | bytes 24580
  282.0 15.8 %copy-start.56 = (f32[4,4,128]{2,1,0:T(4,128)S(1)}, f32[4,4,128]{2,1,0:T(4,128)}, u32[]{:S(2)}) copy-start(f32[4,4,128]{2,1,0:T(4,128)} %get-tuple-element.748) | copy-start | bytes 24580
  305.9 17.2 %copy-start.10 = (bf16[1,16,4,80,128]{4,3,2,1,0:T(8,128)(2,1)}, bf16[1,16,4,80,128]{4,3,2,1,0:T(8,128)(2,1)S(1)}, u32[]{:S(2)}) copy-start(bf16[1,16,4,80,128]{4,3,2,1,0:T(8,128)(2,1)S(1)} %copy.286) | copy-start | bytes 3932164
  509.4 14.1 %all-to-all-start.6 = ((bf16[4,2,32768]{2,1,0:T(2,128)(2,1)}), bf16[4,2,32768]{2,1,0:T(2,128)(2,1)S(1)}, u32[]{:S(2)}, u32[]{:S(2)}) async-start(bf16[4,2,32768]{2,1,0:T(2,128)(2,1)} %reshape.455), calls=%async_computation.6 | async-start | bytes 1048576 | tf_op jit(solution)/shard_map/all_to_all | solution.py:334
  523.6 131.3 %all-to-all-start.5 = ((bf16[4,1,80,2048]{3,2,1,0:T(8,128)(2,1)}), bf16[4,1,80,2048]{3,2,1,0:T(8,128)(2,1)S(1)}, u32[]{:S(2)}, u32[]{:S(2)}) async-start(bf16[4,1,80,2048]{3,2,1,0:T(8,128)(2,1)} %bitcast.503), calls=%async_computation.5 | async-start | bytes 2621440 | tf_op jit(solution)/shard_map/all_to_all | solution.py:321
  527.3 114.9 %copy-start.59 = (f32[4,512]{1,0:T(4,128)S(1)}, f32[4,512]{1,0:T(4,128)}, u32[]{:S(2)}) copy-start(f32[4,512]{1,0:T(4,128)} %copy-done.58) | copy-start | bytes 24580
  654.8 32.4 %all-to-all-start.10 = ((bf16[512,3,1,512]{3,1,2,0:T(4,128)(2,1)}), bf16[512,3,1,512]{3,1,2,0:T(4,128)(2,1)}, u32[]{:S(2)}, u32[]{:S(2)}) async-start(bf16[512,3,1,512]{3,1,2,0:T(4,128)(2,1)} %copy.358), calls=%async_computation.10 | async-start | bytes 4194304 | tf_op jit(solution)/shard_map/all_to_all | solution.py:398
  687.2 50.4 %all-to-all-start.9 = ((bf16[4,1,80,3,2048]{4,2,3,1,0:T(8,128)(2,1)}), bf16[4,1,80,3,2048]{4,2,3,1,0:T(8,128)(2,1)}, u32[]{:S(2)}, u32[]{:S(2)}) async-start(bf16[4,1,80,3,2048]{4,2,3,1,0:T(8,128)(2,1)} %copy.341), calls=%async_computation.9 | async-start | bytes 7864320 | tf_op jit(solution)/shard_map/all_to_all | solution.py:377
  (68 other events, 297.3 us)
Sparse Core Ops, SparseCore 0:
  157.6 136.5 all-gather.7
  296.5 134.5 all-gather.5
where the time goes:
time: 792 us; the launch traced here: 779 us
  local copies, waits for them, and re-layouts  235 us (30%)
  other arithmetic  235 us (30%)
  matrix products  104 us (13%)
  waiting for transfers between devices  76.1 us (10%)
  blocking collectives  65.8 us (8%)
  starting transfers between devices  45.8 us (6%)
  between operations  16.6 us (2%)
    select_n x62, other arithmetic, hop(): jnp.where(position < mine, new, old)  144 us
    unnamed x1, blocking collectives  65.8 us
    mul x62, local copies, waits for them, and re-layouts, combine(): later[0][:, None, None] * earlier[1] + later[1]  42.5 us
    rev x2, local copies, waits for them, and re-layouts, entering(): pieces = jax.tree.map(lambda part: part[::-1], pieces)  30 us
    all_to_all x1, waiting for transfers between devices, body(): lax.all_to_all(packed, 'mem', split_axis=0, concat_axis=0, tiled=True)  26.1 us
    dynamic_update_slice x18, other arithmetic, local_pass(): lax.scan(advance, start, (stretch_decay.T, stretch_state.transpose(1, 0,...  22.4 us
    all_to_all x1, waiting for transfers between devices, body(): lax.all_to_all(grad_stack, 'mem', split_axis=0, concat_axis=0, tiled=True)  20.2 us
    unnamed x177, local copies, waits for them, and re-layouts  18.2 us
  transfers between devices with their start and end apart: 13, of which 9 were waited for; matrix products, arithmetic and copies ran while one was open for 56% of the time, Pallas kernels for 0%

commit v1 on v0

v1 whole, which is shorter than its diff:
```python
import math

import jax
import jax.numpy as jnp
from jax import lax
from jax.experimental import pallas as pl
from jax.experimental.pallas import tpu as pltpu
from jax.sharding import PartitionSpec as P

H = 16
DK = 128
ROWS = 128
MEMS = 4
KINDS = MEMS + 1
GX = 4
GY = 4
GZ = 4
PIECES = 2
LOCAL = H // GX
HP = LOCAL // PIECES
WIDE = HP * DK
MESSAGE = 4 * ROWS + 16
PART = DK // GY
STATE = (2, HP, KINDS, PART, DK)
HALF = (HP, KINDS, PART, DK)
BIG = 1e30
F32 = jnp.float32
BF16 = jnp.bfloat16
MIB = 1 << 20

NT = (((1,), (1,)), ((), ()))
TN = (((0,), (0,)), ((), ()))
NN = (((1,), (0,)), ((), ()))


def mm(a, b, dims=NN):
    return lax.dot_general(a, b, dims, preferred_element_type=F32)


def vmem(count):
    return [pl.BlockSpec(memory_space=pltpu.VMEM)] * count


def smem():
    return pl.BlockSpec(memory_space=pltpu.SMEM)


def params(flops, moved):
    return dict(
        compiler_params=pltpu.CompilerParams(vmem_limit_bytes=40 * MIB),
        cost_estimate=pl.CostEstimate(flops=flops, bytes_accessed=moved, transcendentals=0),
    )


def shape(dims, dtype):
    return jax.ShapeDtypeStruct(dims, dtype)


def pack_kernel(piece, where, q, k, v, dy, gates, meta, *refs):
    outs, small, sems = refs[:GX], refs[GX], refs[GX + 1]
    x = where[0]
    row = lax.broadcasted_iota(jnp.int32, (16, DK), 0)
    copies = []
    for hop in range(GX):
        head = lax.rem(x + hop, GX) * LOCAL + piece * HP
        lanes = pl.ds(pl.multiple_of(head * DK, DK), WIDE)
        for n, ref in enumerate((q, k, v, dy)):
            copy = pltpu.make_async_copy(
                ref.at[0, :, lanes], outs[hop].at[pl.ds(n * ROWS, ROWS), :], sems.at[hop, n]
            )
            copy.start()
            copies.append(copy)
    for hop in range(GX):
        head = lax.rem(x + hop, GX) * LOCAL + piece * HP
        rows = meta[...]
        for i in range(HP):
            rows = jnp.where(row == i, gates[head + i].astype(F32), rows)
        small[hop] = jnp.concatenate([rows.astype(BF16)] * HP, 1)
        copy = pltpu.make_async_copy(
            small.at[hop], outs[hop].at[pl.ds(4 * ROWS, 16), :], sems.at[hop, 4]
        )
        copy.start()
        copies.append(copy)
    for copy in copies:
        copy.wait()


def pack(piece, where, q, k, v, dy, gates, meta):
    hbm = pl.BlockSpec(memory_space=pl.ANY)
    return pl.pallas_call(
        lambda *refs: pack_kernel(piece, *refs),
        out_shape=[shape((MESSAGE, WIDE), BF16)] * GX,
        in_specs=[smem()] + [hbm] * 4 + vmem(2),
        out_specs=[hbm] * GX,
        scratch_shapes=[pltpu.VMEM((GX, 16, WIDE), BF16), pltpu.SemaphoreType.DMA((GX, 5))],
        **params(0, 2 * MIB),
        name="pack",
    )(where, q, k, v, dy, gates, meta)


def token_weights(buf):
    mask_rows, weight_rows, gate_rows = [], [], []
    row = lax.broadcasted_iota(jnp.int32, (8, DK), 0)
    for j in range(GX):
        small = buf[j, 4 * ROWS : MESSAGE, 0:DK].astype(F32)
        first, second = small[8:9], small[9:10]
        first_weight, second_weight = small[10:11], small[11:12]
        kind = row.astype(F32)
        hit_first = (kind == first).astype(F32)
        hit_second = (kind == second).astype(F32)
        mask = jnp.where(row < MEMS, hit_first + hit_second, (row == MEMS).astype(F32))
        weight = jnp.where(
            row < MEMS,
            hit_first * first_weight + hit_second * second_weight,
            (row == MEMS).astype(F32),
        )
        for h in range(HP):
            mask_rows.append(mask)
            weight_rows.append(weight)
            gate_rows.append(mask * small[h : h + 1])
    return tuple(jnp.concatenate(r, 0) for r in (mask_rows, weight_rows, gate_rows))


def triangle():
    t = lax.broadcasted_iota(jnp.int32, (DK, DK), 0)
    s = lax.broadcasted_iota(jnp.int32, (DK, DK), 1)
    return t, s


def order_tokens(x, buf, messages):
    for hop in range(GX):
        buf[lax.rem(x + GX - hop, GX)] = messages[hop][...]


def states_kernel(scale, where, m0, m1, m2, m3, o0, o1, o2, o3, buf, acc):
    x, y = where[0], where[1]
    order_tokens(x, buf, (m0, m1, m2, m3))
    mask, weight, gate = token_weights(buf)
    t, s = triangle()
    gate = gate.astype(BF16)
    upper = (t <= s).astype(BF16)
    running = mm(gate, upper)
    total = mm(gate, jnp.ones((DK, DK), BF16))
    size = HP * 8
    part = lambda a, j: a[j * size : (j + 1) * size]
    write_rows, read_rows = [], []
    for j in range(GX):
        later = sum([part(total, i) for i in range(j + 1, GX)], part(total, j))
        before = sum([part(total, i) for i in range(j)], jnp.zeros((size, DK), F32))
        write_rows.append(part(mask, j) * jnp.exp(later - part(running, j)))
        read_rows.append(part(weight, j) * scale * jnp.exp(before + part(running, j)))
    for h in range(HP):
        lanes = slice(h * DK, (h + 1) * DK)
        for side, (left, right, rows) in enumerate(((1, 2, write_rows), (0, 3, read_rows))):
            sums = None
            for j in range(GX):
                turned = buf[j, left * ROWS : (left + 1) * ROWS, lanes].astype(F32).T
                stacked = jnp.concatenate(
                    [(turned * rows[j][h * 8 + e : h * 8 + e + 1]).astype(BF16) for e in range(KINDS)], 0
                )
                term = mm(stacked, buf[j, right * ROWS : (right + 1) * ROWS, lanes])
                sums = term if sums is None else sums + term
            acc[side, h] = sums.reshape(KINDS, DK, DK).astype(BF16)
    for hop, out in enumerate((o0, o1, o2, o3)):
        there = lax.rem(y + hop, GY)
        out[...] = acc[:, :, :, pl.ds(pl.multiple_of(there * PART, PART), PART), :]


def states(scale, where, messages):
    return pl.pallas_call(
        lambda *refs: states_kernel(scale, *refs),
        out_shape=[shape(STATE, BF16)] * GY,
        in_specs=[smem()] + vmem(GX),
        out_specs=vmem(GY),
        scratch_shapes=[
            pltpu.VMEM((GX, MESSAGE, WIDE), BF16),
            pltpu.VMEM((2, HP, KINDS, DK, DK), BF16),
        ],
        **params(600_000_000 * HP, 2 * MIB),
        name="states",
    )(where, *messages)


TS, TG, BTW, MINE, SIB, TABLE = 0, 4, 8, 24, 32, 40


def column(piece, h, e):
    return (piece * HP + h) * 8 + e


def group_kernel(piece, where, table, s0, s1, s2, s3, own, z1, z2, z3):
    y, z = where[1], where[2]
    parts = (s0, s1, s2, s3)
    for h in range(HP):
        for e in range(KINDS):
            col = column(piece, h, e)
            both = []
            for side, base in ((0, TS), (1, TG)):
                acc = jnp.zeros((PART, DK), F32)
                for hop in range(GY):
                    source = lax.rem(y + GY - hop, GY)
                    acc = acc + table[base + source, col] * parts[hop][side, h, e].astype(F32)
                own[side, h, e] = acc
                both.append(acc)
            for hop, out in ((1, z1), (2, z2), (3, z3)):
                ahead = (z + hop < GZ).astype(F32)
                out[h, e] = (ahead * both[0] + (1.0 - ahead) * both[1]).astype(BF16)


def group(piece, where, table, parts):
    return pl.pallas_call(
        lambda *refs: group_kernel(piece, *refs),
        out_shape=[shape(STATE, F32)] + [shape(HALF, BF16)] * 3,
        in_specs=[smem(), smem()] + vmem(GY),
        out_specs=vmem(4),
        **params(10_000_000, 2 * MIB),
        name="group",
    )(where, table, *parts)


def across_kernel(piece, where, table, own, z1, z2, z3, mine, sib):
    z, c = where[2], where[3]
    first = (c == 0).astype(F32)
    for h in range(HP):
        for e in range(KINDS):
            col = column(piece, h, e)
            to_mine = [jnp.zeros((PART, DK), F32)] * 2
            to_sib = [first * own[0, h, e], (1.0 - first) * own[1, h, e]]
            for hop, ref in ((1, z1), (2, z2), (3, z3)):
                source = lax.rem(z + GZ - hop, GZ)
                ahead = (source < z).astype(F32)
                block = ref[h, e].astype(F32)
                near = table[MINE + source * 2 + c, col]
                far = table[SIB + source * 2 + c, col]
                for side, keep in ((0, ahead), (1, 1.0 - ahead)):
                    to_mine[side] = to_mine[side] + (near * keep) * block
                    to_sib[side] = to_sib[side] + (far * keep) * block
            for side in range(2):
                mine[side, h, e] = to_mine[side]
                sib[side, h, e] = to_sib[side].astype(BF16)


def across(piece, where, table, own, arrived):
    return pl.pallas_call(
        lambda *refs: across_kernel(piece, *refs),
        out_shape=[shape(STATE, F32), shape(STATE, BF16)],
        in_specs=[smem(), smem()] + vmem(4),
        out_specs=vmem(2),
        **params(10_000_000, 2 * MIB),
        name="across",
    )(where, table, own, *arrived)


def entering_kernel(piece, where, table, mine, sib, s0, s1, s2, s3, o0, o1, o2, o3):
    y = where[1]
    parts = (s0, s1, s2, s3)
    for h in range(HP):
        for e in range(KINDS):
            col = column(piece, h, e)
            for side, base in ((0, TG), (1, TS)):
                start = mine[side, h, e] + sib[side, h, e].astype(F32)
                blocks = [p[side, h, e].astype(F32) for p in parts]
                for hop, out in enumerate((o0, o1, o2, o3)):
                    there = lax.rem(y + hop, GY)
                    acc = table[base + there, col] * start
                    for back in range(GY):
                        source = lax.rem(y + GY - back, GY)
                        counts = (source < there) if side == 0 else (source > there)
                        factor = table[BTW + source * GY + there, col] * counts.astype(F32)
                        acc = acc + factor * blocks[back]
                    out[side, h, e] = acc.astype(BF16)


def entering(piece, where, table, mine, sib, parts):
    return pl.pallas_call(
        lambda *refs: entering_kernel(piece, *refs),
        out_shape=[shape(STATE, BF16)] * GY,
        in_specs=[smem(), smem()] + vmem(6),
        out_specs=vmem(GY),
        **params(20_000_000, 2 * MIB),
        name="entering",
    )(where, table, mine, sib, *parts)


def spread(block, cols, r):
    return [(block * cols[:, r + e : r + e + 1]).astype(BF16) for e in range(KINDS)]


def within_kernel(scale, where, m0, m1, m2, m3, res, buf, state, late):
    x = where[0]
    order_tokens(x, buf, (m0, m1, m2, m3))
    mask, weight, gate = token_weights(buf)
    t, s = triangle()
    gate = gate.astype(BF16)
    lower = t >= s
    eye = (t == s).astype(BF16)
    ones = jnp.ones((DK, DK), BF16)
    running = mm(gate, (t <= s).astype(BF16))
    total = mm(gate, ones)
    decay = jnp.exp(total)
    write_row = mask * jnp.exp(total - running)
    read_row = weight * scale * jnp.exp(running)
    barred = jnp.where(mask > 0, running, BIG)
    running_col = mm(lower.astype(BF16), gate, NT)
    total_col = mm(ones, gate, NT)
    weight_col = mm(eye, weight.astype(BF16), NT) * scale
    mask_col = mm(eye, mask.astype(BF16), NT)
    read_col = weight_col * jnp.exp(running_col)
    write_col = mask_col * jnp.exp(total_col - running_col)

    for h in range(HP):
        lanes = slice(h * DK, (h + 1) * DK)
        for j in range(GX):
            r = (j * HP + h) * 8
            q, k, v, dy = (buf[j, n * ROWS : (n + 1) * ROWS, lanes] for n in range(4))
            near = jnp.zeros((DK, DK), F32)
            for e in range(KINDS):
                near = near + weight_col[:, r + e : r + e + 1] * jnp.exp(
                    running_col[:, r + e : r + e + 1] - barred[r + e : r + e + 1]
                )
            near = jnp.where(lower, near, 0.0)
            scores = (mm(q, k, NT) * near).astype(BF16)
            grads = (mm(dy, v, NT) * near).astype(BF16)
            out = mm(scores, v)
            grad_q = mm(grads, k)
            if j > 0:
                half = state[0, h].astype(BF16)
                wide = jnp.concatenate(spread(q.astype(F32), read_col, r), 1)
                out = out + mm(wide, half.reshape(KINDS * DK, DK))
                for e, block in enumerate(spread(dy.astype(F32), read_col, r)):
                    grad_q = grad_q + mm(block, half[e], NT)
            res[j, 0:ROWS, lanes] = out.astype(BF16)
            res[j, ROWS : 2 * ROWS, lanes] = grad_q.astype(BF16)
            late[j, h, 0] = mm(grads, q, TN)
            late[j, h, 1] = mm(scores, dy, TN)
            if j < GX - 1:
                turned = k.astype(F32).T
                for e in range(KINDS):
                    grown = mm((turned * write_row[r + e : r + e + 1]).astype(BF16), v)
                    if j > 0:
                        grown = grown + decay[r + e : r + e + 1] * state[0, h, e]
                    state[0, h, e] = grown
        for j in range(GX - 1, -1, -1):
            r = (j * HP + h) * 8
            q, k, v, dy = (buf[j, n * ROWS : (n + 1) * ROWS, lanes] for n in range(4))
            grad_k = late[j, h, 0]
            grad_v = late[j, h, 1]
            if j < GX - 1:
                half = state[1, h].astype(BF16)
                wide = jnp.concatenate(spread(k.astype(F32), write_col, r), 1)
                grad_v = grad_v + mm(wide, half.reshape(KINDS * DK, DK))
                for e, block in enumerate(spread(v.astype(F32), write_col, r)):
                    grad_k = grad_k + mm(block, half[e], NT)
            res[j, 2 * ROWS : 3 * ROWS, lanes] = grad_k.astype(BF16)
            res[j, 3 * ROWS : 4 * ROWS, lanes] = grad_v.astype(BF16)
            if j > 0:
                turned = q.astype(F32).T
                for e in range(KINDS):
                    grown = mm((turned * read_row[r + e : r + e + 1]).astype(BF16), dy)
                    if j < GX - 1:
                        grown = grown + decay[r + e : r + e + 1] * state[1, h, e]
                    state[1, h, e] = grown


def within(scale, where, messages):
    return pl.pallas_call(
        lambda *refs: within_kernel(scale, *refs),
        out_shape=shape((GX, 4 * ROWS, WIDE), BF16),
        in_specs=[smem()] + vmem(GX),
        out_specs=pl.BlockSpec(memory_space=pltpu.VMEM),
        scratch_shapes=[
            pltpu.VMEM((GX, MESSAGE, WIDE), BF16),
            pltpu.VMEM((2, HP, KINDS, DK, DK), F32),
            pltpu.VMEM((GX, HP, 2, DK, DK), F32),
        ],
        **params(1_000_000_000 * HP, 4 * MIB),
        name="within",
    )(where, *messages)


def finish_kernel(scale, where, m0, m1, m2, m3, p0, p1, p2, p3, part, o0, o1, o2, o3, buf, state, res):
    x, y = where[0], where[1]
    order_tokens(x, buf, (m0, m1, m2, m3))
    for hop, ref in enumerate((p0, p1, p2, p3)):
        source = lax.rem(y + GY - hop, GY)
        state[:, :, :, pl.ds(pl.multiple_of(source * PART, PART), PART), :] = ref[...]
    mask, weight, gate = token_weights(buf)
    t, s = triangle()
    gate = gate.astype(BF16)
    eye = (t == s).astype(BF16)
    ones = jnp.ones((DK, DK), BF16)
    running = mm((t >= s).astype(BF16), gate, NT)
    total = mm(ones, gate, NT)
    size = HP * 8
    cut = lambda a, j: a[:, j * size : (j + 1) * size]
    zero = jnp.zeros((DK, size), F32)
    before = jnp.concatenate([sum([cut(total, i) for i in range(j)], zero) for j in range(GX)], 1)
    after = jnp.concatenate([sum([cut(total, i) for i in range(j, GX)], zero) for j in range(GX)], 1)
    read_col = mm(eye, weight.astype(BF16), NT) * scale * jnp.exp(before + running)
    write_col = mm(eye, mask.astype(BF16), NT) * jnp.exp(after - running)
    for h in range(HP):
        lanes = slice(h * DK, (h + 1) * DK)
        for j in range(GX):
            r = (j * HP + h) * 8
            q, k, v, dy = (buf[j, n * ROWS : (n + 1) * ROWS, lanes].astype(F32) for n in range(4))
            for n, source, side, cols, dims in (
                (0, q, 0, read_col, NN),
                (1, dy, 0, read_col, NT),
                (2, v, 1, write_col, NT),
                (3, k, 1, write_col, NN),
            ):
                rows = slice(n * ROWS, (n + 1) * ROWS)
                acc = part[j, rows, lanes].astype(F32)
                blocks = spread(source, cols, r)
                if dims is NN:
                    acc = acc + mm(jnp.concatenate(blocks, 1), state[side, h].reshape(KINDS * DK, DK))
                else:
                    for e, block in enumerate(blocks):
                        acc = acc + mm(block, state[side, h, e], NT)
                res[j, rows, lanes] = acc.astype(BF16)
    for hop, out in enumerate((o0, o1, o2, o3)):
        out[...] = res[lax.rem(x + hop, GX)]


def finish(scale, where, messages, prefixes, part):
    return pl.pallas_call(
        lambda *refs: finish_kernel(scale, *refs),
        out_shape=[shape((4 * ROWS, WIDE), BF16)] * GX,
        in_specs=[smem()] + vmem(GX + GY + 1),
        out_specs=vmem(GX),
        scratch_shapes=[
            pltpu.VMEM((GX, MESSAGE, WIDE), BF16),
            pltpu.VMEM((2, HP, KINDS, DK, DK), BF16),
            pltpu.VMEM((GX, 4 * ROWS, WIDE), BF16),
        ],
        **params(600_000_000 * HP, 4 * MIB),
        name="finish",
    )(where, *messages, *prefixes, part)


def unpack_kernel(piece, where, *refs):
    x = where[0]
    arrived, outs, sems = refs[:GX], refs[-5:-1], refs[-1]
    copies = []
    for hop in range(GX):
        head = lax.rem(x + GX - hop, GX) * LOCAL + piece * HP
        lanes = pl.ds(pl.multiple_of(head * DK, DK), WIDE)
        for n in range(4):
            copy = pltpu.make_async_copy(
                arrived[hop].at[pl.ds(n * ROWS, ROWS), :], outs[n].at[0, :, lanes], sems.at[hop, n]
            )
            copy.start()
            copies.append(copy)
    for copy in copies:
        copy.wait()


def unpack(piece, where, arrived, outputs):
    hbm = pl.BlockSpec(memory_space=pl.ANY)
    return pl.pallas_call(
        lambda *refs: unpack_kernel(piece, *refs),
        out_shape=[shape((1, ROWS, H * DK), BF16)] * 4,
        in_specs=[smem()] + [hbm] * (GX + len(outputs)),
        out_specs=[hbm] * 4,
        scratch_shapes=[pltpu.SemaphoreType.DMA((GX, 4))],
        input_output_aliases={1 + GX + i: i for i in range(len(outputs))},
        **params(0, 2 * MIB),
        name="unpack",
    )(where, *arrived, *outputs)


def shift(array, axis, hop, count, stride=1):
    pairs = [(i, (i + hop * stride) % count) for i in range(count)]
    return lax.ppermute(array, axis, pairs)


def placed(stack, index):
    count = stack.shape[0]
    order = (index - jnp.arange(count)) % count
    return jnp.where((order[:, None] == jnp.arange(count)[None, :])[:, :, None], stack[None], 0.0).sum(1)


def ring(value, axis, count, stride=1):
    return jnp.stack([value] + [shift(value, axis, hop, count * stride, stride) for hop in range(1, count)])


def decay_table(log_decay, chosen, x, y, seqi):
    names = (chosen[:, :, None] == jnp.arange(MEMS)[None, None, :]).any(1).astype(F32)
    masks = jnp.concatenate([names, jnp.ones((ROWS, 1), F32), jnp.zeros((ROWS, 3), F32)], 1)
    sums = (log_decay[:, 0, :].astype(F32)[:, :, None] * masks[None]).sum(1)
    block = ring(sums.reshape(1, H * 8), "mem", GX).sum(0)
    block = lax.dynamic_slice_in_dim(block, x * LOCAL * 8, LOCAL * 8, 1)
    near = placed(ring(block[0], "seqo", GY), y)
    zone = near.sum(0)
    other = lax.ppermute(zone, "seqi", [(i, i ^ 1) for i in range(2 * GZ)])
    pair = jnp.where(seqi % 2 == 0, jnp.concatenate([zone, other]), jnp.concatenate([other, zone]))
    zones = placed(ring(pair, "seqi", GZ, 2), seqi // 2).reshape(2 * GZ, LOCAL * 8)
    terms = jnp.concatenate([near, zones], 0)
    a = jnp.arange(GY)
    pair = jnp.arange(GY * GY)
    i = jnp.arange(2 * GZ)
    sib = jnp.where(seqi % 2 == 0, seqi + 1, seqi - 1)
    low = jnp.concatenate(
        [a, a * 0 - 1, jnp.minimum(pair // GY, pair % GY), jnp.minimum(i, seqi) + GY, jnp.minimum(i, sib) + GY]
    )
    high = jnp.concatenate(
        [a * 0 + GY, a, jnp.maximum(pair // GY, pair % GY), jnp.maximum(i, seqi) + GY, jnp.maximum(i, sib) + GY]
    )
    place = jnp.arange(GY + 2 * GZ)[None, :]
    between = (low[:, None] < place) & (place < high[:, None])
    return jnp.exp(jnp.where(between[:, :, None], terms[None], 0.0).sum(1))


def body(queries, keys, values, log_decay, routes, route_logits, cotangent):
    scale = 2.0 / math.sqrt(DK * ROWS * GX * GY * GZ * 2)
    x, y, seqi = lax.axis_index("mem"), lax.axis_index("seqo"), lax.axis_index("seqi")
    where = jnp.stack([x, y, seqi // 2, seqi % 2]).astype(jnp.int32)
    logits = route_logits[0].astype(F32)
    margin = logits[:, 0] - logits[:, 1]
    named = routes[0].astype(F32)
    meta = jnp.concatenate(
        [
            jnp.zeros((8, ROWS), F32),
            named.T,
            jax.nn.sigmoid(margin)[None],
            jax.nn.sigmoid(-margin)[None],
            jnp.zeros((4, ROWS), F32),
        ],
        0,
    )
    messages = []
    for piece in range(PIECES):
        own = pack(piece, where, queries, keys, values, cotangent, log_decay, meta)
        if piece > 0:
            own, _ = lax.optimization_barrier((own, messages[-1]))
        messages.append([own[0]] + [shift(own[hop], "mem", hop, GX) for hop in range(1, GX)])
    table = decay_table(log_decay, routes[0], x, y, seqi)
    outputs = ()
    for piece in range(PIECES):
        sent = states(scale, where, messages[piece])
        parts = [sent[0]] + [shift(sent[hop], "seqo", hop, GY) for hop in range(1, GY)]
        own, *ahead = group(piece, where, table, parts)
        arrived = [shift(ahead[hop - 1], "seqi", hop, 2 * GZ, 2) for hop in range(1, GZ)]
        mine, sib = across(piece, where, table, own, arrived)
        sib = lax.ppermute(sib, "seqi", [(i, i ^ 1) for i in range(2 * GZ)])
        starts = entering(piece, where, table, mine, sib, parts)
        prefixes = [starts[0]] + [shift(starts[hop], "seqo", hop, GY) for hop in range(1, GY)]
        part = within(scale, where, messages[piece])
        results = finish(scale, where, messages[piece], prefixes, part)
        returned = [results[0]] + [shift(results[hop], "mem", hop, GX) for hop in range(1, GX)]
        outputs = unpack(piece, where, returned, outputs)
    return tuple(outputs)


def solution(mesh):
    tokens = P(("seqi", "seqo"), "mem", None)
    return jax.shard_map(
        body,
        mesh=mesh,
        in_specs=(tokens, tokens, tokens, P(None, ("seqi", "seqo"), "mem"), tokens, tokens, tokens),
        out_specs=(tokens,) * 4,
        check_vma=False,
    )
```

time: 792 us -> 129 us (0.16); the launches traced: 779 us -> 129 us
  other arithmetic: 235 us -> 0.97 us
  local copies, waits for them, and re-layouts: 235 us -> 6.18 us
  matrix products: 104 us -> 0 us
  blocking collectives: 65.8 us -> 0 us
  waiting for transfers between devices: 76.1 us -> 27.7 us
  Pallas kernels: 0 us -> 35.3 us
  between operations: 16.6 us -> 1.2 us
  starting transfers between devices: 45.8 us -> 57.5 us
    select_n x65 -> x4, other arithmetic: 144 us -> 0.17 us  [the longest x2 0.15 us: decay_table(): jnp.where(seqi % 2 == 0, jnp.concatenate([zone, other]), jnp.concatenate(...]
    dot_general x36 -> x0, matrix products: 104 us -> none  [the longest x2 9.29 us: local_pass(): jnp.einsum('nctd,ncde->ncte', as_blocks(reads, count, span) * jnp.exp(inn...]
    all_to_all x11 -> x0, waiting for transfers between devices: 70.7 us -> none  [the longest x1 26.1 us: body(): lax.all_to_all(packed, 'mem', split_axis=0, concat_axis=0, tiled=True)]
    unnamed x1 -> x0, blocking collectives: 65.8 us -> none
    ppermute x0 -> x42, starting transfers between devices: none -> 57.5 us  [the longest x39 57.2 us: shift(): return lax.ppermute(array, axis, pairs)]
    mul x84 -> x0, local copies, waits for them, and re-layouts: 55.6 us -> none  [the longest x62 42.5 us: combine(): later[0][:, None, None] * earlier[1] + later[1]]
    all_to_all x11 -> x0, starting transfers between devices: 45.3 us -> none  [the longest x1 5.02 us: body(): lax.all_to_all(grad_stack, 'mem', split_axis=0, concat_axis=0, tiled=True)]
    pallas_call x0 -> x16, Pallas kernels: none -> 35.3 us  [the longest x2 10.8 us: within(): pl.pallas_call(lambda *refs: within_kernel(scale, *refs), out_shape=shape...]
  transfers between devices with their start and end apart: 13 -> 42, of which waited for: 9 -> 10; matrix products, arithmetic and copies ran while one was open for 56% -> 1% of each run, Pallas kernels for 0% -> 26%
where the time goes in v1:
time: 129 us
  starting transfers between devices  57.5 us (45%)
  Pallas kernels  35.3 us (27%)
  waiting for transfers between devices  27.7 us (21%)
  local copies, waits for them, and re-layouts  6.18 us (5%)
    ppermute x39, starting transfers between devices, shift(): return lax.ppermute(array, axis, pairs)  57.2 us
    ppermute x39, waiting for transfers between devices, shift(): return lax.ppermute(array, axis, pairs)  27.7 us
    pallas_call x2, Pallas kernels, within(): pl.pallas_call(lambda *refs: within_kernel(scale, *refs), out_shape=shape...  10.8 us
    pallas_call x2, Pallas kernels, finish(): pl.pallas_call(lambda *refs: finish_kernel(scale, *refs), out_shape=[shap...  7.15 us
    unnamed x23, local copies, waits for them, and re-layouts  5.5 us
    pallas_call x2, Pallas kernels, states(): pl.pallas_call(lambda *refs: states_kernel(scale, *refs), out_shape=[shap...  3.57 us
    pallas_call x2, Pallas kernels, pack(): pl.pallas_call(lambda *refs: pack_kernel(piece, *refs), out_shape=[shape(...  3.28 us
    pallas_call x2, Pallas kernels, unpack(): pl.pallas_call(lambda *refs: unpack_kernel(piece, *refs), out_shape=[shap...  3.27 us
  transfers between devices with their start and end apart: 42, of which 10 were waited for; matrix products, arithmetic and copies ran while one was open for 1% of the time, Pallas kernels for 26%

profile of v1, /device:TPU:0, one launch (start us, length us, event | category | flops | bytes accessed | tf_op | source)
XLA Modules:
  0.0 128.8 jit_solution(6597086402732503096)
XLA Ops:
  1.7 2.9 %collective-permute-start.8 = (f32[1,128]{1,0:T(1,128)S(1)}, f32[1,128]{1,0:T(1,128)S(1)}, u32[]{:S(2)}, u32[]{:S(2)}) collective-permute-start(f32[1,128]{1,0:T(1,128)S(1)} %stack_reshape.3), channel_id=1, source_target_pairs={{0,96},{32,0},{64,32},{96,64},{1,97},{33,1},{65,33},{97,65},{2,98}... | collective-permute-start | bytes 1544 | tf_op jit(solution)/shard_map/ppermute | solution.py:474
  12.9 1.9 %collective-permute-start = (bf16[528,256]{1,0:T(8,128)(2,1)}, bf16[528,256]{1,0:T(8,128)(2,1)S(1)}, u32[]{:S(2)}, u32[]{:S(2)}) collective-permute-start(bf16[528,256]{1,0:T(8,128)(2,1)} %get-tuple-element.61), channel_id=1, source_target_pairs={{0,32},{32,64},{64,96},{96,0},{1,33},{33,65},{65,97},{97,1},{2,34}... | collective-permute-start | bytes 811016 | tf_op jit(solution)/shard_map/ppermute | solution.py:474
  14.8 2.0 %collective-permute-start.1 = (bf16[528,256]{1,0:T(8,128)(2,1)}, bf16[528,256]{1,0:T(8,128)(2,1)S(1)}, u32[]{:S(2)}, u32[]{:S(2)}) collective-permute-start(bf16[528,256]{1,0:T(8,128)(2,1)} %get-tuple-element.62), channel_id=1, source_target_pairs={{0,64},{32,96},{64,0},{96,32},{1,65},{33,97},{65,1},{97,33},{2,66}... | collective-permute-start | bytes 811016 | tf_op jit(solution)/shard_map/ppermute | solution.py:474
  17.3 3.0 %collective-permute-start.11 = (f32[32]{0:T(128)S(1)}, f32[32]{0:T(128)S(1)}, u32[]{:S(2)}, u32[]{:S(2)}) collective-permute-start(f32[32]{0:T(128)S(1)} %fusion.6), channel_id=1, source_target_pairs={{0,3},{1,0},{2,1},{3,2},{4,7},{5,4},{6,5},{7,6},{8,11},{9,8},{10,9... | collective-permute-start | bytes 392 | tf_op jit(solution)/shard_map/ppermute | solution.py:474
  22.7 2.6 %collective-permute-done.10 = f32[32]{0:T(128)S(1)} collective-permute-done((f32[32]{0:T(128)S(1)}, f32[32]{0:T(128)S(1)}, u32[]{:S(2)}, u32[]{:S(2)}) %collective-permute-start.10) | collective-permute-done | bytes 160 | tf_op jit(solution)/shard_map/ppermute | solution.py:474
  27.7 4.0 %collective-permute-start.15 = (f32[64]{0:T(128)S(1)}, f32[64]{0:T(128)S(1)}, u32[]{:S(2)}, u32[]{:S(2)}) collective-permute-start(f32[64]{0:T(128)S(1)} %broadcast_select_fusion), channel_id=1, source_target_pairs={{0,24},{4,28},{8,0},{12,4},{16,8},{20,12},{24,16},{28,20},{1,25},{... | collective-permute-start | bytes 776 | tf_op jit(solution)/shard_map/ppermute | solution.py:474
  37.2 1.9 %collective-permute-start.4 = (bf16[528,256]{1,0:T(8,128)(2,1)}, bf16[528,256]{1,0:T(8,128)(2,1)S(1)}, u32[]{:S(2)}, u32[]{:S(2)}) collective-permute-start(bf16[528,256]{1,0:T(8,128)(2,1)} %get-tuple-element.66), channel_id=1, source_target_pairs={{0,64},{32,96},{64,0},{96,32},{1,65},{33,97},{65,1},{97,33},{2,66}... | collective-permute-start | bytes 811016 | tf_op jit(solution)/shard_map/ppermute | solution.py:474
  39.1 1.9 %collective-permute-start.5 = (bf16[528,256]{1,0:T(8,128)(2,1)}, bf16[528,256]{1,0:T(8,128)(2,1)S(1)}, u32[]{:S(2)}, u32[]{:S(2)}) collective-permute-start(bf16[528,256]{1,0:T(8,128)(2,1)} %get-tuple-element.67), channel_id=1, source_target_pairs={{0,96},{32,0},{64,32},{96,64},{1,97},{33,1},{65,33},{97,65},{2,98}... | collective-permute-start | bytes 811016 | tf_op jit(solution)/shard_map/ppermute | solution.py:474
  44.0 4.1 %collective-permute-done.30.refs_4_.refs_6_ = bf16[2,2,5,32,128]{4,3,2,1,0:T(8,128)(2,1)S(1)} collective-permute-done((bf16[2,2,5,32,128]{4,3,2,1,0:T(8,128)(2,1)S(1)}, bf16[2,2,5,32,128]{4,3,2,1,0:T(8,128)(2,1)S(1)}, u32[]{:S(2)}, u32[]{:S(2)}) %collective-permute-start.30) | collective-permute-done | bytes 163872 | tf_op jit(solution)/shard_map/ppermute | solution.py:474
  50.7 2.3 %collective-permute-start.32 = (bf16[2,5,32,128]{3,2,1,0:T(8,128)(2,1)S(1)}, bf16[2,5,32,128]{3,2,1,0:T(8,128)(2,1)S(1)}, u32[]{:S(2)}, u32[]{:S(2)}) collective-permute-start(bf16[2,5,32,128]{3,2,1,0:T(8,128)(2,1)S(1)} %get-tuple-element.91), channel_id=1, source_target_pairs={{0,8},{4,12},{8,16},{12,20},{16,24},{20,28},{24,0},{28,4},{1,9},{5... | collective-permute-start | bytes 245768 | tf_op jit(solution)/shard_map/ppermute | solution.py:474
  58.9 3.1 %collective-permute-start.17 = (bf16[2,2,5,32,128]{4,3,2,1,0:T(8,128)(2,1)S(1)}, bf16[2,2,5,32,128]{4,3,2,1,0:T(8,128)(2,1)S(1)}, u32[]{:S(2)}, u32[]{:S(2)}) collective-permute-start(bf16[2,2,5,32,128]{4,3,2,1,0:T(8,128)(2,1)S(1)} %get-tuple-element.70), channel_id=1, source_target_pairs={{0,2},{1,3},{2,0},{3,1},{4,6},{5,7},{6,4},{7,5},{8,10},{9,11},{10,... | collective-permute-start | bytes 491528 | tf_op jit(solution)/shard_map/ppermute | solution.py:474
  63.3 2.8 %collective-permute-done.16.refs_3_.refs_5_ = bf16[2,2,5,32,128]{4,3,2,1,0:T(8,128)(2,1)S(1)} collective-permute-done((bf16[2,2,5,32,128]{4,3,2,1,0:T(8,128)(2,1)S(1)}, bf16[2,2,5,32,128]{4,3,2,1,0:T(8,128)(2,1)S(1)}, u32[]{:S(2)}, u32[]{:S(2)}) %collective-permute-start.16) | collective-permute-done | bytes 163872 | tf_op jit(solution)/shard_map/ppermute | solution.py:474
  74.4 3.3 %collective-permute-start.37 = (bf16[2,2,5,32,128]{4,3,2,1,0:T(8,128)(2,1)S(1)}, bf16[2,2,5,32,128]{4,3,2,1,0:T(8,128)(2,1)S(1)}, u32[]{:S(2)}, u32[]{:S(2)}) collective-permute-start(bf16[2,2,5,32,128]{4,3,2,1,0:T(8,128)(2,1)S(1)} %get-tuple-element.98), channel_id=1, source_target_pairs={{0,2},{1,3},{2,0},{3,1},{4,6},{5,7},{6,4},{7,5},{8,10},{9,11},{10,... | collective-permute-start | bytes 491528 | tf_op jit(solution)/shard_map/ppermute | solution.py:474
  79.2 5.4 %within.3.refs_9_ = bf16[4,512,256]{2,1,0:T(8,128)(2,1)S(1)} custom-call(s32[4]{0:T(128)S(1)} %pad_add_fusion.refs_0_, bf16[528,256]{1,0:T(8,128)(2,1)S(1)} %get-tuple-element.60.refs_1_, bf16[528,256]{1,0:T(8,128)(2,1)S(1)} %collective-permute-done.refs_2_, bf16[528,256]{1,0:T(8,128)(2,1)S(1)} %collective-permute-done.1.refs_3_, ...), custom_call_target="tpu_custom_call" | custom-call | flops 2000000000 | bytes 4194304 | tf_op jit(solution)/shard_map/within/pallas_call | solution.py:366
  84.7 3.6 %finish.3 = (bf16[512,256]{1,0:T(8,128)(2,1)S(1)}, bf16[512,256]{1,0:T(8,128)(2,1)S(1)}, bf16[512,256]{1,0:T(8,128)(2,1)S(1)}, bf16[512,256]{1,0:T(8,128)(2,1)S(1)}) custom-call(s32[4]{0:T(128)S(1)} %pad_add_fusion.refs_0_, bf16[528,256]{1,0:T(8,128)(2,1)S(1)} %get-tuple-element.60.refs_1_, bf16[528,256]{1,0:T(8,128)(2,1)S(1)} %collective-permute-done.refs_2_, ...), custom_call_target="tpu_custom_call" | custom-call | flops 1200000000 | bytes 4194304 | tf_op jit(solution)/shard_map/finish/pallas_call | solution.py:426
  90.1 2.0 %collective-permute-start.23 = (bf16[2,2,5,32,128]{4,3,2,1,0:T(8,128)(2,1)S(1)}, bf16[2,2,5,32,128]{4,3,2,1,0:T(8,128)(2,1)S(1)}, u32[]{:S(2)}, u32[]{:S(2)}) collective-permute-start(bf16[2,2,5,32,128]{4,3,2,1,0:T(8,128)(2,1)S(1)} %get-tuple-element.79), channel_id=1, source_target_pairs={{0,1},{1,2},{2,3},{3,0},{4,5},{5,6},{6,7},{7,4},{8,9},{9,10},{10,1... | collective-permute-start | bytes 491528 | tf_op jit(solution)/shard_map/ppermute | solution.py:474
  93.0 2.1 %collective-permute-start.25 = (bf16[2,2,5,32,128]{4,3,2,1,0:T(8,128)(2,1)S(1)}, bf16[2,2,5,32,128]{4,3,2,1,0:T(8,128)(2,1)S(1)}, u32[]{:S(2)}, u32[]{:S(2)}) collective-permute-start(bf16[2,2,5,32,128]{4,3,2,1,0:T(8,128)(2,1)S(1)} %get-tuple-element.81), channel_id=1, source_target_pairs={{0,3},{1,0},{2,1},{3,2},{4,7},{5,4},{6,5},{7,6},{8,11},{9,8},{10,9... | collective-permute-start | bytes 491528 | tf_op jit(solution)/shard_map/ppermute | solution.py:474
  95.1 5.4 %within.2.refs_9_ = bf16[4,512,256]{2,1,0:T(8,128)(2,1)S(1)} custom-call(s32[4]{0:T(128)S(1)} %pad_add_fusion.refs_0_, bf16[528,256]{1,0:T(8,128)(2,1)S(1)} %get-tuple-element.64.refs_1_, bf16[528,256]{1,0:T(8,128)(2,1)S(1)} %collective-permute-done.3.refs_2_, bf16[528,256]{1,0:T(8,128)(2,1)S(1)} %collective-permute-done.4.refs_3_, ...), custom_call_target="tpu_custom_call" | custom-call | flops 2000000000 | bytes 4194304 | tf_op jit(solution)/shard_map/within/pallas_call | solution.py:366
  100.5 2.6 %collective-permute-start.40 = (bf16[512,256]{1,0:T(8,128)(2,1)S(1)}, bf16[512,256]{1,0:T(8,128)(2,1)S(1)}, u32[]{:S(2)}, u32[]{:S(2)}) collective-permute-start(bf16[512,256]{1,0:T(8,128)(2,1)S(1)} %get-tuple-element.102), channel_id=1, source_target_pairs={{0,64},{32,96},{64,0},{96,32},{1,65},{33,97},{65,1},{97,33},{2,66}... | collective-permute-start | bytes 786440 | tf_op jit(solution)/shard_map/ppermute | solution.py:474
  104.9 3.6 %finish.2 = (bf16[512,256]{1,0:T(8,128)(2,1)S(1)}, bf16[512,256]{1,0:T(8,128)(2,1)S(1)}, bf16[512,256]{1,0:T(8,128)(2,1)S(1)}, bf16[512,256]{1,0:T(8,128)(2,1)S(1)}) custom-call(s32[4]{0:T(128)S(1)} %pad_add_fusion.refs_0_, bf16[528,256]{1,0:T(8,128)(2,1)S(1)} %get-tuple-element.64.refs_1_, bf16[528,256]{1,0:T(8,128)(2,1)S(1)} %collective-permute-done.3.refs_2_, ...), custom_call_target="tpu_custom_call" | custom-call | flops 1200000000 | bytes 4194304 | tf_op jit(solution)/shard_map/finish/pallas_call | solution.py:426
  110.2 2.5 %collective-permute-start.28 = (bf16[512,256]{1,0:T(8,128)(2,1)S(1)}, bf16[512,256]{1,0:T(8,128)(2,1)S(1)}, u32[]{:S(2)}, u32[]{:S(2)}) collective-permute-start(bf16[512,256]{1,0:T(8,128)(2,1)S(1)} %get-tuple-element.85), channel_id=1, source_target_pairs={{0,96},{32,0},{64,32},{96,64},{1,97},{33,1},{65,33},{97,65},{2,98}... | collective-permute-start | bytes 786440 | tf_op jit(solution)/shard_map/ppermute | solution.py:474
  112.8 4.5 %collective-permute-done.41.refs_4_ = bf16[512,256]{1,0:T(8,128)(2,1)S(1)} collective-permute-done((bf16[512,256]{1,0:T(8,128)(2,1)S(1)}, bf16[512,256]{1,0:T(8,128)(2,1)S(1)}, u32[]{:S(2)}, u32[]{:S(2)}) %collective-permute-start.41) | collective-permute-done | bytes 262176 | tf_op jit(solution)/shard_map/ppermute | solution.py:474
  118.9 3.6 %collective-permute-done.26.refs_2_ = bf16[512,256]{1,0:T(8,128)(2,1)S(1)} collective-permute-done((bf16[512,256]{1,0:T(8,128)(2,1)S(1)}, bf16[512,256]{1,0:T(8,128)(2,1)S(1)}, u32[]{:S(2)}, u32[]{:S(2)}) %collective-permute-start.26) | collective-permute-done | bytes 262176 | tf_op jit(solution)/shard_map/ppermute | solution.py:474
  122.5 4.5 %collective-permute-done.28.refs_4_ = bf16[512,256]{1,0:T(8,128)(2,1)S(1)} collective-permute-done((bf16[512,256]{1,0:T(8,128)(2,1)S(1)}, bf16[512,256]{1,0:T(8,128)(2,1)S(1)}, u32[]{:S(2)}, u32[]{:S(2)}) %collective-permute-start.28) | collective-permute-done | bytes 262176 | tf_op jit(solution)/shard_map/ppermute | solution.py:474
  (144 shorter events, 51.9 us)
Async XLA Ops:
  1.7 15.5 %collective-permute-start.8 = (f32[1,128]{1,0:T(1,128)S(1)}, f32[1,128]{1,0:T(1,128)S(1)}, u32[]{:S(2)}, u32[]{:S(2)}) collective-permute-start(f32[1,128]{1,0:T(1,128)S(1)} %stack_reshape.3), channel_id=1, source_target_pairs={{0,96},{32,0},{64,32},{96,64},{1,97},{33,1},{65,33},{97,65},{2,98}... | collective-permute-start | bytes 1544 | tf_op jit(solution)/shard_map/ppermute | solution.py:474
  4.6 12.6 %collective-permute-start.7 = (f32[1,128]{1,0:T(1,128)S(1)}, f32[1,128]{1,0:T(1,128)S(1)}, u32[]{:S(2)}, u32[]{:S(2)}) collective-permute-start(f32[1,128]{1,0:T(1,128)S(1)} %stack_reshape.3), channel_id=1, source_target_pairs={{0,64},{32,96},{64,0},{96,32},{1,65},{33,97},{65,1},{97,33},{2,66}... | collective-permute-start | bytes 1544 | tf_op jit(solution)/shard_map/ppermute | solution.py:474
  5.4 11.8 %collective-permute-start.6 = (f32[1,128]{1,0:T(1,128)S(1)}, f32[1,128]{1,0:T(1,128)S(1)}, u32[]{:S(2)}, u32[]{:S(2)}) collective-permute-start(f32[1,128]{1,0:T(1,128)S(1)} %stack_reshape.3), channel_id=1, source_target_pairs={{0,32},{32,64},{64,96},{96,0},{1,33},{33,65},{65,97},{97,1},{2,34}... | collective-permute-start | bytes 1544 | tf_op jit(solution)/shard_map/ppermute | solution.py:474
  12.9 18.9 %collective-permute-start = (bf16[528,256]{1,0:T(8,128)(2,1)}, bf16[528,256]{1,0:T(8,128)(2,1)S(1)}, u32[]{:S(2)}, u32[]{:S(2)}) collective-permute-start(bf16[528,256]{1,0:T(8,128)(2,1)} %get-tuple-element.61), channel_id=1, source_target_pairs={{0,32},{32,64},{64,96},{96,0},{1,33},{33,65},{65,97},{97,1},{2,34}... | collective-permute-start | bytes 811016 | tf_op jit(solution)/shard_map/ppermute | solution.py:474
  14.8 18.3 %collective-permute-start.1 = (bf16[528,256]{1,0:T(8,128)(2,1)}, bf16[528,256]{1,0:T(8,128)(2,1)S(1)}, u32[]{:S(2)}, u32[]{:S(2)}) collective-permute-start(bf16[528,256]{1,0:T(8,128)(2,1)} %get-tuple-element.62), channel_id=1, source_target_pairs={{0,64},{32,96},{64,0},{96,32},{1,65},{33,97},{65,1},{97,33},{2,66}... | collective-permute-start | bytes 811016 | tf_op jit(solution)/shard_map/ppermute | solution.py:474
  22.0 11.1 %collective-permute-start.2 = (bf16[528,256]{1,0:T(8,128)(2,1)}, bf16[528,256]{1,0:T(8,128)(2,1)S(1)}, u32[]{:S(2)}, u32[]{:S(2)}) collective-permute-start(bf16[528,256]{1,0:T(8,128)(2,1)} %get-tuple-element.63), channel_id=1, source_target_pairs={{0,96},{32,0},{64,32},{96,64},{1,97},{33,1},{65,33},{97,65},{2,98}... | collective-permute-start | bytes 811016 | tf_op jit(solution)/shard_map/ppermute | solution.py:474
  36.8 17.7 %collective-permute-start.3 = (bf16[528,256]{1,0:T(8,128)(2,1)}, bf16[528,256]{1,0:T(8,128)(2,1)S(1)}, u32[]{:S(2)}, u32[]{:S(2)}) collective-permute-start(bf16[528,256]{1,0:T(8,128)(2,1)} %get-tuple-element.65), channel_id=1, source_target_pairs={{0,32},{32,64},{64,96},{96,0},{1,33},{33,65},{65,97},{97,1},{2,34}... | collective-permute-start | bytes 811016 | tf_op jit(solution)/shard_map/ppermute | solution.py:474
  37.2 18.8 %collective-permute-start.4 = (bf16[528,256]{1,0:T(8,128)(2,1)}, bf16[528,256]{1,0:T(8,128)(2,1)S(1)}, u32[]{:S(2)}, u32[]{:S(2)}) collective-permute-start(bf16[528,256]{1,0:T(8,128)(2,1)} %get-tuple-element.66), channel_id=1, source_target_pairs={{0,64},{32,96},{64,0},{96,32},{1,65},{33,97},{65,1},{97,33},{2,66}... | collective-permute-start | bytes 811016 | tf_op jit(solution)/shard_map/ppermute | solution.py:474
  39.1 16.9 %collective-permute-start.5 = (bf16[528,256]{1,0:T(8,128)(2,1)}, bf16[528,256]{1,0:T(8,128)(2,1)S(1)}, u32[]{:S(2)}, u32[]{:S(2)}) collective-permute-start(bf16[528,256]{1,0:T(8,128)(2,1)} %get-tuple-element.67), channel_id=1, source_target_pairs={{0,96},{32,0},{64,32},{96,64},{1,97},{33,1},{65,33},{97,65},{2,98}... | collective-permute-start | bytes 811016 | tf_op jit(solution)/shard_map/ppermute | solution.py:474
  50.7 11.3 %collective-permute-start.32 = (bf16[2,5,32,128]{3,2,1,0:T(8,128)(2,1)S(1)}, bf16[2,5,32,128]{3,2,1,0:T(8,128)(2,1)S(1)}, u32[]{:S(2)}, u32[]{:S(2)}) collective-permute-start(bf16[2,5,32,128]{3,2,1,0:T(8,128)(2,1)S(1)} %get-tuple-element.91), channel_id=1, source_target_pairs={{0,8},{4,12},{8,16},{12,20},{16,24},{20,28},{24,0},{28,4},{1,9},{5... | collective-permute-start | bytes 245768 | tf_op jit(solution)/shard_map/ppermute | solution.py:474
  53.0 9.2 %collective-permute-start.33 = (bf16[2,5,32,128]{3,2,1,0:T(8,128)(2,1)S(1)}, bf16[2,5,32,128]{3,2,1,0:T(8,128)(2,1)S(1)}, u32[]{:S(2)}, u32[]{:S(2)}) collective-permute-start(bf16[2,5,32,128]{3,2,1,0:T(8,128)(2,1)S(1)} %get-tuple-element.92), channel_id=1, source_target_pairs={{0,16},{4,20},{8,24},{12,28},{16,0},{20,4},{24,8},{28,12},{1,17},{... | collective-permute-start | bytes 245768 | tf_op jit(solution)/shard_map/ppermute | solution.py:474
  63.2 9.2 %collective-permute-start.35 = (bf16[2,2,5,32,128]{4,3,2,1,0:T(8,128)(2,1)S(1)}, bf16[2,2,5,32,128]{4,3,2,1,0:T(8,128)(2,1)S(1)}, u32[]{:S(2)}, u32[]{:S(2)}) collective-permute-start(bf16[2,2,5,32,128]{4,3,2,1,0:T(8,128)(2,1)S(1)} %get-tuple-element.95), channel_id=1, source_target_pairs={{0,4},{4,0},{8,12},{12,8},{16,20},{20,16},{24,28},{28,24},{1,5},{5... | collective-permute-start | bytes 491528 | tf_op jit(solution)/shard_map/ppermute | solution.py:545
  73.9 10.8 %collective-permute-start.36 = (bf16[2,2,5,32,128]{4,3,2,1,0:T(8,128)(2,1)S(1)}, bf16[2,2,5,32,128]{4,3,2,1,0:T(8,128)(2,1)S(1)}, u32[]{:S(2)}, u32[]{:S(2)}) collective-permute-start(bf16[2,2,5,32,128]{4,3,2,1,0:T(8,128)(2,1)S(1)} %get-tuple-element.97), channel_id=1, source_target_pairs={{0,1},{1,2},{2,3},{3,0},{4,5},{5,6},{6,7},{7,4},{8,9},{9,10},{10,1... | collective-permute-start | bytes 491528 | tf_op jit(solution)/shard_map/ppermute | solution.py:474
  74.4 10.2 %collective-permute-start.37 = (bf16[2,2,5,32,128]{4,3,2,1,0:T(8,128)(2,1)S(1)}, bf16[2,2,5,32,128]{4,3,2,1,0:T(8,128)(2,1)S(1)}, u32[]{:S(2)}, u32[]{:S(2)}) collective-permute-start(bf16[2,2,5,32,128]{4,3,2,1,0:T(8,128)(2,1)S(1)} %get-tuple-element.98), channel_id=1, source_target_pairs={{0,2},{1,3},{2,0},{3,1},{4,6},{5,7},{6,4},{7,5},{8,10},{9,11},{10,... | collective-permute-start | bytes 491528 | tf_op jit(solution)/shard_map/ppermute | solution.py:474
  79.1 9.5 %collective-permute-start.22 = (bf16[2,2,5,32,128]{4,3,2,1,0:T(8,128)(2,1)S(1)}, bf16[2,2,5,32,128]{4,3,2,1,0:T(8,128)(2,1)S(1)}, u32[]{:S(2)}, u32[]{:S(2)}) collective-permute-start(bf16[2,2,5,32,128]{4,3,2,1,0:T(8,128)(2,1)S(1)} %get-tuple-element.77), channel_id=1, source_target_pairs={{0,4},{4,0},{8,12},{12,8},{16,20},{20,16},{24,28},{28,24},{1,5},{5... | collective-permute-start | bytes 491528 | tf_op jit(solution)/shard_map/ppermute | solution.py:545
  88.3 22.0 %collective-permute-start.39 = (bf16[512,256]{1,0:T(8,128)(2,1)S(1)}, bf16[512,256]{1,0:T(8,128)(2,1)S(1)}, u32[]{:S(2)}, u32[]{:S(2)}) collective-permute-start(bf16[512,256]{1,0:T(8,128)(2,1)S(1)} %get-tuple-element.101), channel_id=1, source_target_pairs={{0,32},{32,64},{64,96},{96,0},{1,33},{33,65},{65,97},{97,1},{2,34}... | collective-permute-start | bytes 786440 | tf_op jit(solution)/shard_map/ppermute | solution.py:474
  90.1 13.1 %collective-permute-start.23 = (bf16[2,2,5,32,128]{4,3,2,1,0:T(8,128)(2,1)S(1)}, bf16[2,2,5,32,128]{4,3,2,1,0:T(8,128)(2,1)S(1)}, u32[]{:S(2)}, u32[]{:S(2)}) collective-permute-start(bf16[2,2,5,32,128]{4,3,2,1,0:T(8,128)(2,1)S(1)} %get-tuple-element.79), channel_id=1, source_target_pairs={{0,1},{1,2},{2,3},{3,0},{4,5},{5,6},{6,7},{7,4},{8,9},{9,10},{10,1... | collective-permute-start | bytes 491528 | tf_op jit(solution)/shard_map/ppermute | solution.py:474
  92.1 12.8 %collective-permute-start.24 = (bf16[2,2,5,32,128]{4,3,2,1,0:T(8,128)(2,1)S(1)}, bf16[2,2,5,32,128]{4,3,2,1,0:T(8,128)(2,1)S(1)}, u32[]{:S(2)}, u32[]{:S(2)}) collective-permute-start(bf16[2,2,5,32,128]{4,3,2,1,0:T(8,128)(2,1)S(1)} %get-tuple-element.80), channel_id=1, source_target_pairs={{0,2},{1,3},{2,0},{3,1},{4,6},{5,7},{6,4},{7,5},{8,10},{9,11},{10,... | collective-permute-start | bytes 491528 | tf_op jit(solution)/shard_map/ppermute | solution.py:474
  93.0 11.9 %collective-permute-start.25 = (bf16[2,2,5,32,128]{4,3,2,1,0:T(8,128)(2,1)S(1)}, bf16[2,2,5,32,128]{4,3,2,1,0:T(8,128)(2,1)S(1)}, u32[]{:S(2)}, u32[]{:S(2)}) collective-permute-start(bf16[2,2,5,32,128]{4,3,2,1,0:T(8,128)(2,1)S(1)} %get-tuple-element.81), channel_id=1, source_target_pairs={{0,3},{1,0},{2,1},{3,2},{4,7},{5,4},{6,5},{7,6},{8,11},{9,8},{10,9... | collective-permute-start | bytes 491528 | tf_op jit(solution)/shard_map/ppermute | solution.py:474
  100.5 12.2 %collective-permute-start.40 = (bf16[512,256]{1,0:T(8,128)(2,1)S(1)}, bf16[512,256]{1,0:T(8,128)(2,1)S(1)}, u32[]{:S(2)}, u32[]{:S(2)}) collective-permute-start(bf16[512,256]{1,0:T(8,128)(2,1)S(1)} %get-tuple-element.102), channel_id=1, source_target_pairs={{0,64},{32,96},{64,0},{96,32},{1,65},{33,97},{65,1},{97,33},{2,66}... | collective-permute-start | bytes 786440 | tf_op jit(solution)/shard_map/ppermute | solution.py:474
  103.2 14.1 %collective-permute-start.41 = (bf16[512,256]{1,0:T(8,128)(2,1)S(1)}, bf16[512,256]{1,0:T(8,128)(2,1)S(1)}, u32[]{:S(2)}, u32[]{:S(2)}) collective-permute-start(bf16[512,256]{1,0:T(8,128)(2,1)S(1)} %get-tuple-element.103), channel_id=1, source_target_pairs={{0,96},{32,0},{64,32},{96,64},{1,97},{33,1},{65,33},{97,65},{2,98}... | collective-permute-start | bytes 786440 | tf_op jit(solution)/shard_map/ppermute | solution.py:474
  108.5 14.1 %collective-permute-start.26 = (bf16[512,256]{1,0:T(8,128)(2,1)S(1)}, bf16[512,256]{1,0:T(8,128)(2,1)S(1)}, u32[]{:S(2)}, u32[]{:S(2)}) collective-permute-start(bf16[512,256]{1,0:T(8,128)(2,1)S(1)} %get-tuple-element.83), channel_id=1, source_target_pairs={{0,32},{32,64},{64,96},{96,0},{1,33},{33,65},{65,97},{97,1},{2,34}... | collective-permute-start | bytes 786440 | tf_op jit(solution)/shard_map/ppermute | solution.py:474
  108.9 13.6 %collective-permute-start.27 = (bf16[512,256]{1,0:T(8,128)(2,1)S(1)}, bf16[512,256]{1,0:T(8,128)(2,1)S(1)}, u32[]{:S(2)}, u32[]{:S(2)}) collective-permute-start(bf16[512,256]{1,0:T(8,128)(2,1)S(1)} %get-tuple-element.84), channel_id=1, source_target_pairs={{0,64},{32,96},{64,0},{96,32},{1,65},{33,97},{65,1},{97,33},{2,66}... | collective-permute-start | bytes 786440 | tf_op jit(solution)/shard_map/ppermute | solution.py:474
  110.2 16.8 %collective-permute-start.28 = (bf16[512,256]{1,0:T(8,128)(2,1)S(1)}, bf16[512,256]{1,0:T(8,128)(2,1)S(1)}, u32[]{:S(2)}, u32[]{:S(2)}) collective-permute-start(bf16[512,256]{1,0:T(8,128)(2,1)S(1)} %get-tuple-element.85), channel_id=1, source_target_pairs={{0,96},{32,0},{64,32},{96,64},{1,97},{33,1},{65,33},{97,65},{2,98}... | collective-permute-start | bytes 786440 | tf_op jit(solution)/shard_map/ppermute | solution.py:474
  (29 other events, 181.8 us)

commit v2 on v0

v2 whole, which is shorter than its diff:
```python
import math

import jax
import jax.numpy as jnp
from jax import lax
from jax.experimental import pallas as pl
from jax.experimental.pallas import tpu as pltpu
from jax.sharding import PartitionSpec as P

H = 16
DK = 128
ROWS = 128
MEMS = 4
KINDS = MEMS + 1
GX = 4
GY = 4
GZ = 4
CHUNKS = GX * GY
GROUP = 4
MESSAGE = 4 * ROWS + 16
DEEP = KINDS * DK
STATE = DEEP + 16
ZONES = 2 * GZ
OTHERS = ZONES - 1
BIG = 1e30
F32 = jnp.float32
BF16 = jnp.bfloat16
MIB = 1 << 20

NT = (((1,), (1,)), ((), ()))
TN = (((0,), (0,)), ((), ()))
NN = (((1,), (0,)), ((), ()))


def mm(a, b, dims=NN):
    return lax.dot_general(a, b, dims, preferred_element_type=F32)


VMEM = pl.BlockSpec(memory_space=pltpu.VMEM)
SMEM = pl.BlockSpec(memory_space=pltpu.SMEM)
HBM = pl.BlockSpec(memory_space=pltpu.HBM)


def params(flops, moved, grant=40 * MIB):
    return dict(
        compiler_params=pltpu.CompilerParams(vmem_limit_bytes=grant),
        cost_estimate=pl.CostEstimate(flops=flops, bytes_accessed=moved, transcendentals=0),
    )


def shape(dims, dtype):
    return jax.ShapeDtypeStruct(dims, dtype)


def pack_kernel(q, k, v, dy, gates, named, logits, out, held, stage, in_sems, out_sems):
    loads = [pltpu.make_async_copy(ref.at[0], held.at[n], in_sems.at[n]) for n, ref in enumerate((q, k, v, dy))]
    for load in loads:
        load.start()
    row = lax.broadcasted_iota(jnp.int32, (16, DK), 0)
    kinds = named[...].astype(F32)
    scores = logits[...].astype(F32)
    margin = scores[0:1] - scores[1:2]
    meta = jnp.zeros((16, DK), F32)
    for place, value in (
        (8, kinds[0:1]),
        (9, kinds[1:2]),
        (10, jax.nn.sigmoid(margin)),
        (11, jax.nn.sigmoid(-margin)),
    ):
        meta = jnp.where(row == place, value, meta)
    rates = gates[...].astype(F32)
    for h in range(H):
        stage[h, 4 * ROWS : MESSAGE, :] = jnp.where(row == 0, rates[h : h + 1], meta).astype(BF16)
    stores = []
    for n, load in enumerate(loads):
        load.wait()
        for h in range(H):
            stage[h, n * ROWS : (n + 1) * ROWS, :] = held[n, :, h * DK : (h + 1) * DK]
        last = ROWS + 16 if n == 3 else ROWS
        part = pl.ds(n * ROWS, last)
        store = pltpu.make_async_copy(stage.at[:, part, :], out.at[:, part, :], out_sems.at[n])
        store.start()
        stores.append(store)
    for store in stores:
        store.wait()


def pack(q, k, v, dy, gates, named, logits):
    return pl.pallas_call(
        pack_kernel,
        out_shape=shape((CHUNKS, MESSAGE, DK), BF16),
        in_specs=[HBM] * 4 + [VMEM] * 3,
        out_specs=HBM,
        scratch_shapes=[
            pltpu.VMEM((4, ROWS, H * DK), BF16),
            pltpu.VMEM((CHUNKS, MESSAGE, DK), BF16),
            pltpu.SemaphoreType.DMA((4,)),
            pltpu.SemaphoreType.DMA((4,)),
        ],
        **params(0, 4 * MIB, 60 * MIB),
        name="pack",
    )(q, k, v, dy, gates, named, logits)


def token_rows(buf):
    mask_rows, weight_rows, gate_rows = [], [], []
    row = lax.broadcasted_iota(jnp.int32, (8, DK), 0)
    kind = row.astype(F32)
    shared = (row == MEMS).astype(F32)
    for j in range(CHUNKS):
        small = buf[j, 4 * ROWS : MESSAGE, :].astype(F32)
        hit_first = jnp.where(row < MEMS, (kind == small[8:9]).astype(F32), 0.0)
        hit_second = jnp.where(row < MEMS, (kind == small[9:10]).astype(F32), 0.0)
        mask = hit_first + hit_second + shared
        mask_rows.append(mask)
        weight_rows.append(hit_first * small[10:11] + hit_second * small[11:12] + shared)
        gate_rows.append(mask * small[0:1])
    mask, weight, gate = (jnp.concatenate(r, 0) for r in (mask_rows, weight_rows, gate_rows))
    t = lax.broadcasted_iota(jnp.int32, (DK, DK), 0)
    s = lax.broadcasted_iota(jnp.int32, (DK, DK), 1)
    gate = gate.astype(BF16)
    running = mm(gate, (t <= s).astype(BF16))
    total = mm(gate, jnp.ones((DK, DK), BF16))
    return mask, weight, running, total


def piled(total):
    parts = [total[8 * j : 8 * j + 8] for j in range(CHUNKS)]
    before, after = [jnp.zeros((8, DK), F32)], [parts[-1]]
    for j in range(CHUNKS - 1):
        before.append(before[-1] + parts[j])
        after.append(after[-1] + parts[CHUNKS - 2 - j])
    return jnp.concatenate(before, 0), jnp.concatenate(after[::-1], 0)


def row_block(rows, r):
    few = jnp.broadcast_to(rows[r : r + 1], (16, DK)).astype(BF16)
    return jnp.concatenate([few] * (DK // 16), 0)


def col_block(cols, r):
    return jnp.broadcast_to(cols[:, r : r + 1], (DK, DK)).astype(BF16)


def tokens(buf, j):
    return (buf[j, n * ROWS : (n + 1) * ROWS, :] for n in range(4))


def states_kernel(scale, where, buf, *refs):
    outs, wide = refs[:OTHERS], refs[OTHERS]
    mask, weight, running, total = token_rows(buf)
    before, after = piled(total)
    write_rows = mask * jnp.exp(after - running)
    read_rows = weight * scale * jnp.exp(before + running)
    both = []
    for side, (left, right, rows) in enumerate(((1, 2, write_rows), (0, 3, read_rows))):
        for j in range(CHUNKS):
            turned = buf[j, left * ROWS : (left + 1) * ROWS, :].T
            for e in range(KINDS):
                wide[side, e * DK : (e + 1) * DK, j * DK : (j + 1) * DK] = turned * row_block(rows, j * 8 + e)
        facing = jnp.concatenate([buf[j, right * ROWS : (right + 1) * ROWS, :] for j in range(CHUNKS)], 0)
        sums = mm(wide[side], facing)
        both.append(sums.astype(BF16))
    coarse = after[0:8].astype(BF16).astype(F32)
    length = jnp.concatenate([coarse, after[0:8] - coarse], 0).astype(BF16)
    for hop, out in enumerate(outs, 1):
        later = where[0] + hop < 2 * GZ
        out[DEEP:STATE, :] = length

        @pl.when(later)
        def _():
            out[0:DEEP, :] = both[0]

        @pl.when(jnp.logical_not(later))
        def _():
            out[0:DEEP, :] = both[1]


def states(scale, where, messages):
    return pl.pallas_call(
        lambda *refs: states_kernel(scale, *refs),
        out_shape=[shape((STATE, DK), BF16)] * OTHERS,
        in_specs=[SMEM, VMEM],
        out_specs=[VMEM] * OTHERS,
        scratch_shapes=[pltpu.VMEM((2, DEEP, CHUNKS * DK), BF16)],
        **params(700_000_000, 4 * MIB),
        name="states",
    )(where, messages)


def within_kernel(scale, buf, res, state):
    mask, weight, running, total = token_rows(buf)
    t = lax.broadcasted_iota(jnp.int32, (DK, DK), 0)
    s = lax.broadcasted_iota(jnp.int32, (DK, DK), 1)
    lower = t >= s
    decay = jnp.exp(total)
    write_row = mask * jnp.exp(total - running)
    read_row = weight * scale * jnp.exp(running)
    barred = jnp.where(mask > 0, running, BIG)
    running_col = running.T
    weight_col = (weight * scale).T
    read_col = read_row.T
    write_col = write_row.T
    for j in range(CHUNKS):
        q, k, v, dy = tokens(buf, j)
        near = jnp.zeros((DK, DK), F32)
        for r in range(j * 8, j * 8 + KINDS):
            near = near + weight_col[:, r : r + 1] * jnp.exp(running_col[:, r : r + 1] - barred[r : r + 1])
        near = jnp.where(lower, near, 0.0)
        scores = (mm(q, k, NT) * near).astype(BF16)
        grads = (mm(dy, v, NT) * near).astype(BF16)
        res[j, 0] = mm(scores, v)
        res[j, 1] = mm(grads, k)
        res[j, 2] = mm(grads, q, TN)
        res[j, 3] = mm(scores, dy, TN)

    def step(side, j, start, last, cols, rows, places):
        left, right, cross = places
        blocks = list(tokens(buf, j))
        a, b = blocks[left], blocks[right]
        if not start:
            spread = [col_block(cols, j * 8 + e) for e in range(KINDS)]
            half = state[side].astype(BF16)
            res[j, 2 if side else 0] += sum(
                [mm((b if side else a) * spread[e], half[e * DK : (e + 1) * DK], NT if side else NN) for e in range(KINDS)]
            )
            res[j, 3 if side else 1] += sum(
                [mm((a if side else b) * spread[e], half[e * DK : (e + 1) * DK], NN if side else NT) for e in range(KINDS)]
            )
        if not last:
            grow, face = blocks[cross[0]].T, blocks[cross[1]]
            for e in range(KINDS):
                part = slice(e * DK, (e + 1) * DK)
                grown = mm(grow * row_block(rows, j * 8 + e), face)
                if not start:
                    grown = grown + decay[j * 8 + e : j * 8 + e + 1] * state[side, part, :]
                state[side, part, :] = grown

    for i in range(CHUNKS):
        step(0, i, i == 0, i == CHUNKS - 1, read_col, write_row, (0, 3, (1, 2)))
        back = CHUNKS - 1 - i
        step(1, back, i == 0, i == CHUNKS - 1, write_col, read_row, (1, 2, (0, 3)))


def within(scale, messages):
    return pl.pallas_call(
        lambda *refs: within_kernel(scale, *refs),
        out_shape=shape((CHUNKS, 4, ROWS, DK), F32),
        in_specs=[VMEM],
        out_specs=VMEM,
        scratch_shapes=[pltpu.VMEM((2, DEEP, DK), F32)],
        **params(2_000_000_000, 6 * MIB),
        name="within",
    )(messages)


def entering(mine, total, arrived, lengths):
    lengths[mine] = total
    sources = [lax.rem(mine + ZONES - hop, ZONES) for hop in range(1, ZONES)]
    for source, ref in zip(sources, arrived):
        tail = ref[DEEP:STATE, :].astype(F32)
        lengths[source] = tail[0:8] + tail[8:16]
    start = [jnp.zeros((DEEP, DK), F32), jnp.zeros((DEEP, DK), F32)]
    for source, ref in zip(sources, arrived):
        low, high = jnp.minimum(source, mine), jnp.maximum(source, mine)
        gap = jnp.zeros((8, DK), F32)
        for zone in range(ZONES):
            inside = jnp.logical_and(low < zone, zone < high).astype(F32)
            gap = gap + inside * lengths[zone]
        factor = jnp.exp(gap)
        earlier = (source < mine).astype(F32)
        block = ref[0:DEEP, :].astype(F32).reshape(KINDS, DK, DK) * factor[0:KINDS].reshape(KINDS, 1, DK)
        block = block.reshape(DEEP, DK)
        start[0] = start[0] + earlier * block
        start[1] = start[1] + (1.0 - earlier) * block
    return [side.astype(BF16) for side in start]


def turned(state):
    return jnp.concatenate([state[e * DK : (e + 1) * DK].T for e in range(KINDS)], 0)


def finish_kernel(scale, where, buf, part, *refs):
    arrived, out, lengths = refs[:OTHERS], refs[OTHERS], refs[OTHERS + 1]
    mask, weight, running, total = token_rows(buf)
    before, after = piled(total)
    read_col = (weight * scale * jnp.exp(before + running)).T
    write_col = (mask * jnp.exp(after - running)).T
    state = entering(where[0], after[0:8], arrived, lengths)
    flipped = [turned(s) for s in state]
    for first in range(0, CHUNKS, GROUP):
        group = range(first, first + GROUP)
        blocks = [list(tokens(buf, j)) for j in group]
        for cols, jobs in (
            (read_col, ((0, state[0]), (3, flipped[0]))),
            (write_col, ((1, state[1]), (2, flipped[1]))),
        ):
            spread = [[col_block(cols, j * 8 + e) for e in range(KINDS)] for j in group]
            for source, right in jobs:
                left = jnp.concatenate(
                    [jnp.concatenate([blocks[i][source] * w for w in spread[i]], 1) for i in range(GROUP)], 0
                )
                sums = mm(left, right)
                n = (0, 3, 2, 1)[source]
                for i, j in enumerate(group):
                    out[j, n * ROWS : (n + 1) * ROWS, :] = (
                        part[j, n] + sums[i * ROWS : (i + 1) * ROWS]
                    ).astype(BF16)


def finish(scale, where, messages, part, arrived):
    return pl.pallas_call(
        lambda *refs: finish_kernel(scale, *refs),
        out_shape=shape((CHUNKS, 4 * ROWS, DK), BF16),
        in_specs=[SMEM] + [VMEM] * (2 + OTHERS),
        out_specs=VMEM,
        scratch_shapes=[pltpu.VMEM((ZONES, 8, DK), F32)],
        **params(1_300_000_000, 8 * MIB),
        name="finish",
    )(where, messages, part, *arrived)


def unpack_kernel(arrived, *refs):
    outs, stage, sems = refs[:4], refs[4], refs[5]
    stores = []
    for n, out in enumerate(outs):
        for h in range(H):
            stage[n, :, h * DK : (h + 1) * DK] = arrived[h, n * ROWS : (n + 1) * ROWS, :]
        store = pltpu.make_async_copy(stage.at[n], out.at[0], sems.at[n])
        store.start()
        stores.append(store)
    for store in stores:
        store.wait()


def unpack(arrived):
    return pl.pallas_call(
        unpack_kernel,
        out_shape=[shape((1, ROWS, H * DK), BF16)] * 4,
        in_specs=[VMEM],
        out_specs=[HBM] * 4,
        scratch_shapes=[pltpu.VMEM((4, ROWS, H * DK), BF16), pltpu.SemaphoreType.DMA((4,))],
        **params(0, 4 * MIB),
        name="unpack",
    )(arrived)


def body(queries, keys, values, log_decay, routes, route_logits, cotangent):
    scale = 2.0 / math.sqrt(DK * ROWS * GX * GY * ZONES)
    where = lax.axis_index("seqi").astype(jnp.int32).reshape(1)
    packed = pack(queries, keys, values, cotangent, log_decay[:, 0, :], routes[0].T, route_logits[0].T)
    messages = lax.all_to_all(packed, ("seqo", "mem"), 0, 0, tiled=True)
    sent = states(scale, where, messages)
    arrived = [
        lax.ppermute(block, "seqi", [(i, (i + hop) % ZONES) for i in range(ZONES)])
        for hop, block in enumerate(sent, 1)
    ]
    part = within(scale, messages)
    results = finish(scale, where, messages, part, arrived)
    returned = lax.all_to_all(results, ("seqo", "mem"), 0, 0, tiled=True)
    return tuple(unpack(returned))


def solution(mesh):
    tokens_spec = P(("seqi", "seqo"), "mem", None)
    return jax.shard_map(
        body,
        mesh=mesh,
        in_specs=(tokens_spec,) * 3 + (P(None, ("seqi", "seqo"), "mem"),) + (tokens_spec,) * 3,
        out_specs=(tokens_spec,) * 4,
        check_vma=False,
    )
```

time: 792 us -> 106 us (0.13); the launches traced: 779 us -> 105 us
  other arithmetic: 235 us -> 0 us
  local copies, waits for them, and re-layouts: 235 us -> 0 us
  matrix products: 104 us -> 0 us
  waiting for transfers between devices: 76.1 us -> 32.6 us
  blocking collectives: 65.8 us -> 29.2 us
  starting transfers between devices: 45.8 us -> 20.5 us
  Pallas kernels: 0 us -> 22.2 us
  between operations: 16.6 us -> 0.89 us
    select_n x65 -> x0, other arithmetic: 144 us -> none  [the longest x62 144 us: hop(): jnp.where(position < mine, new, old)]
    dot_general x36 -> x0, matrix products: 104 us -> none  [the longest x2 9.29 us: local_pass(): jnp.einsum('nctd,ncde->ncte', as_blocks(reads, count, span) * jnp.exp(inn...]
    unnamed x1 -> x0, blocking collectives: 65.8 us -> none
    mul x84 -> x0, local copies, waits for them, and re-layouts: 55.6 us -> none  [the longest x62 42.5 us: combine(): later[0][:, None, None] * earlier[1] + later[1]]
    all_to_all x11 -> x1, starting transfers between devices: 45.3 us -> 7.13 us  [body(): messages = lax.all_to_all(packed, ('seqo', 'mem'), 0, 0, tiled=True)]
    all_to_all x11 -> x1, waiting for transfers between devices: 70.7 us -> 32.6 us  [body(): messages = lax.all_to_all(packed, ('seqo', 'mem'), 0, 0, tiled=True)]
    gather x5 -> x0, local copies, waits for them, and re-layouts: 32.8 us -> none  [the longest x1 13.3 us: body(): packed = stacked[slot_table].reshape(groups, MEM_DEV, CAP, 3, features)]
    another operation x27 -> x0, local copies, waits for them, and re-layouts: 30.4 us -> none  [the longest x4 10.1 us: body(): jnp.stack([route_rows(grad_query_slots.astype(jnp.bfloat16), groups), rou...]
  transfers between devices with their start and end apart: 13 -> 8, of which waited for: 9 -> 1; matrix products, arithmetic and copies ran while one was open for 56% -> 0% of each run, Pallas kernels for 0% -> 10%
where the time goes in v2:
time: 106 us; the launch traced here: 105 us
  waiting for transfers between devices  32.6 us (31%)
  blocking collectives  29.2 us (28%)
  Pallas kernels  22.2 us (21%)
  starting transfers between devices  20.5 us (19%)
    all_to_all x1, waiting for transfers between devices, body(): messages = lax.all_to_all(packed, ('seqo', 'mem'), 0, 0, tiled=True)  32.6 us
    all_to_all x1, blocking collectives, body(): returned = lax.all_to_all(results, ('seqo', 'mem'), 0, 0, tiled=True)  29.2 us
    ppermute x7, starting transfers between devices, body(): lax.ppermute(block, 'seqi', [(i, (i + hop) % ZONES) for i in range(ZONES)])  13.4 us
    pallas_call x1, Pallas kernels, within(): pl.pallas_call(lambda *refs: within_kernel(scale, *refs), out_shape=shape...  10.8 us
    all_to_all x1, starting transfers between devices, body(): messages = lax.all_to_all(packed, ('seqo', 'mem'), 0, 0, tiled=True)  7.13 us
    pallas_call x1, Pallas kernels, finish(): pl.pallas_call(lambda *refs: finish_kernel(scale, *refs), out_shape=shape...  4.16 us
    pallas_call x1, Pallas kernels, pack(): pl.pallas_call(pack_kernel, out_shape=shape((CHUNKS, MESSAGE, DK), BF16),...  3.25 us
    pallas_call x1, Pallas kernels, states(): pl.pallas_call(lambda *refs: states_kernel(scale, *refs), out_shape=[shap...  2.5 us
  transfers between devices with their start and end apart: 8, of which 1 were waited for; matrix products, arithmetic and copies ran while one was open for 0% of the time, Pallas kernels for 10%

profile of v2, /device:TPU:0, one launch (start us, length us, event | category | flops | bytes accessed | tf_op | source)
XLA Modules:
  0.0 105.4 jit_solution(6060168629453502394)
XLA Ops:
  0.6 3.2 %pack.1 = bf16[16,528,128]{2,1,0:T(8,128)(2,1)} custom-call(bf16[1,128,2048]{2,1,0:T(8,128)(2,1)} %q.1, bf16[1,128,2048]{2,1,0:T(8,128)(2,1)} %k.1, bf16[1,128,2048]{2,1,0:T(8,128)(2,1)} %v.1, bf16[1,128,2048]{2,1,0:T(8,128)(2,1)} %dy.1, bf16[16,128]{1,0:T(8,128)(2,1)} %bitcast.8, s32[2,128]{1,0:T(2,128)} %bitcast.9, bf16[2,128]{1,0:T(2,128)(2,1)} %bitcast.10), custom_call_target="tpu_custom_call" | custom-call | bytes 4194304 | tf_op jit(solution)/shard_map/pack/pallas_call | solution.py:89
  3.9 7.1 %all-to-all-start = ((bf16[16,528,128]{2,1,0:T(8,128)(2,1)}), bf16[16,528,128]{2,1,0:T(8,128)(2,1)S(1)}, u32[]{:S(2)}, u32[]{:S(2)}) async-start(bf16[16,528,128]{2,1,0:T(8,128)(2,1)} %pack.1), calls=%async_computation | async-start | bytes 4325376 | tf_op jit(solution)/shard_map/all_to_all | solution.py:352
  11.0 32.6 %all-to-all-done.refs_0_.refs_1_ = bf16[16,528,128]{2,1,0:T(8,128)(2,1)S(1)} async-done(((bf16[16,528,128]{2,1,0:T(8,128)(2,1)}), bf16[16,528,128]{2,1,0:T(8,128)(2,1)S(1)}, u32[]{:S(2)}, u32[]{:S(2)}) %all-to-all-start) | async-done | bytes 2162720 | tf_op jit(solution)/shard_map/all_to_all | solution.py:352
  43.6 2.5 %states.1 = (bf16[656,128]{1,0:T(8,128)(2,1)S(1)}, bf16[656,128]{1,0:T(8,128)(2,1)S(1)}, bf16[656,128]{1,0:T(8,128)(2,1)S(1)}, bf16[656,128]{1,0:T(8,128)(2,1)S(...) custom-call(s32[1]{0:T(128)} %bitcast.refs_0_, ...), custom_call_target="tpu_custom_call" | custom-call | flops 700000000 | bytes 4194304 | tf_op jit(solution)/shard_map/states/pallas_call | solution.py:180
  46.1 0.0 collective-permute-start
  46.2 2.0 %collective-permute-start.1 = (bf16[656,128]{1,0:T(8,128)(2,1)S(1)}, bf16[656,128]{1,0:T(8,128)(2,1)S(1)}, u32[]{:S(2)}, u32[]{:S(2)}) collective-permute-start(bf16[656,128]{1,0:T(8,128)(2,1)S(1)} %get-tuple-element.12), channel_id=1, source_target_pairs={{0,8},{4,12},{8,16},{12,20},{16,24},{20,28},{24,0},{28,4},{1,9},{5... | collective-permute-start | bytes 503816 | tf_op jit(solution)/shard_map/ppermute | solution.py:355
  48.2 2.9 %collective-permute-start.2 = (bf16[656,128]{1,0:T(8,128)(2,1)S(1)}, bf16[656,128]{1,0:T(8,128)(2,1)S(1)}, u32[]{:S(2)}, u32[]{:S(2)}) collective-permute-start(bf16[656,128]{1,0:T(8,128)(2,1)S(1)} %get-tuple-element.13), channel_id=1, source_target_pairs={{0,12},{4,16},{8,20},{12,24},{16,28},{20,0},{24,4},{28,8},{1,13},{... | collective-permute-start | bytes 503816 | tf_op jit(solution)/shard_map/ppermute | solution.py:355
  51.1 1.1 %collective-permute-start.3 = (bf16[656,128]{1,0:T(8,128)(2,1)S(1)}, bf16[656,128]{1,0:T(8,128)(2,1)S(1)}, u32[]{:S(2)}, u32[]{:S(2)}) collective-permute-start(bf16[656,128]{1,0:T(8,128)(2,1)S(1)} %get-tuple-element.14), channel_id=1, source_target_pairs={{0,16},{4,20},{8,24},{12,28},{16,0},{20,4},{24,8},{28,12},{1,17},{... | collective-permute-start | bytes 503816 | tf_op jit(solution)/shard_map/ppermute | solution.py:355
  52.2 2.5 %collective-permute-start.4 = (bf16[656,128]{1,0:T(8,128)(2,1)S(1)}, bf16[656,128]{1,0:T(8,128)(2,1)S(1)}, u32[]{:S(2)}, u32[]{:S(2)}) collective-permute-start(bf16[656,128]{1,0:T(8,128)(2,1)S(1)} %get-tuple-element.15), channel_id=1, source_target_pairs={{0,20},{4,24},{8,28},{12,0},{16,4},{20,8},{24,12},{28,16},{1,21},{... | collective-permute-start | bytes 503816 | tf_op jit(solution)/shard_map/ppermute | solution.py:355
  54.7 0.0 collective-permute-done.refs_3_
  54.7 1.5 %collective-permute-start.5 = (bf16[656,128]{1,0:T(8,128)(2,1)S(1)}, bf16[656,128]{1,0:T(8,128)(2,1)S(1)}, u32[]{:S(2)}, u32[]{:S(2)}) collective-permute-start(bf16[656,128]{1,0:T(8,128)(2,1)S(1)} %get-tuple-element.16), channel_id=1, source_target_pairs={{0,24},{4,28},{8,0},{12,4},{16,8},{20,12},{24,16},{28,20},{1,25},{... | collective-permute-start | bytes 503816 | tf_op jit(solution)/shard_map/ppermute | solution.py:355
  56.2 0.0 collective-permute-done.1.refs_4_
  56.2 3.3 %collective-permute-start.6 = (bf16[656,128]{1,0:T(8,128)(2,1)S(1)}, bf16[656,128]{1,0:T(8,128)(2,1)S(1)}, u32[]{:S(2)}, u32[]{:S(2)}) collective-permute-start(bf16[656,128]{1,0:T(8,128)(2,1)S(1)} %get-tuple-element.17), channel_id=1, source_target_pairs={{0,28},{4,0},{8,4},{12,8},{16,12},{20,16},{24,20},{28,24},{1,29},{... | collective-permute-start | bytes 503816 | tf_op jit(solution)/shard_map/ppermute | solution.py:355
  59.5 10.8 %within.1.refs_2_ = f32[16,4,128,128]{3,2,1,0:T(8,128)S(1)} custom-call(bf16[16,528,128]{2,1,0:T(8,128)(2,1)S(1)} %all-to-all-done.refs_0_.refs_1_), custom_call_target="tpu_custom_call" | custom-call | flops 2000000000 | bytes 6291456 | tf_op jit(solution)/shard_map/within/pallas_call | solution.py:246
  70.3 0.0 collective-permute-done.2.refs_5_
  70.3 0.0 collective-permute-done.3.refs_6_
  70.3 0.0 collective-permute-done.4.refs_7_
  70.3 0.0 collective-permute-done.5.refs_8_
  70.3 0.0 collective-permute-done.6.refs_9_
  70.4 4.2 %finish.1 = bf16[16,512,128]{2,1,0:T(8,128)(2,1)S(1)} custom-call(s32[1]{0:T(128)} %bitcast.refs_0_, bf16[16,528,128]{2,1,0:T(8,128)(2,1)S(1)} %all-to-all-done.refs_0_.refs_1_, f32[16,4,128,128]{3,2,1,0:T(8,128)S(1)} %within.1.refs_2_, bf16[656,128]{1,0:T(8,128)(2,1)S(1)} %collective-permute-done.refs_3_, ...), custom_call_target="tpu_custom_call" | custom-call | flops 1300000000 | bytes 8388608 | tf_op jit(solution)/shard_map/finish/pallas_call | solution.py:312
  74.5 29.2 %all_to_all.10.arrived = bf16[16,512,128]{2,1,0:T(8,128)(2,1)S(1)} all-to-all(bf16[16,512,128]{2,1,0:T(8,128)(2,1)S(1)} %finish.1), channel_id=1, replica_groups=mesh['mem'=4,'seqi'=8,'seqo'=4] {'seqo','mem'}, dimensions={0} | all-to-all | bytes 4194304 | tf_op jit(solution)/shard_map/all_to_all | solution.py:360
  103.8 1.5 %unpack.1 = (bf16[1,128,2048]{2,1,0:T(8,128)(2,1)}, bf16[1,128,2048]{2,1,0:T(8,128)(2,1)}, bf16[1,128,2048]{2,1,0:T(8,128)(2,1)}, bf16[1,128,2048]{2,1,0:T(8,128)(2,1)}) custom-call(bf16[16,512,128]{2,1,0:T(8,128)(2,1)S(1)} %all_to_all.10.arrived), custom_call_target="tpu_custom_call" | custom-call | bytes 4194304 | tf_op jit(solution)/shard_map/unpack/pallas_call | solution.py:337
Async XLA Ops:
  3.9 39.7 %all-to-all-start = ((bf16[16,528,128]{2,1,0:T(8,128)(2,1)}), bf16[16,528,128]{2,1,0:T(8,128)(2,1)S(1)}, u32[]{:S(2)}, u32[]{:S(2)}) async-start(bf16[16,528,128]{2,1,0:T(8,128)(2,1)} %pack.1), calls=%async_computation | async-start | bytes 4325376 | tf_op jit(solution)/shard_map/all_to_all | solution.py:352
  46.1 8.6 %collective-permute-start = (bf16[656,128]{1,0:T(8,128)(2,1)S(1)}, bf16[656,128]{1,0:T(8,128)(2,1)S(1)}, u32[]{:S(2)}, u32[]{:S(2)}) collective-permute-start(bf16[656,128]{1,0:T(8,128)(2,1)S(1)} %get-tuple-element.11), channel_id=1, source_target_pairs={{0,4},{4,8},{8,12},{12,16},{16,20},{20,24},{24,28},{28,0},{1,5},{5... | collective-permute-start | bytes 503816 | tf_op jit(solution)/shard_map/ppermute | solution.py:355
  46.2 10.0 %collective-permute-start.1 = (bf16[656,128]{1,0:T(8,128)(2,1)S(1)}, bf16[656,128]{1,0:T(8,128)(2,1)S(1)}, u32[]{:S(2)}, u32[]{:S(2)}) collective-permute-start(bf16[656,128]{1,0:T(8,128)(2,1)S(1)} %get-tuple-element.12), channel_id=1, source_target_pairs={{0,8},{4,12},{8,16},{12,20},{16,24},{20,28},{24,0},{28,4},{1,9},{5... | collective-permute-start | bytes 503816 | tf_op jit(solution)/shard_map/ppermute | solution.py:355
  48.2 22.1 %collective-permute-start.2 = (bf16[656,128]{1,0:T(8,128)(2,1)S(1)}, bf16[656,128]{1,0:T(8,128)(2,1)S(1)}, u32[]{:S(2)}, u32[]{:S(2)}) collective-permute-start(bf16[656,128]{1,0:T(8,128)(2,1)S(1)} %get-tuple-element.13), channel_id=1, source_target_pairs={{0,12},{4,16},{8,20},{12,24},{16,28},{20,0},{24,4},{28,8},{1,13},{... | collective-permute-start | bytes 503816 | tf_op jit(solution)/shard_map/ppermute | solution.py:355
  51.1 19.2 %collective-permute-start.3 = (bf16[656,128]{1,0:T(8,128)(2,1)S(1)}, bf16[656,128]{1,0:T(8,128)(2,1)S(1)}, u32[]{:S(2)}, u32[]{:S(2)}) collective-permute-start(bf16[656,128]{1,0:T(8,128)(2,1)S(1)} %get-tuple-element.14), channel_id=1, source_target_pairs={{0,16},{4,20},{8,24},{12,28},{16,0},{20,4},{24,8},{28,12},{1,17},{... | collective-permute-start | bytes 503816 | tf_op jit(solution)/shard_map/ppermute | solution.py:355
  52.2 18.1 %collective-permute-start.4 = (bf16[656,128]{1,0:T(8,128)(2,1)S(1)}, bf16[656,128]{1,0:T(8,128)(2,1)S(1)}, u32[]{:S(2)}, u32[]{:S(2)}) collective-permute-start(bf16[656,128]{1,0:T(8,128)(2,1)S(1)} %get-tuple-element.15), channel_id=1, source_target_pairs={{0,20},{4,24},{8,28},{12,0},{16,4},{20,8},{24,12},{28,16},{1,21},{... | collective-permute-start | bytes 503816 | tf_op jit(solution)/shard_map/ppermute | solution.py:355
  54.7 15.6 %collective-permute-start.5 = (bf16[656,128]{1,0:T(8,128)(2,1)S(1)}, bf16[656,128]{1,0:T(8,128)(2,1)S(1)}, u32[]{:S(2)}, u32[]{:S(2)}) collective-permute-start(bf16[656,128]{1,0:T(8,128)(2,1)S(1)} %get-tuple-element.16), channel_id=1, source_target_pairs={{0,24},{4,28},{8,0},{12,4},{16,8},{20,12},{24,16},{28,20},{1,25},{... | collective-permute-start | bytes 503816 | tf_op jit(solution)/shard_map/ppermute | solution.py:355
  56.2 14.2 %collective-permute-start.6 = (bf16[656,128]{1,0:T(8,128)(2,1)S(1)}, bf16[656,128]{1,0:T(8,128)(2,1)S(1)}, u32[]{:S(2)}, u32[]{:S(2)}) collective-permute-start(bf16[656,128]{1,0:T(8,128)(2,1)S(1)} %get-tuple-element.17), channel_id=1, source_target_pairs={{0,28},{4,0},{8,4},{12,8},{16,12},{20,16},{24,20},{28,24},{1,29},{... | collective-permute-start | bytes 503816 | tf_op jit(solution)/shard_map/ppermute | solution.py:355

commit v3 on v2

v3 whole, which is shorter than its diff:
```python
import math

import jax
import jax.numpy as jnp
from jax import lax
from jax.experimental import pallas as pl
from jax.experimental.pallas import tpu as pltpu
from jax.sharding import PartitionSpec as P

H = 16
DK = 128
ROWS = 128
MEMS = 4
KINDS = MEMS + 1
GX = 4
GY = 4
GZ = 4
CHUNKS = GX * GY
GROUP = 4
GROUPS = CHUNKS // GROUP
MESSAGE = 4 * ROWS + 16
DEEP = KINDS * DK
STATE = DEEP + 16
ZONES = 2 * GZ
OTHERS = GZ
BIG = 1e30
F32 = jnp.float32
BF16 = jnp.bfloat16
MIB = 1 << 20

NT = (((1,), (1,)), ((), ()))
TN = (((0,), (0,)), ((), ()))
NN = (((1,), (0,)), ((), ()))


def mm(a, b, dims=NN):
    return lax.dot_general(a, b, dims, preferred_element_type=F32)


VMEM = pl.BlockSpec(memory_space=pltpu.VMEM)
HBM = pl.BlockSpec(memory_space=pltpu.HBM)


def params(flops, moved, grant=20 * MIB):
    return dict(
        compiler_params=pltpu.CompilerParams(vmem_limit_bytes=grant),
        cost_estimate=pl.CostEstimate(flops=flops, bytes_accessed=moved, transcendentals=0),
    )


def shape(dims, dtype):
    return jax.ShapeDtypeStruct(dims, dtype)


def pack_kernel(q, k, v, dy, *refs):
    small, (out, held, stage, gates, named, logits, in_sems, out_sems) = refs[:3], refs[3:]
    fetches = [
        pltpu.make_async_copy(ref, place, in_sems.at[4 + n])
        for n, (ref, place) in enumerate(zip(small, (gates, named, logits)))
    ]
    for fetch in fetches:
        fetch.start()
    loads = [pltpu.make_async_copy(ref.at[0], held.at[n], in_sems.at[n]) for n, ref in enumerate((q, k, v, dy))]
    for load in loads:
        load.start()
    for fetch in fetches:
        fetch.wait()
    row = lax.broadcasted_iota(jnp.int32, (16, DK), 0)
    kinds = named[...].astype(F32)
    scores = logits[...].astype(F32)
    margin = scores[0:1] - scores[1:2]
    meta = jnp.zeros((16, DK), F32)
    for place, value in (
        (8, kinds[0:1]),
        (9, kinds[1:2]),
        (10, jax.nn.sigmoid(margin)),
        (11, jax.nn.sigmoid(-margin)),
    ):
        meta = jnp.where(row == place, value, meta)
    rates = gates[...].astype(F32)
    for h in range(H):
        stage[h, 4 * ROWS : MESSAGE, :] = jnp.where(row == 0, rates[h : h + 1], meta).astype(BF16)
    stores = []
    for n, load in enumerate(loads):
        load.wait()
        for h in range(H):
            stage[h, n * ROWS : (n + 1) * ROWS, :] = held[n, :, h * DK : (h + 1) * DK]
        last = ROWS + 16 if n == 3 else ROWS
        part = pl.ds(n * ROWS, last)
        store = pltpu.make_async_copy(stage.at[:, part, :], out.at[:, part, :], out_sems.at[n])
        store.start()
        stores.append(store)
    for store in stores:
        store.wait()


def pack(q, k, v, dy, gates, named, logits):
    return pl.pallas_call(
        pack_kernel,
        out_shape=shape((CHUNKS, MESSAGE, DK), BF16),
        in_specs=[HBM] * 7,
        out_specs=HBM,
        scratch_shapes=[
            pltpu.VMEM((4, ROWS, H * DK), BF16),
            pltpu.VMEM((CHUNKS, MESSAGE, DK), BF16),
            pltpu.VMEM((H, DK), BF16),
            pltpu.VMEM((2, DK), jnp.int32),
            pltpu.VMEM((2, DK), BF16),
            pltpu.SemaphoreType.DMA((7,)),
            pltpu.SemaphoreType.DMA((4,)),
        ],
        **params(0, 4 * MIB, 60 * MIB),
        name="pack",
    )(q, k, v, dy, gates, named, logits)


def kind_rows(first, second, first_weight, second_weight):
    row = lax.broadcasted_iota(jnp.int32, (8, DK), 0)
    kind = row.astype(F32)
    shared = (row == MEMS).astype(F32)
    hit_first = jnp.where(row < MEMS, (kind == first).astype(F32), 0.0)
    hit_second = jnp.where(row < MEMS, (kind == second).astype(F32), 0.0)
    return hit_first + hit_second + shared, hit_first * first_weight + hit_second * second_weight + shared


def running_sums(gate):
    t = lax.broadcasted_iota(jnp.int32, (DK, DK), 0)
    s = lax.broadcasted_iota(jnp.int32, (DK, DK), 1)
    gate = gate.astype(BF16)
    return mm(gate, (t <= s).astype(BF16)), mm(gate, jnp.ones((DK, DK), BF16))


def token_rows(buf):
    mask_rows, weight_rows, gate_rows = [], [], []
    for j in range(CHUNKS):
        small = buf[j, 4 * ROWS : MESSAGE, :].astype(F32)
        mask, weight = kind_rows(small[8:9], small[9:10], small[10:11], small[11:12])
        mask_rows.append(mask)
        weight_rows.append(weight)
        gate_rows.append(mask * small[0:1])
    mask, weight, gate = (jnp.concatenate(r, 0) for r in (mask_rows, weight_rows, gate_rows))
    return (mask, weight) + running_sums(gate)


def piled(total):
    parts = [total[8 * j : 8 * j + 8] for j in range(CHUNKS)]
    before, after, whole = [], [], []
    for first in range(0, CHUNKS, GROUP):
        group = parts[first : first + GROUP]
        ahead, behind = [jnp.zeros((8, DK), F32)], [group[-1]]
        for j in range(GROUP - 1):
            ahead.append(ahead[-1] + group[j])
            behind.append(behind[-1] + group[GROUP - 2 - j])
        before += ahead
        after += behind[::-1]
        whole.append(behind[-1])
    return jnp.concatenate(before, 0), jnp.concatenate(after, 0), whole


def by_kind(rows, block):
    return (block.reshape(KINDS, DK, DK) * rows[0:KINDS].reshape(KINDS, 1, DK)).reshape(DEEP, DK)


def row_block(rows, r):
    few = jnp.broadcast_to(rows[r : r + 1], (16, DK)).astype(BF16)
    return jnp.concatenate([few] * (DK // 16), 0)


def col_block(cols, r):
    return jnp.broadcast_to(cols[:, r : r + 1], (DK, DK)).astype(BF16)


def tokens(buf, j):
    return (buf[j, n * ROWS : (n + 1) * ROWS, :] for n in range(4))


def states_kernel(scale, buf, local, *refs):
    mine = lax.axis_index("seqi")
    outs, wide = refs[:OTHERS], refs[OTHERS]
    mask, weight, running, total = token_rows(buf)
    before, after, whole = piled(total)
    write_rows = mask * jnp.exp(after - running)
    read_rows = weight * scale * jnp.exp(before + running)
    decay = [jnp.exp(w) for w in whole]
    both = []
    for side, (left, right, rows) in enumerate(((1, 2, write_rows), (0, 3, read_rows))):
        sums = jnp.zeros((DEEP, DK), F32)
        for g in range(GROUPS) if side == 0 else range(GROUPS - 1, -1, -1):
            local[side, g] = sums.astype(BF16)
            group = range(g * GROUP, (g + 1) * GROUP)
            for j in group:
                flipped = buf[j, left * ROWS : (left + 1) * ROWS, :].T
                for e in range(KINDS):
                    wide[side, e * DK : (e + 1) * DK, j * DK : (j + 1) * DK] = flipped * row_block(rows, j * 8 + e)
            facing = jnp.concatenate([buf[j, right * ROWS : (right + 1) * ROWS, :] for j in group], 0)
            grown = mm(wide[side, :, g * GROUP * DK : (g + 1) * GROUP * DK], facing)
            sums = by_kind(decay[g], sums) + grown
        both.append(sums.astype(BF16))
    zone = sum(whole[1:], whole[0])
    coarse = zone.astype(BF16).astype(F32)
    length = jnp.concatenate([coarse, zone - coarse], 0).astype(BF16)
    for hop, out in enumerate(outs):
        z, c = mine // 2, mine % 2
        later = z + hop < GZ if hop > 0 else c == 0
        out[DEEP:STATE, :] = length

        @pl.when(later)
        def _():
            out[0:DEEP, :] = both[0]

        @pl.when(jnp.logical_not(later))
        def _():
            out[0:DEEP, :] = both[1]


def states(scale, messages):
    return pl.pallas_call(
        lambda *refs: states_kernel(scale, *refs),
        out_shape=[shape((2, GROUPS, DEEP, DK), BF16)] + [shape((STATE, DK), BF16)] * OTHERS,
        in_specs=[VMEM],
        out_specs=[VMEM] * (1 + OTHERS),
        scratch_shapes=[pltpu.VMEM((2, DEEP, CHUNKS * DK), BF16)],
        **params(700_000_000, 4 * MIB),
        name="states",
    )(messages)


def split(rows):
    coarse = rows.astype(BF16).astype(F32)
    return coarse, rows - coarse


def cross_kernel(scale, buf, res):
    mask, weight, running, total = token_rows(buf)
    write_row = mask * jnp.exp(total - running)
    read_row = weight * scale * jnp.exp(running)
    part = lambda a, j: a[8 * j : 8 * j + 8]
    barred = jnp.where(mask > 0, running, BIG)
    running_col = running.T
    weight_col = (weight * scale).T
    t = lax.broadcasted_iota(jnp.int32, (DK, DK), 0)
    lower = t >= lax.broadcasted_iota(jnp.int32, (DK, DK), 1)
    for g in range(GROUPS):
        first = g * GROUP
        last = first + GROUP
        sums = {}

        def add(j, n, value):
            sums[j, n] = sums[j, n] + value if (j, n) in sums else value

        for j in range(first, last):
            q, k, v, dy = tokens(buf, j)
            rows = range(j, last)
            later = range(j + 1, last)
            stack = lambda n: jnp.concatenate([buf[i, n * ROWS : (n + 1) * ROWS, :] for i in rows], 0)
            decay = jnp.zeros((DK, DK), F32)
            for r in range(j * 8, j * 8 + KINDS):
                decay = decay + weight_col[:, r : r + 1] * jnp.exp(running_col[:, r : r + 1] - barred[r : r + 1])
            decay = jnp.where(lower, decay, 0.0)
            reads, gap = [], jnp.zeros((8, DK), F32)
            for i in later:
                coarse, fine = split(part(read_row, i) * jnp.exp(gap))
                reads.append(jnp.concatenate([coarse, fine, coarse, jnp.zeros((8, DK), F32)], 0))
                gap = gap + part(total, i)
            if reads:
                coarse, fine = split(part(write_row, j))
                writes = jnp.concatenate([coarse, coarse, fine, jnp.zeros((8, DK), F32)], 0).astype(BF16)
                below = mm(jnp.concatenate(reads, 1).astype(BF16), writes, TN)
                decay = jnp.concatenate([decay, below], 0)
            queries, cotangents = stack(0), stack(3)
            attend = (mm(queries, k, NT) * decay).astype(BF16)
            grads = (mm(cotangents, v, NT) * decay).astype(BF16)
            out, grad_q = mm(attend, v), mm(grads, k)
            for place, i in enumerate(rows):
                add(i, 0, out[place * ROWS : (place + 1) * ROWS])
                add(i, 1, grad_q[place * ROWS : (place + 1) * ROWS])
            add(j, 2, mm(grads, queries, TN))
            add(j, 3, mm(attend, cotangents, TN))
        for (j, n), value in sums.items():
            res[j, n] = value


def cross(scale, messages):
    return pl.pallas_call(
        lambda *refs: cross_kernel(scale, *refs),
        out_shape=shape((CHUNKS, 4, ROWS, DK), F32),
        in_specs=[VMEM],
        out_specs=VMEM,
        **params(2_000_000_000, 6 * MIB),
        name="cross",
    )(messages)


def entering(mine, zone, arrived, lengths):
    z, c = mine // 2, mine % 2
    lengths[mine] = zone
    sources = [lax.rem(z + GZ - hop, GZ) * 2 + c for hop in range(1, GZ)]
    sources += [lax.rem(z + GZ - hop, GZ) * 2 + 1 - c for hop in range(GZ)]
    for source, ref in zip(sources, arrived):
        tail = ref[DEEP:STATE, :].astype(F32)
        lengths[source] = tail[0:8] + tail[8:16]
    start = [jnp.zeros((DEEP, DK), F32), jnp.zeros((DEEP, DK), F32)]
    for source, ref in zip(sources, arrived):
        low, high = jnp.minimum(source, mine), jnp.maximum(source, mine)
        gap = jnp.zeros((8, DK), F32)
        for other in range(ZONES):
            inside = jnp.logical_and(low < other, other < high).astype(F32)
            gap = gap + inside * lengths[other]
        earlier = (source < mine).astype(F32)
        factor = jnp.exp(gap)
        block = ref[0:DEEP, :].astype(F32)
        start[0] = start[0] + by_kind(factor * earlier, block)
        start[1] = start[1] + by_kind(factor * (1.0 - earlier), block)
    return start


def turned(state):
    return jnp.concatenate([state[e * DK : (e + 1) * DK].T for e in range(KINDS)], 0)


def finish_kernel(scale, buf, part, local, *refs):
    arrived, (out, lengths, stage, sems) = refs[: ZONES - 1], refs[ZONES - 1 :]
    stores = []
    mask, weight, running, total = token_rows(buf)
    before, after, whole = piled(total)
    read_col = (weight * scale * jnp.exp(before + running)).T
    write_col = (mask * jnp.exp(after - running)).T
    start = entering(lax.axis_index("seqi"), sum(whole[1:], whole[0]), arrived, lengths)
    for g in range(GROUPS):
        group = range(g * GROUP, (g + 1) * GROUP)
        ahead = sum(whole[:g], jnp.zeros((8, DK), F32))
        behind = sum(whole[g + 1 :], jnp.zeros((8, DK), F32))
        state = [
            (local[side, g].astype(F32) + by_kind(jnp.exp(gap), start[side])).astype(BF16)
            for side, gap in enumerate((ahead, behind))
        ]
        flipped = [turned(block) for block in state]
        blocks = [list(tokens(buf, j)) for j in group]
        for cols, jobs in (
            (read_col, ((0, state[0]), (3, flipped[0]))),
            (write_col, ((1, state[1]), (2, flipped[1]))),
        ):
            spread = [[col_block(cols, j * 8 + e) for e in range(KINDS)] for j in group]
            for source, right in jobs:
                left = jnp.concatenate(
                    [jnp.concatenate([blocks[i][source] * w for w in spread[i]], 1) for i in range(GROUP)], 0
                )
                sums = mm(left, right)
                n = (0, 3, 2, 1)[source]
                for i, j in enumerate(group):
                    stage[j, n * ROWS : (n + 1) * ROWS, :] = (
                        part[j, n] + sums[i * ROWS : (i + 1) * ROWS]
                    ).astype(BF16)
        rows = pl.ds(g * GROUP, GROUP)
        store = pltpu.make_async_copy(stage.at[rows], out.at[rows], sems.at[g])
        store.start()
        stores.append(store)
    for store in stores:
        store.wait()


def finish(scale, messages, part, local, arrived):
    return pl.pallas_call(
        lambda *refs: finish_kernel(scale, *refs),
        out_shape=shape((CHUNKS, 4 * ROWS, DK), BF16),
        in_specs=[VMEM] * (2 + ZONES),
        out_specs=HBM,
        scratch_shapes=[
            pltpu.VMEM((ZONES, 8, DK), F32),
            pltpu.VMEM((CHUNKS, 4 * ROWS, DK), BF16),
            pltpu.SemaphoreType.DMA((GROUPS,)),
        ],
        **params(1_300_000_000, 8 * MIB),
        name="finish",
    )(messages, part, local, *arrived)


def unpack_kernel(arrived, *refs):
    outs, stage, sems = refs[:4], refs[4], refs[5]
    stores = []
    for n, out in enumerate(outs):
        rows = slice(n * ROWS, (n + 1) * ROWS)
        for h in range(H):
            stage[n, :, h * DK : (h + 1) * DK] = arrived[h, rows, :]
        store = pltpu.make_async_copy(stage.at[n], out.at[0], sems.at[n])
        store.start()
        stores.append(store)
    for store in stores:
        store.wait()


def unpack(arrived):
    return pl.pallas_call(
        unpack_kernel,
        out_shape=[shape((1, ROWS, H * DK), BF16)] * 4,
        in_specs=[VMEM],
        out_specs=[HBM] * 4,
        scratch_shapes=[pltpu.VMEM((4, ROWS, H * DK), BF16), pltpu.SemaphoreType.DMA((4,))],
        **params(0, 4 * MIB),
        name="unpack",
    )(arrived)


def body(queries, keys, values, log_decay, routes, route_logits, cotangent):
    scale = 2.0 / math.sqrt(DK * ROWS * GX * GY * ZONES)
    packed = pack(queries, keys, values, cotangent, log_decay[:, 0, :], routes[0].T, route_logits[0].T)
    messages = lax.all_to_all(packed, ("seqo", "mem"), 0, 0, tiled=True)
    local, to_sibling, *sent = states(scale, messages)
    sibling = [(i, i ^ 1) for i in range(ZONES)]
    arrived = [
        lax.ppermute(block, "seqi", [(i, (i + 2 * hop) % ZONES) for i in range(ZONES)])
        for hop, block in enumerate(sent, 1)
    ]
    beside = [lax.ppermute(to_sibling, "seqi", sibling)]
    part = cross(scale, messages)
    arrived, part = lax.optimization_barrier((arrived, part))
    beside += [lax.ppermute(block, "seqi", sibling) for block in arrived]
    results = finish(scale, messages, part, local, arrived + beside)
    returned = lax.all_to_all(results, ("seqo", "mem"), 0, 0, tiled=True)
    return tuple(unpack(returned))


def solution(mesh):
    tokens_spec = P(("seqi", "seqo"), "mem", None)
    return jax.shard_map(
        body,
        mesh=mesh,
        in_specs=(tokens_spec,) * 3 + (P(None, ("seqi", "seqo"), "mem"),) + (tokens_spec,) * 3,
        out_specs=(tokens_spec,) * 4,
        check_vma=False,
    )
```

time: 106 us -> 96.1 us (0.907)
  blocking collectives: 29.2 us -> 68.2 us
  waiting for transfers between devices: 32.6 us -> 1.14 us
  starting transfers between devices: 20.5 us -> 7.67 us
  Pallas kernels: 22.2 us -> 18.1 us
    all_to_all x0 -> x1, blocking collectives: none -> 36.2 us  [body(): messages = lax.all_to_all(packed, ('seqo', 'mem'), 0, 0, tiled=True)]
    all_to_all x1 -> x0, waiting for transfers between devices: 32.6 us -> none  [body(): messages = lax.all_to_all(packed, ('seqo', 'mem'), 0, 0, tiled=True)]
    all_to_all x1 -> x0, starting transfers between devices: 7.13 us -> none  [body(): messages = lax.all_to_all(packed, ('seqo', 'mem'), 0, 0, tiled=True)]
    ppermute x7, starting transfers between devices: 13.4 us -> 7.67 us  [the longest x3 6.57 us: body(): lax.ppermute(block, 'seqi', [(i, (i + 2 * hop) % ZONES) for i in range(ZO...]
    pallas_call x1, Pallas kernels: 10.8 us -> 6.42 us  [cross(): pl.pallas_call(lambda *refs: cross_kernel(scale, *refs), out_shape=shape(...]
    all_to_all x1, blocking collectives: 29.2 us -> 31.9 us  [body(): returned = lax.all_to_all(results, ('seqo', 'mem'), 0, 0, tiled=True)]
    pallas_call x1, Pallas kernels: 4.16 us -> 5.42 us  [finish(): pl.pallas_call(lambda *refs: finish_kernel(scale, *refs), out_shape=shape...]
    ppermute x7, waiting for transfers between devices: 0.02 us -> 1.14 us  [the longest x3 1.13 us: body(): beside += [lax.ppermute(block, 'seqi', sibling) for block in arrived]]
  transfers between devices with their start and end apart: 8 -> 7, of which waited for: 1 -> 3; matrix products, arithmetic and copies ran while one was open for 0% -> 0% of each run, Pallas kernels for 10% -> 7%
where the time goes in v3:
time: 96.1 us; the launch traced here: 95.9 us
  blocking collectives  68.2 us (71%)
  Pallas kernels  18.1 us (19%)
  starting transfers between devices  7.67 us (8%)
  waiting for transfers between devices  1.14 us (1%)
    all_to_all x1, blocking collectives, body(): messages = lax.all_to_all(packed, ('seqo', 'mem'), 0, 0, tiled=True)  36.2 us
    all_to_all x1, blocking collectives, body(): returned = lax.all_to_all(results, ('seqo', 'mem'), 0, 0, tiled=True)  31.9 us
    ppermute x3, starting transfers between devices, body(): lax.ppermute(block, 'seqi', [(i, (i + 2 * hop) % ZONES) for i in range(ZO...  6.57 us
    pallas_call x1, Pallas kernels, cross(): pl.pallas_call(lambda *refs: cross_kernel(scale, *refs), out_shape=shape(...  6.42 us
    pallas_call x1, Pallas kernels, finish(): pl.pallas_call(lambda *refs: finish_kernel(scale, *refs), out_shape=shape...  5.42 us
    pallas_call x1, Pallas kernels, pack(): pl.pallas_call(pack_kernel, out_shape=shape((CHUNKS, MESSAGE, DK), BF16),...  2.61 us
    pallas_call x1, Pallas kernels, states(): pl.pallas_call(lambda *refs: states_kernel(scale, *refs), out_shape=[shap...  2.13 us
  transfers between devices with their start and end apart: 7, of which 3 were waited for; matrix products, arithmetic and copies ran while one was open for 0% of the time, Pallas kernels for 7%

profile of v3, /device:TPU:0, one launch (start us, length us, event | category | flops | bytes accessed | tf_op | source)
XLA Modules:
  0.0 95.9 jit_solution(13736063307663602330)
XLA Ops:
  0.6 2.6 %pack.1 = bf16[16,528,128]{2,1,0:T(8,128)(2,1)} custom-call(bf16[1,128,2048]{2,1,0:T(8,128)(2,1)} %q.1, bf16[1,128,2048]{2,1,0:T(8,128)(2,1)} %k.1, bf16[1,128,2048]{2,1,0:T(8,128)(2,1)} %v.1, bf16[1,128,2048]{2,1,0:T(8,128)(2,1)} %dy.1, bf16[16,128]{1,0:T(8,128)(2,1)} %bitcast.7, s32[2,128]{1,0:T(2,128)} %bitcast.8, bf16[2,128]{1,0:T(2,128)(2,1)} %bitcast.9), custom_call_target="tpu_custom_call" | custom-call | bytes 4194304 | tf_op jit(solution)/shard_map/pack/pallas_call | solution.py:98
  3.3 36.2 %all_to_all.10.refs_0_ = bf16[16,528,128]{2,1,0:T(8,128)(2,1)S(1)} all-to-all(bf16[16,528,128]{2,1,0:T(8,128)(2,1)} %pack.1), channel_id=1, replica_groups=mesh['mem'=4,'seqi'=8,'seqo'=4] {'seqo','mem'}, dimensions={0} | all-to-all | bytes 4325376 | tf_op jit(solution)/shard_map/all_to_all | solution.py:407
  39.5 2.1 %states.1 = (bf16[2,4,640,128]{3,2,1,0:T(8,128)(2,1)S(1)}, bf16[656,128]{1,0:T(8,128)(2,1)S(1)}, bf16[656,128]{1,0:T(8,128)(2,1)S(1)}, bf16[656,128]{1,0:T(8,128)(2,1)S(1)}, bf16[656,128]{1,0:T(8,128)(2,1)S(1)}) custom-call(bf16[16,528,128]{2,1,0:T(8,128)(2,1)S(1)} %all_to_all.10.refs_0_), custom_call_target="tpu_custom_call" | custom-call | flops 700000000 | bytes 4194304 | tf_op jit(solution)/shard_map/states/pallas_call | solution.py:217
  41.6 2.0 %collective-permute-start = (bf16[656,128]{1,0:T(8,128)(2,1)S(1)}, bf16[656,128]{1,0:T(8,128)(2,1)S(1)}, u32[]{:S(2)}, u32[]{:S(2)}) collective-permute-start(bf16[656,128]{1,0:T(8,128)(2,1)S(1)} %get-tuple-element.13), channel_id=1, source_target_pairs={{0,8},{4,12},{8,16},{12,20},{16,24},{20,28},{24,0},{28,4},{1,9},{5... | collective-permute-start | bytes 503816 | tf_op jit(solution)/shard_map/ppermute | solution.py:411
  43.6 3.6 %collective-permute-start.1 = (bf16[656,128]{1,0:T(8,128)(2,1)S(1)}, bf16[656,128]{1,0:T(8,128)(2,1)S(1)}, u32[]{:S(2)}, u32[]{:S(2)}) collective-permute-start(bf16[656,128]{1,0:T(8,128)(2,1)S(1)} %get-tuple-element.14), channel_id=1, source_target_pairs={{0,16},{4,20},{8,24},{12,28},{16,0},{20,4},{24,8},{28,12},{1,17},{... | collective-permute-start | bytes 503816 | tf_op jit(solution)/shard_map/ppermute | solution.py:411
  47.2 1.0 %collective-permute-start.2 = (bf16[656,128]{1,0:T(8,128)(2,1)S(1)}, bf16[656,128]{1,0:T(8,128)(2,1)S(1)}, u32[]{:S(2)}, u32[]{:S(2)}) collective-permute-start(bf16[656,128]{1,0:T(8,128)(2,1)S(1)} %get-tuple-element.15), channel_id=1, source_target_pairs={{0,24},{4,28},{8,0},{12,4},{16,8},{20,12},{24,16},{28,20},{1,25},{... | collective-permute-start | bytes 503816 | tf_op jit(solution)/shard_map/ppermute | solution.py:411
  48.2 0.0 collective-permute-start.3
  48.2 6.4 %cross.1.refs_1_ = f32[16,4,128,128]{3,2,1,0:T(8,128)S(1)} custom-call(bf16[16,528,128]{2,1,0:T(8,128)(2,1)S(1)} %all_to_all.10.refs_0_), custom_call_target="tpu_custom_call" | custom-call | flops 2000000000 | bytes 6291456 | tf_op jit(solution)/shard_map/cross/pallas_call | solution.py:284
  54.6 0.0 collective-permute-done.refs_3_
  54.6 0.0 collective-permute-done.1.refs_4_
  54.6 0.0 collective-permute-done.2.refs_5_
  54.7 0.6 collective-permute-start.4
  55.2 0.1 collective-permute-start.5
  55.3 0.4 collective-permute-start.6
  55.8 0.0 collective-permute-done.3.refs_6_
  55.8 0.5 collective-permute-done.4.refs_7_
  56.3 0.4 collective-permute-done.5.refs_8_
  56.7 0.2 collective-permute-done.6.refs_9_
  56.9 5.4 %finish.1 = bf16[16,512,128]{2,1,0:T(8,128)(2,1)S(1)} custom-call(bf16[16,528,128]{2,1,0:T(8,128)(2,1)S(1)} %all_to_all.10.refs_0_, f32[16,4,128,128]{3,2,1,0:T(8,128)S(1)} %cross.1.refs_1_, bf16[2,4,640,128]{3,2,1,0:T(8,128)(2,1)S(1)} %get-tuple-element.17.refs_2_, bf16[656,128]{1,0:T(8,128)(2,1)S(1)} %collective-permute-done.refs_3_, ...), custom_call_target="tpu_custom_call" | custom-call | flops 1300000000 | bytes 8388608 | tf_op jit(solution)/shard_map/finish/pallas_call | solution.py:363
  62.3 31.9 %all_to_all.11.arrived = bf16[16,512,128]{2,1,0:T(8,128)(2,1)S(1)} all-to-all(bf16[16,512,128]{2,1,0:T(8,128)(2,1)S(1)} %finish.1), channel_id=1, replica_groups=mesh['mem'=4,'seqi'=8,'seqo'=4] {'seqo','mem'}, dimensions={0} | all-to-all | bytes 4194304 | tf_op jit(solution)/shard_map/all_to_all | solution.py:419
  94.3 1.5 %unpack.1 = (bf16[1,128,2048]{2,1,0:T(8,128)(2,1)}, bf16[1,128,2048]{2,1,0:T(8,128)(2,1)}, bf16[1,128,2048]{2,1,0:T(8,128)(2,1)}, bf16[1,128,2048]{2,1,0:T(8,128)(2,1)}) custom-call(bf16[16,512,128]{2,1,0:T(8,128)(2,1)S(1)} %all_to_all.11.arrived), custom_call_target="tpu_custom_call" | custom-call | bytes 4194304 | tf_op jit(solution)/shard_map/unpack/pallas_call | solution.py:393
Async XLA Ops:
  41.6 13.0 %collective-permute-start = (bf16[656,128]{1,0:T(8,128)(2,1)S(1)}, bf16[656,128]{1,0:T(8,128)(2,1)S(1)}, u32[]{:S(2)}, u32[]{:S(2)}) collective-permute-start(bf16[656,128]{1,0:T(8,128)(2,1)S(1)} %get-tuple-element.13), channel_id=1, source_target_pairs={{0,8},{4,12},{8,16},{12,20},{16,24},{20,28},{24,0},{28,4},{1,9},{5... | collective-permute-start | bytes 503816 | tf_op jit(solution)/shard_map/ppermute | solution.py:411
  43.6 11.0 %collective-permute-start.1 = (bf16[656,128]{1,0:T(8,128)(2,1)S(1)}, bf16[656,128]{1,0:T(8,128)(2,1)S(1)}, u32[]{:S(2)}, u32[]{:S(2)}) collective-permute-start(bf16[656,128]{1,0:T(8,128)(2,1)S(1)} %get-tuple-element.14), channel_id=1, source_target_pairs={{0,16},{4,20},{8,24},{12,28},{16,0},{20,4},{24,8},{28,12},{1,17},{... | collective-permute-start | bytes 503816 | tf_op jit(solution)/shard_map/ppermute | solution.py:411
  47.2 7.5 %collective-permute-start.2 = (bf16[656,128]{1,0:T(8,128)(2,1)S(1)}, bf16[656,128]{1,0:T(8,128)(2,1)S(1)}, u32[]{:S(2)}, u32[]{:S(2)}) collective-permute-start(bf16[656,128]{1,0:T(8,128)(2,1)S(1)} %get-tuple-element.15), channel_id=1, source_target_pairs={{0,24},{4,28},{8,0},{12,4},{16,8},{20,12},{24,16},{28,20},{1,25},{... | collective-permute-start | bytes 503816 | tf_op jit(solution)/shard_map/ppermute | solution.py:411
  48.2 7.6 %collective-permute-start.3 = (bf16[656,128]{1,0:T(8,128)(2,1)S(1)}, bf16[656,128]{1,0:T(8,128)(2,1)S(1)}, u32[]{:S(2)}, u32[]{:S(2)}) collective-permute-start(bf16[656,128]{1,0:T(8,128)(2,1)S(1)} %get-tuple-element.21), channel_id=1, source_target_pairs={{0,4},{4,0},{8,12},{12,8},{16,20},{20,16},{24,28},{28,24},{1,5},{5... | collective-permute-start | bytes 503816 | tf_op jit(solution)/shard_map/ppermute | solution.py:414
  54.7 1.6 %collective-permute-start.4 = (bf16[656,128]{1,0:T(8,128)(2,1)S(1)}, bf16[656,128]{1,0:T(8,128)(2,1)S(1)}, u32[]{:S(2)}, u32[]{:S(2)}) collective-permute-start(bf16[656,128]{1,0:T(8,128)(2,1)S(1)} %collective-permute-done.refs_3_), channel_id=1, source_target_pairs={{0,4},{4,0},{8,12},{12,8},{16,20},{20,16},{24,28},{28,24},{1,5},{5... | collective-permute-start | bytes 503816 | tf_op jit(solution)/shard_map/ppermute | solution.py:417
  55.2 1.4 %collective-permute-start.5 = (bf16[656,128]{1,0:T(8,128)(2,1)S(1)}, bf16[656,128]{1,0:T(8,128)(2,1)S(1)}, u32[]{:S(2)}, u32[]{:S(2)}) collective-permute-start(bf16[656,128]{1,0:T(8,128)(2,1)S(1)} %collective-permute-done.1.refs_4_), channel_id=1, source_target_pairs={{0,4},{4,0},{8,12},{12,8},{16,20},{20,16},{24,28},{28,24},{1,5},{5... | collective-permute-start | bytes 503816 | tf_op jit(solution)/shard_map/ppermute | solution.py:417
  55.3 1.5 %collective-permute-start.6 = (bf16[656,128]{1,0:T(8,128)(2,1)S(1)}, bf16[656,128]{1,0:T(8,128)(2,1)S(1)}, u32[]{:S(2)}, u32[]{:S(2)}) collective-permute-start(bf16[656,128]{1,0:T(8,128)(2,1)S(1)} %collective-permute-done.2.refs_5_), channel_id=1, source_target_pairs={{0,4},{4,0},{8,12},{12,8},{16,20},{20,16},{24,28},{28,24},{1,5},{5... | collective-permute-start | bytes 503816 | tf_op jit(solution)/shard_map/ppermute | solution.py:417

commit v4 on v3

--- a/solution.py
+++ b/solution.py
@@ -236,46 +236,63 @@
     read_row = weight * scale * jnp.exp(running)
     part = lambda a, j: a[8 * j : 8 * j + 8]
     barred = jnp.where(mask > 0, running, BIG)
-    running_col = running.T
-    weight_col = (weight * scale).T
+    named = weight > 0
+    shifted_col = (running + jnp.where(named, jnp.log(jnp.where(named, weight, 1.0) * scale), -BIG)).T
     t = lax.broadcasted_iota(jnp.int32, (DK, DK), 0)
     lower = t >= lax.broadcasted_iota(jnp.int32, (DK, DK), 1)
+    def own_decay(j):
+        decay = jnp.zeros((DK, DK), F32)
+        for r in range(j * 8, j * 8 + KINDS):
+            decay = decay + jnp.exp(shifted_col[:, r : r + 1] - barred[r : r + 1])
+        return jnp.where(lower, decay, 0.0)
+
+    def factors(early, late):
+        reads, writes, gap = [], [], jnp.zeros((8, DK), F32)
+        for i in late:
+            coarse, fine = split(part(read_row, i) * jnp.exp(gap))
+            reads.append(jnp.concatenate([coarse, fine, coarse, jnp.zeros((8, DK), F32)], 0))
+            gap = gap + part(total, i)
+        gap = jnp.zeros((8, DK), F32)
+        for j in early[::-1]:
+            coarse, fine = split(part(write_row, j) * jnp.exp(gap))
+            writes.insert(0, jnp.concatenate([coarse, coarse, fine, jnp.zeros((8, DK), F32)], 0))
+            gap = gap + part(total, j)
+        reads, writes = (jnp.concatenate(r, 1).astype(BF16) for r in (reads, writes))
+        return mm(reads, writes, TN)
+
+    def tile(add, early, late, decay):
+        stack = lambda n, js: jnp.concatenate([buf[j, n * ROWS : (n + 1) * ROWS, :] for j in js], 0)
+        q, dy = stack(0, late), stack(3, late)
+        k, v = stack(1, early), stack(2, early)
+        attend = (mm(q, k, NT) * decay).astype(BF16)
+        grads = (mm(dy, v, NT) * decay).astype(BF16)
+        for n, js, left, right, dims in (
+            (0, late, attend, v, NN),
+            (1, late, grads, k, NN),
+            (2, early, grads, q, TN),
+            (3, early, attend, dy, TN),
+        ):
+            value = mm(left, right, dims)
+            for place, j in enumerate(js):
+                add(j, n, value[place * ROWS : (place + 1) * ROWS])
+
     for g in range(GROUPS):
         first = g * GROUP
-        last = first + GROUP
         sums = {}
 
         def add(j, n, value):
             sums[j, n] = sums[j, n] + value if (j, n) in sums else value
 
-        for j in range(first, last):
-            q, k, v, dy = tokens(buf, j)
-            rows = range(j, last)
-            later = range(j + 1, last)
-            stack = lambda n: jnp.concatenate([buf[i, n * ROWS : (n + 1) * ROWS, :] for i in rows], 0)
-            decay = jnp.zeros((DK, DK), F32)
-            for r in range(j * 8, j * 8 + KINDS):
-                decay = decay + weight_col[:, r : r + 1] * jnp.exp(running_col[:, r : r + 1] - barred[r : r + 1])
-            decay = jnp.where(lower, decay, 0.0)
-            reads, gap = [], jnp.zeros((8, DK), F32)
-            for i in later:
-                coarse, fine = split(part(read_row, i) * jnp.exp(gap))
-                reads.append(jnp.concatenate([coarse, fine, coarse, jnp.zeros((8, DK), F32)], 0))
-                gap = gap + part(total, i)
-            if reads:
-                coarse, fine = split(part(write_row, j))
-                writes = jnp.concatenate([coarse, coarse, fine, jnp.zeros((8, DK), F32)], 0).astype(BF16)
-                below = mm(jnp.concatenate(reads, 1).astype(BF16), writes, TN)
-                decay = jnp.concatenate([decay, below], 0)
-            queries, cotangents = stack(0), stack(3)
-            attend = (mm(queries, k, NT) * decay).astype(BF16)
-            grads = (mm(cotangents, v, NT) * decay).astype(BF16)
-            out, grad_q = mm(attend, v), mm(grads, k)
-            for place, i in enumerate(rows):
-                add(i, 0, out[place * ROWS : (place + 1) * ROWS])
-                add(i, 1, grad_q[place * ROWS : (place + 1) * ROWS])
-            add(j, 2, mm(grads, queries, TN))
-            add(j, 3, mm(attend, cotangents, TN))
+        for pair in ((first, first + 1), (first + 2, first + 3)):
+            ends = [own_decay(j) for j in pair]
+            below = factors(pair[:1], pair[1:])
+            empty = jnp.zeros((DK, DK), F32)
+            decay = jnp.concatenate(
+                [jnp.concatenate([ends[0], empty], 1), jnp.concatenate([below, ends[1]], 1)], 0
+            )
+            tile(add, pair, pair, decay)
+        early, late = (first, first + 1), (first + 2, first + 3)
+        tile(add, early, late, factors(early, late))
         for (j, n), value in sums.items():
             res[j, n] = value
 
@@ -319,8 +336,7 @@
 
 
 def finish_kernel(scale, buf, part, local, *refs):
-    arrived, (out, lengths, stage, sems) = refs[: ZONES - 1], refs[ZONES - 1 :]
-    stores = []
+    arrived, (out, lengths) = refs[: ZONES - 1], refs[ZONES - 1 :]
     mask, weight, running, total = token_rows(buf)
     before, after, whole = piled(total)
     read_col = (weight * scale * jnp.exp(before + running)).T
@@ -348,15 +364,9 @@
                 sums = mm(left, right)
                 n = (0, 3, 2, 1)[source]
                 for i, j in enumerate(group):
-                    stage[j, n * ROWS : (n + 1) * ROWS, :] = (
+                    out[j, n * ROWS : (n + 1) * ROWS, :] = (
                         part[j, n] + sums[i * ROWS : (i + 1) * ROWS]
                     ).astype(BF16)
-        rows = pl.ds(g * GROUP, GROUP)
-        store = pltpu.make_async_copy(stage.at[rows], out.at[rows], sems.at[g])
-        store.start()
-        stores.append(store)
-    for store in stores:
-        store.wait()
 
 
 def finish(scale, messages, part, local, arrived):
@@ -364,12 +374,8 @@
         lambda *refs: finish_kernel(scale, *refs),
         out_shape=shape((CHUNKS, 4 * ROWS, DK), BF16),
         in_specs=[VMEM] * (2 + ZONES),
-        out_specs=HBM,
-        scratch_shapes=[
-            pltpu.VMEM((ZONES, 8, DK), F32),
-            pltpu.VMEM((CHUNKS, 4 * ROWS, DK), BF16),
-            pltpu.SemaphoreType.DMA((GROUPS,)),
-        ],
+        out_specs=VMEM,
+        scratch_shapes=[pltpu.VMEM((ZONES, 8, DK), F32)],
         **params(1_300_000_000, 8 * MIB),
         name="finish",
     )(messages, part, local, *arrived)

time: 96.1 us -> 93.7 us (0.975)
  Pallas kernels: 18.1 us -> 15.7 us
    pallas_call x1, Pallas kernels: 6.42 us -> 5.13 us  [cross(): pl.pallas_call(lambda *refs: cross_kernel(scale, *refs), out_shape=shape(...]
    pallas_call x1, Pallas kernels: 5.42 us -> 4.32 us  [finish(): pl.pallas_call(lambda *refs: finish_kernel(scale, *refs), out_shape=shape...]
  transfers between devices with their start and end apart: 7 -> 7, of which waited for: 3 -> 4; matrix products, arithmetic and copies ran while one was open for 0% -> 0% of each run, Pallas kernels for 7% -> 5%
where the time goes in v4:
time: 93.7 us; the launch traced here: 93.5 us
  blocking collectives  68.2 us (73%)
  Pallas kernels  15.7 us (17%)
  starting transfers between devices  7.54 us (8%)
  waiting for transfers between devices  1.29 us (1%)
    all_to_all x1, blocking collectives, body(): messages = lax.all_to_all(packed, ('seqo', 'mem'), 0, 0, tiled=True)  36.2 us
    all_to_all x1, blocking collectives, body(): returned = lax.all_to_all(results, ('seqo', 'mem'), 0, 0, tiled=True)  31.9 us
    ppermute x3, starting transfers between devices, body(): lax.ppermute(block, 'seqi', [(i, (i + 2 * hop) % ZONES) for i in range(ZO...  6.57 us
    pallas_call x1, Pallas kernels, cross(): pl.pallas_call(lambda *refs: cross_kernel(scale, *refs), out_shape=shape(...  5.13 us
    pallas_call x1, Pallas kernels, finish(): pl.pallas_call(lambda *refs: finish_kernel(scale, *refs), out_shape=shape...  4.32 us
    pallas_call x1, Pallas kernels, pack(): pl.pallas_call(pack_kernel, out_shape=shape((CHUNKS, MESSAGE, DK), BF16),...  2.61 us
    pallas_call x1, Pallas kernels, states(): pl.pallas_call(lambda *refs: states_kernel(scale, *refs), out_shape=[shap...  2.13 us
  transfers between devices with their start and end apart: 7, of which 4 were waited for; matrix products, arithmetic and copies ran while one was open for 0% of the time, Pallas kernels for 5%

profile of v4, /device:TPU:0, one launch (start us, length us, event | category | flops | bytes accessed | tf_op | source)
XLA Modules:
  0.0 93.5 jit_solution(15264659842621504465)
XLA Ops:
  0.6 2.6 %pack.1 = bf16[16,528,128]{2,1,0:T(8,128)(2,1)} custom-call(bf16[1,128,2048]{2,1,0:T(8,128)(2,1)} %q.1, bf16[1,128,2048]{2,1,0:T(8,128)(2,1)} %k.1, bf16[1,128,2048]{2,1,0:T(8,128)(2,1)} %v.1, bf16[1,128,2048]{2,1,0:T(8,128)(2,1)} %dy.1, bf16[16,128]{1,0:T(8,128)(2,1)} %bitcast.7, s32[2,128]{1,0:T(2,128)} %bitcast.8, bf16[2,128]{1,0:T(2,128)(2,1)} %bitcast.9), custom_call_target="tpu_custom_call" | custom-call | bytes 4194304 | tf_op jit(solution)/shard_map/pack/pallas_call | solution.py:98
  3.3 36.2 %all_to_all.10.refs_0_ = bf16[16,528,128]{2,1,0:T(8,128)(2,1)S(1)} all-to-all(bf16[16,528,128]{2,1,0:T(8,128)(2,1)} %pack.1), channel_id=1, replica_groups=mesh['mem'=4,'seqi'=8,'seqo'=4] {'seqo','mem'}, dimensions={0} | all-to-all | bytes 4325376 | tf_op jit(solution)/shard_map/all_to_all | solution.py:413
  39.5 2.1 %states.1 = (bf16[2,4,640,128]{3,2,1,0:T(8,128)(2,1)S(1)}, bf16[656,128]{1,0:T(8,128)(2,1)S(1)}, bf16[656,128]{1,0:T(8,128)(2,1)S(1)}, bf16[656,128]{1,0:T(8,128)(2,1)S(1)}, bf16[656,128]{1,0:T(8,128)(2,1)S(1)}) custom-call(bf16[16,528,128]{2,1,0:T(8,128)(2,1)S(1)} %all_to_all.10.refs_0_), custom_call_target="tpu_custom_call" | custom-call | flops 700000000 | bytes 4194304 | tf_op jit(solution)/shard_map/states/pallas_call | solution.py:217
  41.6 2.0 %collective-permute-start = (bf16[656,128]{1,0:T(8,128)(2,1)S(1)}, bf16[656,128]{1,0:T(8,128)(2,1)S(1)}, u32[]{:S(2)}, u32[]{:S(2)}) collective-permute-start(bf16[656,128]{1,0:T(8,128)(2,1)S(1)} %get-tuple-element.13), channel_id=1, source_target_pairs={{0,8},{4,12},{8,16},{12,20},{16,24},{20,28},{24,0},{28,4},{1,9},{5... | collective-permute-start | bytes 503816 | tf_op jit(solution)/shard_map/ppermute | solution.py:417
  43.6 3.6 %collective-permute-start.1 = (bf16[656,128]{1,0:T(8,128)(2,1)S(1)}, bf16[656,128]{1,0:T(8,128)(2,1)S(1)}, u32[]{:S(2)}, u32[]{:S(2)}) collective-permute-start(bf16[656,128]{1,0:T(8,128)(2,1)S(1)} %get-tuple-element.14), channel_id=1, source_target_pairs={{0,16},{4,20},{8,24},{12,28},{16,0},{20,4},{24,8},{28,12},{1,17},{... | collective-permute-start | bytes 503816 | tf_op jit(solution)/shard_map/ppermute | solution.py:417
  47.2 1.0 %collective-permute-start.2 = (bf16[656,128]{1,0:T(8,128)(2,1)S(1)}, bf16[656,128]{1,0:T(8,128)(2,1)S(1)}, u32[]{:S(2)}, u32[]{:S(2)}) collective-permute-start(bf16[656,128]{1,0:T(8,128)(2,1)S(1)} %get-tuple-element.15), channel_id=1, source_target_pairs={{0,24},{4,28},{8,0},{12,4},{16,8},{20,12},{24,16},{28,20},{1,25},{... | collective-permute-start | bytes 503816 | tf_op jit(solution)/shard_map/ppermute | solution.py:417
  48.2 0.0 collective-permute-start.3
  48.2 5.1 %cross.1.refs_1_ = f32[16,4,128,128]{3,2,1,0:T(8,128)S(1)} custom-call(bf16[16,528,128]{2,1,0:T(8,128)(2,1)S(1)} %all_to_all.10.refs_0_), custom_call_target="tpu_custom_call" | custom-call | flops 2000000000 | bytes 6291456 | tf_op jit(solution)/shard_map/cross/pallas_call | solution.py:301
  53.3 0.0 collective-permute-done.refs_3_
  53.4 0.2 collective-permute-done.1.refs_4_
  53.5 0.0 collective-permute-done.2.refs_5_
  53.5 0.5 collective-permute-start.4
  54.0 0.1 collective-permute-start.5
  54.1 0.4 collective-permute-start.6
  54.5 0.0 collective-permute-done.3.refs_6_
  54.5 0.5 collective-permute-done.4.refs_7_
  55.0 0.4 collective-permute-done.5.refs_8_
  55.4 0.2 collective-permute-done.6.refs_9_
  55.6 4.3 %finish.1 = bf16[16,512,128]{2,1,0:T(8,128)(2,1)S(1)} custom-call(bf16[16,528,128]{2,1,0:T(8,128)(2,1)S(1)} %all_to_all.10.refs_0_, f32[16,4,128,128]{3,2,1,0:T(8,128)S(1)} %cross.1.refs_1_, bf16[2,4,640,128]{3,2,1,0:T(8,128)(2,1)S(1)} %get-tuple-element.17.refs_2_, bf16[656,128]{1,0:T(8,128)(2,1)S(1)} %collective-permute-done.refs_3_, ...), custom_call_target="tpu_custom_call" | custom-call | flops 1300000000 | bytes 8388608 | tf_op jit(solution)/shard_map/finish/pallas_call | solution.py:373
  59.9 31.9 %all_to_all.11.arrived = bf16[16,512,128]{2,1,0:T(8,128)(2,1)S(1)} all-to-all(bf16[16,512,128]{2,1,0:T(8,128)(2,1)S(1)} %finish.1), channel_id=1, replica_groups=mesh['mem'=4,'seqi'=8,'seqo'=4] {'seqo','mem'}, dimensions={0} | all-to-all | bytes 4194304 | tf_op jit(solution)/shard_map/all_to_all | solution.py:425
  91.9 1.5 %unpack.1 = (bf16[1,128,2048]{2,1,0:T(8,128)(2,1)}, bf16[1,128,2048]{2,1,0:T(8,128)(2,1)}, bf16[1,128,2048]{2,1,0:T(8,128)(2,1)}, bf16[1,128,2048]{2,1,0:T(8,128)(2,1)}) custom-call(bf16[16,512,128]{2,1,0:T(8,128)(2,1)S(1)} %all_to_all.11.arrived), custom_call_target="tpu_custom_call" | custom-call | bytes 4194304 | tf_op jit(solution)/shard_map/unpack/pallas_call | solution.py:399
Async XLA Ops:
  41.6 11.7 %collective-permute-start = (bf16[656,128]{1,0:T(8,128)(2,1)S(1)}, bf16[656,128]{1,0:T(8,128)(2,1)S(1)}, u32[]{:S(2)}, u32[]{:S(2)}) collective-permute-start(bf16[656,128]{1,0:T(8,128)(2,1)S(1)} %get-tuple-element.13), channel_id=1, source_target_pairs={{0,8},{4,12},{8,16},{12,20},{16,24},{20,28},{24,0},{28,4},{1,9},{5... | collective-permute-start | bytes 503816 | tf_op jit(solution)/shard_map/ppermute | solution.py:417
  43.6 9.9 %collective-permute-start.1 = (bf16[656,128]{1,0:T(8,128)(2,1)S(1)}, bf16[656,128]{1,0:T(8,128)(2,1)S(1)}, u32[]{:S(2)}, u32[]{:S(2)}) collective-permute-start(bf16[656,128]{1,0:T(8,128)(2,1)S(1)} %get-tuple-element.14), channel_id=1, source_target_pairs={{0,16},{4,20},{8,24},{12,28},{16,0},{20,4},{24,8},{28,12},{1,17},{... | collective-permute-start | bytes 503816 | tf_op jit(solution)/shard_map/ppermute | solution.py:417
  47.2 6.3 %collective-permute-start.2 = (bf16[656,128]{1,0:T(8,128)(2,1)S(1)}, bf16[656,128]{1,0:T(8,128)(2,1)S(1)}, u32[]{:S(2)}, u32[]{:S(2)}) collective-permute-start(bf16[656,128]{1,0:T(8,128)(2,1)S(1)} %get-tuple-element.15), channel_id=1, source_target_pairs={{0,24},{4,28},{8,0},{12,4},{16,8},{20,12},{24,16},{28,20},{1,25},{... | collective-permute-start | bytes 503816 | tf_op jit(solution)/shard_map/ppermute | solution.py:417
  48.2 6.3 %collective-permute-start.3 = (bf16[656,128]{1,0:T(8,128)(2,1)S(1)}, bf16[656,128]{1,0:T(8,128)(2,1)S(1)}, u32[]{:S(2)}, u32[]{:S(2)}) collective-permute-start(bf16[656,128]{1,0:T(8,128)(2,1)S(1)} %get-tuple-element.21), channel_id=1, source_target_pairs={{0,4},{4,0},{8,12},{12,8},{16,20},{20,16},{24,28},{28,24},{1,5},{5... | collective-permute-start | bytes 503816 | tf_op jit(solution)/shard_map/ppermute | solution.py:420
  53.5 1.5 %collective-permute-start.4 = (bf16[656,128]{1,0:T(8,128)(2,1)S(1)}, bf16[656,128]{1,0:T(8,128)(2,1)S(1)}, u32[]{:S(2)}, u32[]{:S(2)}) collective-permute-start(bf16[656,128]{1,0:T(8,128)(2,1)S(1)} %collective-permute-done.refs_3_), channel_id=1, source_target_pairs={{0,4},{4,0},{8,12},{12,8},{16,20},{20,16},{24,28},{28,24},{1,5},{5... | collective-permute-start | bytes 503816 | tf_op jit(solution)/shard_map/ppermute | solution.py:423
  54.0 1.4 %collective-permute-start.5 = (bf16[656,128]{1,0:T(8,128)(2,1)S(1)}, bf16[656,128]{1,0:T(8,128)(2,1)S(1)}, u32[]{:S(2)}, u32[]{:S(2)}) collective-permute-start(bf16[656,128]{1,0:T(8,128)(2,1)S(1)} %collective-permute-done.1.refs_4_), channel_id=1, source_target_pairs={{0,4},{4,0},{8,12},{12,8},{16,20},{20,16},{24,28},{28,24},{1,5},{5... | collective-permute-start | bytes 503816 | tf_op jit(solution)/shard_map/ppermute | solution.py:423
  54.1 1.5 %collective-permute-start.6 = (bf16[656,128]{1,0:T(8,128)(2,1)S(1)}, bf16[656,128]{1,0:T(8,128)(2,1)S(1)}, u32[]{:S(2)}, u32[]{:S(2)}) collective-permute-start(bf16[656,128]{1,0:T(8,128)(2,1)S(1)} %collective-permute-done.2.refs_5_), channel_id=1, source_target_pairs={{0,4},{4,0},{8,12},{12,8},{16,20},{20,16},{24,28},{28,24},{1,5},{5... | collective-permute-start | bytes 503816 | tf_op jit(solution)/shard_map/ppermute | solution.py:423

commit v5 on v4

--- a/solution.py
+++ b/solution.py
@@ -53,10 +53,10 @@
 
 
 def pack_kernel(q, k, v, dy, *refs):
-    small, (out, held, stage, gates, named, logits, in_sems, out_sems) = refs[:3], refs[3:]
+    small, (logits, out, held, stage, gates, named, in_sems, out_sems) = refs[:2], refs[2:]
     fetches = [
         pltpu.make_async_copy(ref, place, in_sems.at[4 + n])
-        for n, (ref, place) in enumerate(zip(small, (gates, named, logits)))
+        for n, (ref, place) in enumerate(zip(small, (gates, named)))
     ]
     for fetch in fetches:
         fetch.start()
@@ -98,15 +98,14 @@
     return pl.pallas_call(
         pack_kernel,
         out_shape=shape((CHUNKS, MESSAGE, DK), BF16),
-        in_specs=[HBM] * 7,
+        in_specs=[HBM] * 6 + [VMEM],
         out_specs=HBM,
         scratch_shapes=[
             pltpu.VMEM((4, ROWS, H * DK), BF16),
             pltpu.VMEM((CHUNKS, MESSAGE, DK), BF16),
             pltpu.VMEM((H, DK), BF16),
             pltpu.VMEM((2, DK), jnp.int32),
-            pltpu.VMEM((2, DK), BF16),
-            pltpu.SemaphoreType.DMA((7,)),
+            pltpu.SemaphoreType.DMA((6,)),
             pltpu.SemaphoreType.DMA((4,)),
         ],
         **params(0, 4 * MIB, 60 * MIB),
@@ -358,15 +357,13 @@
         ):
             spread = [[col_block(cols, j * 8 + e) for e in range(KINDS)] for j in group]
             for source, right in jobs:
-                left = jnp.concatenate(
-                    [jnp.concatenate([blocks[i][source] * w for w in spread[i]], 1) for i in range(GROUP)], 0
-                )
-                sums = mm(left, right)
                 n = (0, 3, 2, 1)[source]
+                sums = jnp.concatenate([part[j, n] for j in group], 0)
+                for e in range(KINDS):
+                    left = jnp.concatenate([blocks[i][source] * spread[i][e] for i in range(GROUP)], 0)
+                    sums = sums + mm(left, right[e * DK : (e + 1) * DK])
                 for i, j in enumerate(group):
-                    out[j, n * ROWS : (n + 1) * ROWS, :] = (
-                        part[j, n] + sums[i * ROWS : (i + 1) * ROWS]
-                    ).astype(BF16)
+                    out[j, n * ROWS : (n + 1) * ROWS, :] = sums[i * ROWS : (i + 1) * ROWS].astype(BF16)
 
 
 def finish(scale, messages, part, local, arrived):

time: 93.7 us -> 94.2 us (level)
  no operation moved by 1% of the time
where the time goes in v5:
time: 94.2 us; the launch traced here: 93.9 us
  blocking collectives  68.2 us (72%)
  Pallas kernels  16.1 us (17%)
  starting transfers between devices  7.53 us (8%)
  waiting for transfers between devices  1.29 us (1%)
    all_to_all x1, blocking collectives, body(): messages = lax.all_to_all(packed, ('seqo', 'mem'), 0, 0, tiled=True)  36.2 us
    all_to_all x1, blocking collectives, body(): returned = lax.all_to_all(results, ('seqo', 'mem'), 0, 0, tiled=True)  32 us
    ppermute x3, starting transfers between devices, body(): lax.ppermute(block, 'seqi', [(i, (i + 2 * hop) % ZONES) for i in range(ZO...  6.57 us
    pallas_call x1, Pallas kernels, cross(): pl.pallas_call(lambda *refs: cross_kernel(scale, *refs), out_shape=shape(...  5.14 us
    pallas_call x1, Pallas kernels, finish(): pl.pallas_call(lambda *refs: finish_kernel(scale, *refs), out_shape=shape...  4.08 us
    pallas_call x1, Pallas kernels, pack(): pl.pallas_call(pack_kernel, out_shape=shape((CHUNKS, MESSAGE, DK), BF16),...  3.24 us
    pallas_call x1, Pallas kernels, states(): pl.pallas_call(lambda *refs: states_kernel(scale, *refs), out_shape=[shap...  2.13 us
  transfers between devices with their start and end apart: 7, of which 4 were waited for; matrix products, arithmetic and copies ran while one was open for 0% of the time, Pallas kernels for 5%

profile of v5, /device:TPU:0, one launch (start us, length us, event | category | flops | bytes accessed | tf_op | source)
XLA Modules:
  0.0 93.9 jit_solution(12957179171417292438)
XLA Ops:
  0.6 3.2 %pack.1 = bf16[16,528,128]{2,1,0:T(8,128)(2,1)} custom-call(bf16[1,128,2048]{2,1,0:T(8,128)(2,1)} %q.1, bf16[1,128,2048]{2,1,0:T(8,128)(2,1)} %k.1, bf16[1,128,2048]{2,1,0:T(8,128)(2,1)} %v.1, bf16[1,128,2048]{2,1,0:T(8,128)(2,1)} %dy.1, bf16[16,128]{1,0:T(8,128)(2,1)} %bitcast.7, s32[2,128]{1,0:T(2,128)} %bitcast.8, bf16[2,128]{1,0:T(2,128)(2,1)} %bitcast.9), custom_call_target="tpu_custom_call" | custom-call | bytes 4194304 | tf_op jit(solution)/shard_map/pack/pallas_call | solution.py:98
  3.9 36.2 %all_to_all.10.refs_0_ = bf16[16,528,128]{2,1,0:T(8,128)(2,1)S(1)} all-to-all(bf16[16,528,128]{2,1,0:T(8,128)(2,1)} %pack.1), channel_id=1, replica_groups=mesh['mem'=4,'seqi'=8,'seqo'=4] {'seqo','mem'}, dimensions={0} | all-to-all | bytes 4325376 | tf_op jit(solution)/shard_map/all_to_all | solution.py:410
  40.1 2.1 %states.1 = (bf16[2,4,640,128]{3,2,1,0:T(8,128)(2,1)S(1)}, bf16[656,128]{1,0:T(8,128)(2,1)S(1)}, bf16[656,128]{1,0:T(8,128)(2,1)S(1)}, bf16[656,128]{1,0:T(8,128)(2,1)S(1)}, bf16[656,128]{1,0:T(8,128)(2,1)S(1)}) custom-call(bf16[16,528,128]{2,1,0:T(8,128)(2,1)S(1)} %all_to_all.10.refs_0_), custom_call_target="tpu_custom_call" | custom-call | flops 700000000 | bytes 4194304 | tf_op jit(solution)/shard_map/states/pallas_call | solution.py:216
  42.3 2.0 %collective-permute-start = (bf16[656,128]{1,0:T(8,128)(2,1)S(1)}, bf16[656,128]{1,0:T(8,128)(2,1)S(1)}, u32[]{:S(2)}, u32[]{:S(2)}) collective-permute-start(bf16[656,128]{1,0:T(8,128)(2,1)S(1)} %get-tuple-element.13), channel_id=1, source_target_pairs={{0,8},{4,12},{8,16},{12,20},{16,24},{20,28},{24,0},{28,4},{1,9},{5... | collective-permute-start | bytes 503816 | tf_op jit(solution)/shard_map/ppermute | solution.py:414
  44.2 3.6 %collective-permute-start.1 = (bf16[656,128]{1,0:T(8,128)(2,1)S(1)}, bf16[656,128]{1,0:T(8,128)(2,1)S(1)}, u32[]{:S(2)}, u32[]{:S(2)}) collective-permute-start(bf16[656,128]{1,0:T(8,128)(2,1)S(1)} %get-tuple-element.14), channel_id=1, source_target_pairs={{0,16},{4,20},{8,24},{12,28},{16,0},{20,4},{24,8},{28,12},{1,17},{... | collective-permute-start | bytes 503816 | tf_op jit(solution)/shard_map/ppermute | solution.py:414
  47.8 1.0 %collective-permute-start.2 = (bf16[656,128]{1,0:T(8,128)(2,1)S(1)}, bf16[656,128]{1,0:T(8,128)(2,1)S(1)}, u32[]{:S(2)}, u32[]{:S(2)}) collective-permute-start(bf16[656,128]{1,0:T(8,128)(2,1)S(1)} %get-tuple-element.15), channel_id=1, source_target_pairs={{0,24},{4,28},{8,0},{12,4},{16,8},{20,12},{24,16},{28,20},{1,25},{... | collective-permute-start | bytes 503816 | tf_op jit(solution)/shard_map/ppermute | solution.py:414
  48.8 0.0 collective-permute-start.3
  48.8 5.1 %cross.1.refs_1_ = f32[16,4,128,128]{3,2,1,0:T(8,128)S(1)} custom-call(bf16[16,528,128]{2,1,0:T(8,128)(2,1)S(1)} %all_to_all.10.refs_0_), custom_call_target="tpu_custom_call" | custom-call | flops 2000000000 | bytes 6291456 | tf_op jit(solution)/shard_map/cross/pallas_call | solution.py:300
  54.0 0.0 collective-permute-done.refs_3_
  54.0 0.2 collective-permute-done.1.refs_4_
  54.1 0.0 collective-permute-done.2.refs_5_
  54.1 0.5 collective-permute-start.4
  54.6 0.1 collective-permute-start.5
  54.7 0.4 collective-permute-start.6
  55.1 0.0 collective-permute-done.3.refs_6_
  55.1 0.5 collective-permute-done.4.refs_7_
  55.6 0.4 collective-permute-done.5.refs_8_
  56.0 0.2 collective-permute-done.6.refs_9_
  56.2 4.1 %finish.1 = bf16[16,512,128]{2,1,0:T(8,128)(2,1)S(1)} custom-call(bf16[16,528,128]{2,1,0:T(8,128)(2,1)S(1)} %all_to_all.10.refs_0_, f32[16,4,128,128]{3,2,1,0:T(8,128)S(1)} %cross.1.refs_1_, bf16[2,4,640,128]{3,2,1,0:T(8,128)(2,1)S(1)} %get-tuple-element.17.refs_2_, bf16[656,128]{1,0:T(8,128)(2,1)S(1)} %collective-permute-done.refs_3_, ...), custom_call_target="tpu_custom_call" | custom-call | flops 1300000000 | bytes 8388608 | tf_op jit(solution)/shard_map/finish/pallas_call | solution.py:370
  60.3 32.0 %all_to_all.11.arrived = bf16[16,512,128]{2,1,0:T(8,128)(2,1)S(1)} all-to-all(bf16[16,512,128]{2,1,0:T(8,128)(2,1)S(1)} %finish.1), channel_id=1, replica_groups=mesh['mem'=4,'seqi'=8,'seqo'=4] {'seqo','mem'}, dimensions={0} | all-to-all | bytes 4194304 | tf_op jit(solution)/shard_map/all_to_all | solution.py:422
  92.3 1.5 %unpack.1 = (bf16[1,128,2048]{2,1,0:T(8,128)(2,1)}, bf16[1,128,2048]{2,1,0:T(8,128)(2,1)}, bf16[1,128,2048]{2,1,0:T(8,128)(2,1)}, bf16[1,128,2048]{2,1,0:T(8,128)(2,1)}) custom-call(bf16[16,512,128]{2,1,0:T(8,128)(2,1)S(1)} %all_to_all.11.arrived), custom_call_target="tpu_custom_call" | custom-call | bytes 4194304 | tf_op jit(solution)/shard_map/unpack/pallas_call | solution.py:396
Async XLA Ops:
  42.3 11.7 %collective-permute-start = (bf16[656,128]{1,0:T(8,128)(2,1)S(1)}, bf16[656,128]{1,0:T(8,128)(2,1)S(1)}, u32[]{:S(2)}, u32[]{:S(2)}) collective-permute-start(bf16[656,128]{1,0:T(8,128)(2,1)S(1)} %get-tuple-element.13), channel_id=1, source_target_pairs={{0,8},{4,12},{8,16},{12,20},{16,24},{20,28},{24,0},{28,4},{1,9},{5... | collective-permute-start | bytes 503816 | tf_op jit(solution)/shard_map/ppermute | solution.py:414
  44.2 9.9 %collective-permute-start.1 = (bf16[656,128]{1,0:T(8,128)(2,1)S(1)}, bf16[656,128]{1,0:T(8,128)(2,1)S(1)}, u32[]{:S(2)}, u32[]{:S(2)}) collective-permute-start(bf16[656,128]{1,0:T(8,128)(2,1)S(1)} %get-tuple-element.14), channel_id=1, source_target_pairs={{0,16},{4,20},{8,24},{12,28},{16,0},{20,4},{24,8},{28,12},{1,17},{... | collective-permute-start | bytes 503816 | tf_op jit(solution)/shard_map/ppermute | solution.py:414
  47.8 6.3 %collective-permute-start.2 = (bf16[656,128]{1,0:T(8,128)(2,1)S(1)}, bf16[656,128]{1,0:T(8,128)(2,1)S(1)}, u32[]{:S(2)}, u32[]{:S(2)}) collective-permute-start(bf16[656,128]{1,0:T(8,128)(2,1)S(1)} %get-tuple-element.15), channel_id=1, source_target_pairs={{0,24},{4,28},{8,0},{12,4},{16,8},{20,12},{24,16},{28,20},{1,25},{... | collective-permute-start | bytes 503816 | tf_op jit(solution)/shard_map/ppermute | solution.py:414
  48.8 6.3 %collective-permute-start.3 = (bf16[656,128]{1,0:T(8,128)(2,1)S(1)}, bf16[656,128]{1,0:T(8,128)(2,1)S(1)}, u32[]{:S(2)}, u32[]{:S(2)}) collective-permute-start(bf16[656,128]{1,0:T(8,128)(2,1)S(1)} %get-tuple-element.21), channel_id=1, source_target_pairs={{0,4},{4,0},{8,12},{12,8},{16,20},{20,16},{24,28},{28,24},{1,5},{5... | collective-permute-start | bytes 503816 | tf_op jit(solution)/shard_map/ppermute | solution.py:417
  54.1 1.5 %collective-permute-start.4 = (bf16[656,128]{1,0:T(8,128)(2,1)S(1)}, bf16[656,128]{1,0:T(8,128)(2,1)S(1)}, u32[]{:S(2)}, u32[]{:S(2)}) collective-permute-start(bf16[656,128]{1,0:T(8,128)(2,1)S(1)} %collective-permute-done.refs_3_), channel_id=1, source_target_pairs={{0,4},{4,0},{8,12},{12,8},{16,20},{20,16},{24,28},{28,24},{1,5},{5... | collective-permute-start | bytes 503816 | tf_op jit(solution)/shard_map/ppermute | solution.py:420
  54.6 1.4 %collective-permute-start.5 = (bf16[656,128]{1,0:T(8,128)(2,1)S(1)}, bf16[656,128]{1,0:T(8,128)(2,1)S(1)}, u32[]{:S(2)}, u32[]{:S(2)}) collective-permute-start(bf16[656,128]{1,0:T(8,128)(2,1)S(1)} %collective-permute-done.1.refs_4_), channel_id=1, source_target_pairs={{0,4},{4,0},{8,12},{12,8},{16,20},{20,16},{24,28},{28,24},{1,5},{5... | collective-permute-start | bytes 503816 | tf_op jit(solution)/shard_map/ppermute | solution.py:420
  54.7 1.5 %collective-permute-start.6 = (bf16[656,128]{1,0:T(8,128)(2,1)S(1)}, bf16[656,128]{1,0:T(8,128)(2,1)S(1)}, u32[]{:S(2)}, u32[]{:S(2)}) collective-permute-start(bf16[656,128]{1,0:T(8,128)(2,1)S(1)} %collective-permute-done.2.refs_5_), channel_id=1, source_target_pairs={{0,4},{4,0},{8,12},{12,8},{16,20},{20,16},{24,28},{28,24},{1,5},{5... | collective-permute-start | bytes 503816 | tf_op jit(solution)/shard_map/ppermute | solution.py:420

commit v6 on v5

--- a/solution.py
+++ b/solution.py
@@ -18,6 +18,7 @@
 CHUNKS = GX * GY
 GROUP = 4
 GROUPS = CHUNKS // GROUP
+SOONER = CHUNKS - GROUP
 MESSAGE = 4 * ROWS + 16
 DEEP = KINDS * DK
 STATE = DEEP + 16
@@ -229,7 +230,7 @@
     return coarse, rows - coarse
 
 
-def cross_kernel(scale, buf, res):
+def cross_kernel(scale, groups, buf, res):
     mask, weight, running, total = token_rows(buf)
     write_row = mask * jnp.exp(total - running)
     read_row = weight * scale * jnp.exp(running)
@@ -275,7 +276,7 @@
             for place, j in enumerate(js):
                 add(j, n, value[place * ROWS : (place + 1) * ROWS])
 
-    for g in range(GROUPS):
+    for g in groups:
         first = g * GROUP
         sums = {}
 
@@ -293,16 +294,16 @@
         early, late = (first, first + 1), (first + 2, first + 3)
         tile(add, early, late, factors(early, late))
         for (j, n), value in sums.items():
-            res[j, n] = value
-
-
-def cross(scale, messages):
+            res[j - groups[0] * GROUP, n] = value
+
+
+def cross(scale, groups, messages):
     return pl.pallas_call(
-        lambda *refs: cross_kernel(scale, *refs),
-        out_shape=shape((CHUNKS, 4, ROWS, DK), F32),
+        lambda *refs: cross_kernel(scale, groups, *refs),
+        out_shape=shape((len(groups) * GROUP, 4, ROWS, DK), F32),
         in_specs=[VMEM],
         out_specs=VMEM,
-        **params(2_000_000_000, 6 * MIB),
+        **params(400_000_000 * len(groups), 2 * MIB * len(groups)),
         name="cross",
     )(messages)
 
@@ -334,7 +335,7 @@
     return jnp.concatenate([state[e * DK : (e + 1) * DK].T for e in range(KINDS)], 0)
 
 
-def finish_kernel(scale, buf, part, local, *refs):
+def finish_kernel(scale, buf, part, rest, local, *refs):
     arrived, (out, lengths) = refs[: ZONES - 1], refs[ZONES - 1 :]
     mask, weight, running, total = token_rows(buf)
     before, after, whole = piled(total)
@@ -358,7 +359,7 @@
             spread = [[col_block(cols, j * 8 + e) for e in range(KINDS)] for j in group]
             for source, right in jobs:
                 n = (0, 3, 2, 1)[source]
-                sums = jnp.concatenate([part[j, n] for j in group], 0)
+                sums = jnp.concatenate([part[j, n] if j < SOONER else rest[j - SOONER, n] for j in group], 0)
                 for e in range(KINDS):
                     left = jnp.concatenate([blocks[i][source] * spread[i][e] for i in range(GROUP)], 0)
                     sums = sums + mm(left, right[e * DK : (e + 1) * DK])
@@ -366,16 +367,16 @@
                     out[j, n * ROWS : (n + 1) * ROWS, :] = sums[i * ROWS : (i + 1) * ROWS].astype(BF16)
 
 
-def finish(scale, messages, part, local, arrived):
+def finish(scale, messages, part, rest, local, arrived):
     return pl.pallas_call(
         lambda *refs: finish_kernel(scale, *refs),
         out_shape=shape((CHUNKS, 4 * ROWS, DK), BF16),
-        in_specs=[VMEM] * (2 + ZONES),
+        in_specs=[VMEM] * (3 + ZONES),
         out_specs=VMEM,
         scratch_shapes=[pltpu.VMEM((ZONES, 8, DK), F32)],
         **params(1_300_000_000, 8 * MIB),
         name="finish",
-    )(messages, part, local, *arrived)
+    )(messages, part, rest, local, *arrived)
 
 
 def unpack_kernel(arrived, *refs):
@@ -415,10 +416,11 @@
         for hop, block in enumerate(sent, 1)
     ]
     beside = [lax.ppermute(to_sibling, "seqi", sibling)]
-    part = cross(scale, messages)
-    arrived, part = lax.optimization_barrier((arrived, part))
+    part = cross(scale, tuple(range(GROUPS - 1)), messages)
+    arrived, part, messages = lax.optimization_barrier((arrived, part, messages))
     beside += [lax.ppermute(block, "seqi", sibling) for block in arrived]
-    results = finish(scale, messages, part, local, arrived + beside)
+    rest = cross(scale, (GROUPS - 1,), messages)
+    results = finish(scale, messages, part, rest, local, arrived + beside)
     returned = lax.all_to_all(results, ("seqo", "mem"), 0, 0, tiled=True)
     return tuple(unpack(returned))
 

time: 94.2 us -> 94.6 us (level)
    ppermute x3, waiting for transfers between devices: 0.16 us -> 1.36 us  [body(): lax.ppermute(block, 'seqi', [(i, (i + 2 * hop) % ZONES) for i in range(ZO...]
    ppermute x3, waiting for transfers between devices: 1.13 us -> 0.01 us  [body(): beside += [lax.ppermute(block, 'seqi', sibling) for block in arrived]]
    pallas_call x1 -> x2, Pallas kernels: 5.14 us -> 5.51 us  [cross(): pl.pallas_call(lambda *refs: cross_kernel(scale, groups, *refs), out_shap...]
  transfers between devices with their start and end apart: 7 -> 7, of which waited for: 4 -> 1; matrix products, arithmetic and copies ran while one was open for 0% -> 0% of each run, Pallas kernels for 5% -> 6%
where the time goes in v6:
time: 94.6 us; the launch traced here: 94.4 us
  blocking collectives  68.6 us (73%)
  Pallas kernels  16.4 us (17%)
  starting transfers between devices  7.08 us (7%)
  waiting for transfers between devices  1.37 us (1%)
    all_to_all x1, blocking collectives, body(): messages = lax.all_to_all(packed, ('seqo', 'mem'), 0, 0, tiled=True)  36.2 us
    all_to_all x1, blocking collectives, body(): returned = lax.all_to_all(results, ('seqo', 'mem'), 0, 0, tiled=True)  32.4 us
    ppermute x3, starting transfers between devices, body(): lax.ppermute(block, 'seqi', [(i, (i + 2 * hop) % ZONES) for i in range(ZO...  6.57 us
    pallas_call x2, Pallas kernels, cross(): pl.pallas_call(lambda *refs: cross_kernel(scale, groups, *refs), out_shap...  5.51 us
    pallas_call x1, Pallas kernels, finish(): pl.pallas_call(lambda *refs: finish_kernel(scale, *refs), out_shape=shape...  4.08 us
    pallas_call x1, Pallas kernels, pack(): pl.pallas_call(pack_kernel, out_shape=shape((CHUNKS, MESSAGE, DK), BF16),...  3.24 us
    pallas_call x1, Pallas kernels, states(): pl.pallas_call(lambda *refs: states_kernel(scale, *refs), out_shape=[shap...  2.13 us
  transfers between devices with their start and end apart: 7, of which 1 were waited for; matrix products, arithmetic and copies ran while one was open for 0% of the time, Pallas kernels for 6%

profile of v6, /device:TPU:0, one launch (start us, length us, event | category | flops | bytes accessed | tf_op | source)
XLA Modules:
  0.0 94.4 jit_solution(5063046886696099113)
XLA Ops:
  0.6 3.2 %pack.1 = bf16[16,528,128]{2,1,0:T(8,128)(2,1)} custom-call(bf16[1,128,2048]{2,1,0:T(8,128)(2,1)} %q.1, bf16[1,128,2048]{2,1,0:T(8,128)(2,1)} %k.1, bf16[1,128,2048]{2,1,0:T(8,128)(2,1)} %v.1, bf16[1,128,2048]{2,1,0:T(8,128)(2,1)} %dy.1, bf16[16,128]{1,0:T(8,128)(2,1)} %bitcast.7, s32[2,128]{1,0:T(2,128)} %bitcast.8, bf16[2,128]{1,0:T(2,128)(2,1)} %bitcast.9), custom_call_target="tpu_custom_call" | custom-call | bytes 4194304 | tf_op jit(solution)/shard_map/pack/pallas_call | solution.py:99
  3.9 36.2 %all_to_all.10.refs_0_ = bf16[16,528,128]{2,1,0:T(8,128)(2,1)S(1)} all-to-all(bf16[16,528,128]{2,1,0:T(8,128)(2,1)} %pack.1), channel_id=1, replica_groups=mesh['mem'=4,'seqi'=8,'seqo'=4] {'seqo','mem'}, dimensions={0} | all-to-all | bytes 4325376 | tf_op jit(solution)/shard_map/all_to_all | solution.py:411
  40.1 2.1 %states.1 = (bf16[2,4,640,128]{3,2,1,0:T(8,128)(2,1)S(1)}, bf16[656,128]{1,0:T(8,128)(2,1)S(1)}, bf16[656,128]{1,0:T(8,128)(2,1)S(1)}, bf16[656,128]{1,0:T(8,128)(2,1)S(1)}, bf16[656,128]{1,0:T(8,128)(2,1)S(1)}) custom-call(bf16[16,528,128]{2,1,0:T(8,128)(2,1)S(1)} %all_to_all.10.refs_0_), custom_call_target="tpu_custom_call" | custom-call | flops 700000000 | bytes 4194304 | tf_op jit(solution)/shard_map/states/pallas_call | solution.py:217
  42.3 2.0 %collective-permute-start = (bf16[656,128]{1,0:T(8,128)(2,1)S(1)}, bf16[656,128]{1,0:T(8,128)(2,1)S(1)}, u32[]{:S(2)}, u32[]{:S(2)}) collective-permute-start(bf16[656,128]{1,0:T(8,128)(2,1)S(1)} %get-tuple-element.14), channel_id=1, source_target_pairs={{0,8},{4,12},{8,16},{12,20},{16,24},{20,28},{24,0},{28,4},{1,9},{5... | collective-permute-start | bytes 503816 | tf_op jit(solution)/shard_map/ppermute | solution.py:415
  44.2 3.6 %collective-permute-start.1 = (bf16[656,128]{1,0:T(8,128)(2,1)S(1)}, bf16[656,128]{1,0:T(8,128)(2,1)S(1)}, u32[]{:S(2)}, u32[]{:S(2)}) collective-permute-start(bf16[656,128]{1,0:T(8,128)(2,1)S(1)} %get-tuple-element.15), channel_id=1, source_target_pairs={{0,16},{4,20},{8,24},{12,28},{16,0},{20,4},{24,8},{28,12},{1,17},{... | collective-permute-start | bytes 503816 | tf_op jit(solution)/shard_map/ppermute | solution.py:415
  47.8 1.0 %collective-permute-start.2 = (bf16[656,128]{1,0:T(8,128)(2,1)S(1)}, bf16[656,128]{1,0:T(8,128)(2,1)S(1)}, u32[]{:S(2)}, u32[]{:S(2)}) collective-permute-start(bf16[656,128]{1,0:T(8,128)(2,1)S(1)} %get-tuple-element.16), channel_id=1, source_target_pairs={{0,24},{4,28},{8,0},{12,4},{16,8},{20,12},{24,16},{28,20},{1,25},{... | collective-permute-start | bytes 503816 | tf_op jit(solution)/shard_map/ppermute | solution.py:415
  48.8 0.0 collective-permute-start.3
  48.8 3.9 %cross.2.refs_1_ = f32[12,4,128,128]{3,2,1,0:T(8,128)S(1)} custom-call(bf16[16,528,128]{2,1,0:T(8,128)(2,1)S(1)} %all_to_all.10.refs_0_), custom_call_target="tpu_custom_call" | custom-call | flops 1200000000 | bytes 6291456 | tf_op jit(solution)/shard_map/cross/pallas_call | solution.py:301
  52.8 0.0 collective-permute-done.refs_4_
  52.8 1.4 %collective-permute-done.1.refs_5_ = bf16[656,128]{1,0:T(8,128)(2,1)S(1)} collective-permute-done((bf16[656,128]{1,0:T(8,128)(2,1)S(1)}, bf16[656,128]{1,0:T(8,128)(2,1)S(1)}, u32[]{:S(2)}, u32[]{:S(2)}) %collective-permute-start.1) | collective-permute-done | bytes 167968 | tf_op jit(solution)/shard_map/ppermute | solution.py:415
  54.1 0.0 collective-permute-done.2.refs_6_
  54.1 0.0 collective-permute-start.4
  54.1 0.5 collective-permute-start.5
  54.7 0.0 collective-permute-start.6
  54.7 1.6 %cross.3.refs_2_ = f32[4,4,128,128]{3,2,1,0:T(8,128)S(1)} custom-call(bf16[16,528,128]{2,1,0:T(8,128)(2,1)S(1)} %all_to_all.10.refs_0_), custom_call_target="tpu_custom_call" | custom-call | flops 400000000 | bytes 2097152 | tf_op jit(solution)/shard_map/cross/pallas_call | solution.py:301
  56.2 0.0 collective-permute-done.3.refs_7_
  56.2 0.0 collective-permute-done.4.refs_8_
  56.3 0.0 collective-permute-done.5.refs_9_
  56.3 0.0 collective-permute-done.6.refs_10_
  56.3 4.1 %finish.1 = bf16[16,512,128]{2,1,0:T(8,128)(2,1)S(1)} custom-call(bf16[16,528,128]{2,1,0:T(8,128)(2,1)S(1)} %all_to_all.10.refs_0_, f32[12,4,128,128]{3,2,1,0:T(8,128)S(1)} %cross.2.refs_1_, f32[4,4,128,128]{3,2,1,0:T(8,128)S(1)} %cross.3.refs_2_, bf16[2,4,640,128]{3,2,1,0:T(8,128)(2,1)S(1)} %get-tuple-element.19.refs_3_, ...), custom_call_target="tpu_custom_call" | custom-call | flops 1300000000 | bytes 8388608 | tf_op jit(solution)/shard_map/finish/pallas_call | solution.py:371
  60.4 32.4 %all_to_all.11.arrived = bf16[16,512,128]{2,1,0:T(8,128)(2,1)S(1)} all-to-all(bf16[16,512,128]{2,1,0:T(8,128)(2,1)S(1)} %finish.1), channel_id=1, replica_groups=mesh['mem'=4,'seqi'=8,'seqo'=4] {'seqo','mem'}, dimensions={0} | all-to-all | bytes 4194304 | tf_op jit(solution)/shard_map/all_to_all | solution.py:424
  92.7 1.5 %unpack.1 = (bf16[1,128,2048]{2,1,0:T(8,128)(2,1)}, bf16[1,128,2048]{2,1,0:T(8,128)(2,1)}, bf16[1,128,2048]{2,1,0:T(8,128)(2,1)}, bf16[1,128,2048]{2,1,0:T(8,128)(2,1)}) custom-call(bf16[16,512,128]{2,1,0:T(8,128)(2,1)S(1)} %all_to_all.11.arrived), custom_call_target="tpu_custom_call" | custom-call | bytes 4194304 | tf_op jit(solution)/shard_map/unpack/pallas_call | solution.py:397
Async XLA Ops:
  42.3 10.5 %collective-permute-start = (bf16[656,128]{1,0:T(8,128)(2,1)S(1)}, bf16[656,128]{1,0:T(8,128)(2,1)S(1)}, u32[]{:S(2)}, u32[]{:S(2)}) collective-permute-start(bf16[656,128]{1,0:T(8,128)(2,1)S(1)} %get-tuple-element.14), channel_id=1, source_target_pairs={{0,8},{4,12},{8,16},{12,20},{16,24},{20,28},{24,0},{28,4},{1,9},{5... | collective-permute-start | bytes 503816 | tf_op jit(solution)/shard_map/ppermute | solution.py:415
  44.2 9.9 %collective-permute-start.1 = (bf16[656,128]{1,0:T(8,128)(2,1)S(1)}, bf16[656,128]{1,0:T(8,128)(2,1)S(1)}, u32[]{:S(2)}, u32[]{:S(2)}) collective-permute-start(bf16[656,128]{1,0:T(8,128)(2,1)S(1)} %get-tuple-element.15), channel_id=1, source_target_pairs={{0,16},{4,20},{8,24},{12,28},{16,0},{20,4},{24,8},{28,12},{1,17},{... | collective-permute-start | bytes 503816 | tf_op jit(solution)/shard_map/ppermute | solution.py:415
  47.8 6.3 %collective-permute-start.2 = (bf16[656,128]{1,0:T(8,128)(2,1)S(1)}, bf16[656,128]{1,0:T(8,128)(2,1)S(1)}, u32[]{:S(2)}, u32[]{:S(2)}) collective-permute-start(bf16[656,128]{1,0:T(8,128)(2,1)S(1)} %get-tuple-element.16), channel_id=1, source_target_pairs={{0,24},{4,28},{8,0},{12,4},{16,8},{20,12},{24,16},{28,20},{1,25},{... | collective-permute-start | bytes 503816 | tf_op jit(solution)/shard_map/ppermute | solution.py:415
  48.8 7.4 %collective-permute-start.3 = (bf16[656,128]{1,0:T(8,128)(2,1)S(1)}, bf16[656,128]{1,0:T(8,128)(2,1)S(1)}, u32[]{:S(2)}, u32[]{:S(2)}) collective-permute-start(bf16[656,128]{1,0:T(8,128)(2,1)S(1)} %get-tuple-element.23), channel_id=1, source_target_pairs={{0,4},{4,0},{8,12},{12,8},{16,20},{20,16},{24,28},{28,24},{1,5},{5... | collective-permute-start | bytes 503816 | tf_op jit(solution)/shard_map/ppermute | solution.py:418
  54.1 2.1 %collective-permute-start.4 = (bf16[656,128]{1,0:T(8,128)(2,1)S(1)}, bf16[656,128]{1,0:T(8,128)(2,1)S(1)}, u32[]{:S(2)}, u32[]{:S(2)}) collective-permute-start(bf16[656,128]{1,0:T(8,128)(2,1)S(1)} %collective-permute-done.refs_4_), channel_id=1, source_target_pairs={{0,4},{4,0},{8,12},{12,8},{16,20},{20,16},{24,28},{28,24},{1,5},{5... | collective-permute-start | bytes 503816 | tf_op jit(solution)/shard_map/ppermute | solution.py:421
  54.1 2.1 %collective-permute-start.5 = (bf16[656,128]{1,0:T(8,128)(2,1)S(1)}, bf16[656,128]{1,0:T(8,128)(2,1)S(1)}, u32[]{:S(2)}, u32[]{:S(2)}) collective-permute-start(bf16[656,128]{1,0:T(8,128)(2,1)S(1)} %collective-permute-done.1.refs_5_), channel_id=1, source_target_pairs={{0,4},{4,0},{8,12},{12,8},{16,20},{20,16},{24,28},{28,24},{1,5},{5... | collective-permute-start | bytes 503816 | tf_op jit(solution)/shard_map/ppermute | solution.py:421
  54.7 1.6 %collective-permute-start.6 = (bf16[656,128]{1,0:T(8,128)(2,1)S(1)}, bf16[656,128]{1,0:T(8,128)(2,1)S(1)}, u32[]{:S(2)}, u32[]{:S(2)}) collective-permute-start(bf16[656,128]{1,0:T(8,128)(2,1)S(1)} %collective-permute-done.2.refs_6_), channel_id=1, source_target_pairs={{0,4},{4,0},{8,12},{12,8},{16,20},{20,16},{24,28},{28,24},{1,5},{5... | collective-permute-start | bytes 503816 | tf_op jit(solution)/shard_map/ppermute | solution.py:421

commit v7 on v5

--- a/solution.py
+++ b/solution.py
@@ -410,10 +410,9 @@
     messages = lax.all_to_all(packed, ("seqo", "mem"), 0, 0, tiled=True)
     local, to_sibling, *sent = states(scale, messages)
     sibling = [(i, i ^ 1) for i in range(ZONES)]
-    arrived = [
-        lax.ppermute(block, "seqi", [(i, (i + 2 * hop) % ZONES) for i in range(ZONES)])
-        for hop, block in enumerate(sent, 1)
-    ]
+    ring = lambda hop: [(i, (i + 2 * hop) % ZONES) for i in range(ZONES)]
+    farthest = lax.ppermute(sent[1], "seqi", ring(2))
+    arrived = [lax.ppermute(sent[0], "seqi", ring(1)), farthest, lax.ppermute(sent[2], "seqi", ring(3))]
     beside = [lax.ppermute(to_sibling, "seqi", sibling)]
     part = cross(scale, messages)
     arrived, part = lax.optimization_barrier((arrived, part))

time: 94.2 us -> 94.2 us (level)
  no operation moved by 1% of the time
where the time goes in v7:
time: 94.2 us; the launch traced here: 93.9 us
  blocking collectives  68.2 us (72%)
  Pallas kernels  16.1 us (17%)
  starting transfers between devices  7.53 us (8%)
  waiting for transfers between devices  1.29 us (1%)
    all_to_all x1, blocking collectives, body(): messages = lax.all_to_all(packed, ('seqo', 'mem'), 0, 0, tiled=True)  36.2 us
    all_to_all x1, blocking collectives, body(): returned = lax.all_to_all(results, ('seqo', 'mem'), 0, 0, tiled=True)  32 us
    pallas_call x1, Pallas kernels, cross(): pl.pallas_call(lambda *refs: cross_kernel(scale, *refs), out_shape=shape(...  5.14 us
    pallas_call x1, Pallas kernels, finish(): pl.pallas_call(lambda *refs: finish_kernel(scale, *refs), out_shape=shape...  4.08 us
    ppermute x1, starting transfers between devices, body(): farthest = lax.ppermute(sent[1], 'seqi', ring(2))  3.57 us
    pallas_call x1, Pallas kernels, pack(): pl.pallas_call(pack_kernel, out_shape=shape((CHUNKS, MESSAGE, DK), BF16),...  3.24 us
    pallas_call x1, Pallas kernels, states(): pl.pallas_call(lambda *refs: states_kernel(scale, *refs), out_shape=[shap...  2.13 us
    ppermute x1, starting transfers between devices, body(): lax.ppermute(sent[0], 'seqi', ring(1))  1.98 us
  transfers between devices with their start and end apart: 7, of which 4 were waited for; matrix products, arithmetic and copies ran while one was open for 0% of the time, Pallas kernels for 5%

profile of v7, /device:TPU:0, one launch (start us, length us, event | category | flops | bytes accessed | tf_op | source)
XLA Modules:
  0.0 93.9 jit_solution(12957179171417292438)
XLA Ops:
  0.6 3.2 %pack.1 = bf16[16,528,128]{2,1,0:T(8,128)(2,1)} custom-call(bf16[1,128,2048]{2,1,0:T(8,128)(2,1)} %q.1, bf16[1,128,2048]{2,1,0:T(8,128)(2,1)} %k.1, bf16[1,128,2048]{2,1,0:T(8,128)(2,1)} %v.1, bf16[1,128,2048]{2,1,0:T(8,128)(2,1)} %dy.1, bf16[16,128]{1,0:T(8,128)(2,1)} %bitcast.7, s32[2,128]{1,0:T(2,128)} %bitcast.8, bf16[2,128]{1,0:T(2,128)(2,1)} %bitcast.9), custom_call_target="tpu_custom_call" | custom-call | bytes 4194304 | tf_op jit(solution)/shard_map/pack/pallas_call | solution.py:98
  3.9 36.2 %all_to_all.10.refs_0_ = bf16[16,528,128]{2,1,0:T(8,128)(2,1)S(1)} all-to-all(bf16[16,528,128]{2,1,0:T(8,128)(2,1)} %pack.1), channel_id=1, replica_groups=mesh['mem'=4,'seqi'=8,'seqo'=4] {'seqo','mem'}, dimensions={0} | all-to-all | bytes 4325376 | tf_op jit(solution)/shard_map/all_to_all | solution.py:410
  40.1 2.1 %states.1 = (bf16[2,4,640,128]{3,2,1,0:T(8,128)(2,1)S(1)}, bf16[656,128]{1,0:T(8,128)(2,1)S(1)}, bf16[656,128]{1,0:T(8,128)(2,1)S(1)}, bf16[656,128]{1,0:T(8,128)(2,1)S(1)}, bf16[656,128]{1,0:T(8,128)(2,1)S(1)}) custom-call(bf16[16,528,128]{2,1,0:T(8,128)(2,1)S(1)} %all_to_all.10.refs_0_), custom_call_target="tpu_custom_call" | custom-call | flops 700000000 | bytes 4194304 | tf_op jit(solution)/shard_map/states/pallas_call | solution.py:216
  42.3 2.0 %collective-permute-start = (bf16[656,128]{1,0:T(8,128)(2,1)S(1)}, bf16[656,128]{1,0:T(8,128)(2,1)S(1)}, u32[]{:S(2)}, u32[]{:S(2)}) collective-permute-start(bf16[656,128]{1,0:T(8,128)(2,1)S(1)} %get-tuple-element.13), channel_id=1, source_target_pairs={{0,8},{4,12},{8,16},{12,20},{16,24},{20,28},{24,0},{28,4},{1,9},{5... | collective-permute-start | bytes 503816 | tf_op jit(solution)/shard_map/ppermute | solution.py:415
  44.2 3.6 %collective-permute-start.1 = (bf16[656,128]{1,0:T(8,128)(2,1)S(1)}, bf16[656,128]{1,0:T(8,128)(2,1)S(1)}, u32[]{:S(2)}, u32[]{:S(2)}) collective-permute-start(bf16[656,128]{1,0:T(8,128)(2,1)S(1)} %get-tuple-element.14), channel_id=1, source_target_pairs={{0,16},{4,20},{8,24},{12,28},{16,0},{20,4},{24,8},{28,12},{1,17},{... | collective-permute-start | bytes 503816 | tf_op jit(solution)/shard_map/ppermute | solution.py:414
  47.8 1.0 %collective-permute-start.2 = (bf16[656,128]{1,0:T(8,128)(2,1)S(1)}, bf16[656,128]{1,0:T(8,128)(2,1)S(1)}, u32[]{:S(2)}, u32[]{:S(2)}) collective-permute-start(bf16[656,128]{1,0:T(8,128)(2,1)S(1)} %get-tuple-element.15), channel_id=1, source_target_pairs={{0,24},{4,28},{8,0},{12,4},{16,8},{20,12},{24,16},{28,20},{1,25},{... | collective-permute-start | bytes 503816 | tf_op jit(solution)/shard_map/ppermute | solution.py:415
  48.8 0.0 collective-permute-start.3
  48.8 5.1 %cross.1.refs_1_ = f32[16,4,128,128]{3,2,1,0:T(8,128)S(1)} custom-call(bf16[16,528,128]{2,1,0:T(8,128)(2,1)S(1)} %all_to_all.10.refs_0_), custom_call_target="tpu_custom_call" | custom-call | flops 2000000000 | bytes 6291456 | tf_op jit(solution)/shard_map/cross/pallas_call | solution.py:300
  54.0 0.0 collective-permute-done.refs_3_
  54.0 0.2 collective-permute-done.1.refs_4_
  54.1 0.0 collective-permute-done.2.refs_5_
  54.1 0.5 collective-permute-start.4
  54.6 0.1 collective-permute-start.5
  54.7 0.4 collective-permute-start.6
  55.1 0.0 collective-permute-done.3.refs_6_
  55.1 0.5 collective-permute-done.4.refs_7_
  55.6 0.4 collective-permute-done.5.refs_8_
  56.0 0.2 collective-permute-done.6.refs_9_
  56.2 4.1 %finish.1 = bf16[16,512,128]{2,1,0:T(8,128)(2,1)S(1)} custom-call(bf16[16,528,128]{2,1,0:T(8,128)(2,1)S(1)} %all_to_all.10.refs_0_, f32[16,4,128,128]{3,2,1,0:T(8,128)S(1)} %cross.1.refs_1_, bf16[2,4,640,128]{3,2,1,0:T(8,128)(2,1)S(1)} %get-tuple-element.17.refs_2_, bf16[656,128]{1,0:T(8,128)(2,1)S(1)} %collective-permute-done.refs_3_, ...), custom_call_target="tpu_custom_call" | custom-call | flops 1300000000 | bytes 8388608 | tf_op jit(solution)/shard_map/finish/pallas_call | solution.py:370
  60.3 32.0 %all_to_all.11.arrived = bf16[16,512,128]{2,1,0:T(8,128)(2,1)S(1)} all-to-all(bf16[16,512,128]{2,1,0:T(8,128)(2,1)S(1)} %finish.1), channel_id=1, replica_groups=mesh['mem'=4,'seqi'=8,'seqo'=4] {'seqo','mem'}, dimensions={0} | all-to-all | bytes 4194304 | tf_op jit(solution)/shard_map/all_to_all | solution.py:421
  92.3 1.5 %unpack.1 = (bf16[1,128,2048]{2,1,0:T(8,128)(2,1)}, bf16[1,128,2048]{2,1,0:T(8,128)(2,1)}, bf16[1,128,2048]{2,1,0:T(8,128)(2,1)}, bf16[1,128,2048]{2,1,0:T(8,128)(2,1)}) custom-call(bf16[16,512,128]{2,1,0:T(8,128)(2,1)S(1)} %all_to_all.11.arrived), custom_call_target="tpu_custom_call" | custom-call | bytes 4194304 | tf_op jit(solution)/shard_map/unpack/pallas_call | solution.py:396
Async XLA Ops:
  42.3 11.7 %collective-permute-start = (bf16[656,128]{1,0:T(8,128)(2,1)S(1)}, bf16[656,128]{1,0:T(8,128)(2,1)S(1)}, u32[]{:S(2)}, u32[]{:S(2)}) collective-permute-start(bf16[656,128]{1,0:T(8,128)(2,1)S(1)} %get-tuple-element.13), channel_id=1, source_target_pairs={{0,8},{4,12},{8,16},{12,20},{16,24},{20,28},{24,0},{28,4},{1,9},{5... | collective-permute-start | bytes 503816 | tf_op jit(solution)/shard_map/ppermute | solution.py:415
  44.2 9.9 %collective-permute-start.1 = (bf16[656,128]{1,0:T(8,128)(2,1)S(1)}, bf16[656,128]{1,0:T(8,128)(2,1)S(1)}, u32[]{:S(2)}, u32[]{:S(2)}) collective-permute-start(bf16[656,128]{1,0:T(8,128)(2,1)S(1)} %get-tuple-element.14), channel_id=1, source_target_pairs={{0,16},{4,20},{8,24},{12,28},{16,0},{20,4},{24,8},{28,12},{1,17},{... | collective-permute-start | bytes 503816 | tf_op jit(solution)/shard_map/ppermute | solution.py:414
  47.8 6.3 %collective-permute-start.2 = (bf16[656,128]{1,0:T(8,128)(2,1)S(1)}, bf16[656,128]{1,0:T(8,128)(2,1)S(1)}, u32[]{:S(2)}, u32[]{:S(2)}) collective-permute-start(bf16[656,128]{1,0:T(8,128)(2,1)S(1)} %get-tuple-element.15), channel_id=1, source_target_pairs={{0,24},{4,28},{8,0},{12,4},{16,8},{20,12},{24,16},{28,20},{1,25},{... | collective-permute-start | bytes 503816 | tf_op jit(solution)/shard_map/ppermute | solution.py:415
  48.8 6.3 %collective-permute-start.3 = (bf16[656,128]{1,0:T(8,128)(2,1)S(1)}, bf16[656,128]{1,0:T(8,128)(2,1)S(1)}, u32[]{:S(2)}, u32[]{:S(2)}) collective-permute-start(bf16[656,128]{1,0:T(8,128)(2,1)S(1)} %get-tuple-element.21), channel_id=1, source_target_pairs={{0,4},{4,0},{8,12},{12,8},{16,20},{20,16},{24,28},{28,24},{1,5},{5... | collective-permute-start | bytes 503816 | tf_op jit(solution)/shard_map/ppermute | solution.py:416
  54.1 1.5 %collective-permute-start.4 = (bf16[656,128]{1,0:T(8,128)(2,1)S(1)}, bf16[656,128]{1,0:T(8,128)(2,1)S(1)}, u32[]{:S(2)}, u32[]{:S(2)}) collective-permute-start(bf16[656,128]{1,0:T(8,128)(2,1)S(1)} %collective-permute-done.refs_3_), channel_id=1, source_target_pairs={{0,4},{4,0},{8,12},{12,8},{16,20},{20,16},{24,28},{28,24},{1,5},{5... | collective-permute-start | bytes 503816 | tf_op jit(solution)/shard_map/ppermute | solution.py:419
  54.6 1.4 %collective-permute-start.5 = (bf16[656,128]{1,0:T(8,128)(2,1)S(1)}, bf16[656,128]{1,0:T(8,128)(2,1)S(1)}, u32[]{:S(2)}, u32[]{:S(2)}) collective-permute-start(bf16[656,128]{1,0:T(8,128)(2,1)S(1)} %collective-permute-done.1.refs_4_), channel_id=1, source_target_pairs={{0,4},{4,0},{8,12},{12,8},{16,20},{20,16},{24,28},{28,24},{1,5},{5... | collective-permute-start | bytes 503816 | tf_op jit(solution)/shard_map/ppermute | solution.py:419
  54.7 1.5 %collective-permute-start.6 = (bf16[656,128]{1,0:T(8,128)(2,1)S(1)}, bf16[656,128]{1,0:T(8,128)(2,1)S(1)}, u32[]{:S(2)}, u32[]{:S(2)}) collective-permute-start(bf16[656,128]{1,0:T(8,128)(2,1)S(1)} %collective-permute-done.2.refs_5_), channel_id=1, source_target_pairs={{0,4},{4,0},{8,12},{12,8},{16,20},{20,16},{24,28},{28,24},{1,5},{5... | collective-permute-start | bytes 503816 | tf_op jit(solution)/shard_map/ppermute | solution.py:419
